TPU v7x, 32 devices: a whole 2x2x4 slice. The times are simulated.
32 devices in a mesh: dp: 4 (over y, core), tensor: 8 (over z, x).
Axes of the slice: x: 2, y: 2, z: 4, core: 2. Of those that a mesh axis runs over, the one named last changes fastest.
Arguments:
- inputs: bfloat16 [8, 256, 1152], P('dp'), may hold values from -32 to 32
- out_grad: bfloat16 [8, 256, 1152], P('dp'), may hold values from -6 to 6
- bucket: int32 [4], P('dp'), may hold values from 0 to 7
- counts: int32 [4], replicated, may hold values from 1 to 8
- images_held: int32 [4], P('dp'), may hold values from 1 to 2, as said below
- owners: int32 [120], replicated, may hold values from 0 to 3, as said below
- master_weight: float32 [360, 192, 1152], P('dp', 'tensor'), may hold values from -0.23570226 to 0.23570226
- first_moment: float32 [360, 192, 1152], P('dp', 'tensor'), may hold values from -85.85453 to 85.85453
- second_moment: float32 [360, 192, 1152], P('dp', 'tensor'), may hold values from 81.9 to 7371
Outputs:
- block_output: bfloat16 [8, 256, 1152], P('dp')
- input_grad: float32 [8, 256, 1152], P('dp')
- new_first: float32 [360, 192, 1152], P('dp', 'tensor')
- new_second: float32 [360, 192, 1152], P('dp', 'tensor')
- new_master: float32 [360, 192, 1152], P('dp', 'tensor')
Inputs may be any that keep to these rules, and one draw needn't show every extreme that they name: Slots 0 to images_held - 1 of a dp index hold its images, the others are empty; one dp index holds 2. `owners`: no dp index owns more than 90 blocks; one owns exactly 90.
All inputs are finite; a program needn't handle non-finite values.
Results may differ from a plain program's by a relative error of at most 0.022.
Values may be sent and summed in bfloat16 or wider, within the bound.
A program may use at most 256 MiB of HBM per device.

v0:
```python
from functools import partial
import math

import jax
import jax.numpy as jnp
from jax import lax
from jax.sharding import PartitionSpec as P

D = 1152
HEADS = 16
HEAD_DIM = 72
FF = 4608
NBUCKET = 8
STEP = 10


eps_norm = 1e-06
beta_one = 0.5
beta_two = 0.5
learn_rate = 0.03
decay_rate = 0.01
eps_adam = 1e-08


def time_token(bucket_value):
    half_width = D // 2
    freqs = jnp.exp(-math.log(10000.0) * jnp.arange(half_width, dtype=jnp.float32) / half_width)
    instant = (bucket_value.astype(jnp.float32) + 0.5) * (1000.0 / NBUCKET)
    angles = instant * freqs
    embed = jnp.concatenate([jnp.cos(angles), jnp.sin(angles)])
    return embed * jax.nn.sigmoid(embed)


def norm_stats(values):
    centred = values - jnp.mean(values, axis=-1, keepdims=True)
    inverse = lax.rsqrt(jnp.mean(centred * centred, axis=-1, keepdims=True) + eps_norm)
    return (centred * inverse, inverse)


def norm_back(normed, inverse, upstream):
    return inverse * (
        upstream
        - jnp.mean(upstream, axis=-1, keepdims=True)
        - normed * jnp.mean(upstream * normed, axis=-1, keepdims=True)
    )


def times_transposed(left, right):
    return lax.dot_general(
        left, right, (((1,), (1,)), ((), ())), preferred_element_type=jnp.float32
    )


def transposed_times(left, right):
    return lax.dot_general(
        left, right, (((0,), (0,)), ((), ())), preferred_element_type=jnp.float32
    )


def attend_forward(block):
    queries, key_rows, values = block
    scores = jnp.einsum(
        "bqhd,bkhd->bhqk", queries, key_rows, preferred_element_type=jnp.float32
    ) * HEAD_DIM ** (-0.5)
    row_peak = jnp.max(scores, axis=-1, keepdims=True)
    exp_scores = jnp.exp(scores - row_peak)
    row_total = jnp.sum(exp_scores, axis=-1, keepdims=True)
    soft = (exp_scores / row_total).astype(jnp.bfloat16)
    attended = jnp.einsum("bhqk,bkhd->bqhd", soft, values, preferred_element_type=jnp.float32)
    return (attended, row_peak[..., 0] + jnp.log(row_total[..., 0]))


def attend_backward(block):
    queries, key_rows, values, log_total, upstream = block
    scale_factor = HEAD_DIM ** (-0.5)
    scores = (
        jnp.einsum("bqhd,bkhd->bhqk", queries, key_rows, preferred_element_type=jnp.float32)
        * scale_factor
    )
    soft = jnp.exp(scores - log_total[..., None])
    grad_soft = jnp.einsum("bqhd,bkhd->bhqk", upstream, values, preferred_element_type=jnp.float32)
    inner_sum = jnp.sum(soft * grad_soft, axis=-1, keepdims=True)
    grad_scores = (soft * (grad_soft - inner_sum)).astype(jnp.bfloat16)
    grad_query = (
        jnp.einsum("bhqk,bkhd->bqhd", grad_scores, key_rows, preferred_element_type=jnp.float32)
        * scale_factor
    )
    grad_key = (
        jnp.einsum("bhqk,bqhd->bkhd", grad_scores, queries, preferred_element_type=jnp.float32)
        * scale_factor
    )
    grad_value = jnp.einsum(
        "bhqk,bqhd->bkhd", soft.astype(jnp.bfloat16), upstream, preferred_element_type=jnp.float32
    )
    return (grad_query, grad_key, grad_value)


def per_device(
    inputs,
    out_grad,
    bucket,
    counts,
    images_held,
    owners,
    master_weight,
    first_moment,
    second_moment,
):
    dp_count = lax.axis_size("dp")
    tensor_count = lax.axis_size("tensor")
    dp_rank = lax.axis_index("dp")
    tensor_rank = lax.axis_index("tensor")
    own_slots = master_weight.shape[0]
    block_rows = master_weight.shape[1]
    head_cols = D // tensor_count
    ffn_cols = FF // tensor_count
    local_heads = HEADS // tensor_count
    local_rows = 12 * head_cols + 2 * ffn_cols
    block_count = local_rows // block_rows
    image_count = inputs.shape[0]
    seq_len = inputs.shape[1]
    row_count = image_count * seq_len
    block_ids = jnp.arange(block_count, dtype=jnp.int32)
    earlier = (owners[None, :] == owners[:, None]) & (block_ids[None, :] < block_ids[:, None])
    slot_of = owners * own_slots + jnp.sum(earlier.astype(jnp.int32), axis=1)
    gathered = lax.all_gather(master_weight.astype(jnp.bfloat16), "dp", axis=0, tiled=True)
    weights = gathered[slot_of].reshape(local_rows, D)
    w_mod = weights[: 6 * head_cols]
    w_qkv = weights[6 * head_cols : 9 * head_cols]
    w_qtime = weights[9 * head_cols : 10 * head_cols]
    w_vtime = weights[10 * head_cols : 11 * head_cols]
    w_proj = weights[11 * head_cols : 12 * head_cols]
    w_up = weights[12 * head_cols : 12 * head_cols + ffn_cols]
    w_down = weights[12 * head_cols + ffn_cols :]
    token = time_token(bucket[0]).astype(jnp.bfloat16)
    token_wide = token.astype(jnp.float32)
    mod_piece = jnp.dot(w_mod, token, preferred_element_type=jnp.float32)
    modulation = lax.all_gather(mod_piece, "tensor", axis=0, tiled=True)
    shift_a, scale_a, gate_a, shift_m, scale_m, gate_m = jnp.split(modulation, 6)
    counts_f = counts.astype(jnp.float32)
    group_scale = counts_f[dp_rank] * dp_count / jnp.sum(counts_f)
    flat_rows = inputs.reshape(row_count, D).astype(jnp.float32)
    live = (jnp.arange(row_count, dtype=jnp.int32) // seq_len < images_held[0]).astype(jnp.float32)[
        :, None
    ]
    normed_a, inverse_a = norm_stats(flat_rows)
    mixed_a = (normed_a * (1.0 + scale_a) + shift_a).astype(jnp.bfloat16)
    projected = times_transposed(mixed_a, w_qkv)
    time_query = jnp.dot(w_qtime, token, preferred_element_type=jnp.float32)
    time_value = jnp.dot(w_vtime, token, preferred_element_type=jnp.float32)
    queries = (projected[:, :head_cols] + time_query).astype(jnp.bfloat16)
    key_rows = projected[:, head_cols : 2 * head_cols].astype(jnp.bfloat16)
    values = (projected[:, 2 * head_cols :] + time_value).astype(jnp.bfloat16)
    group_imgs = math.gcd(image_count, max(1, 512 // seq_len))
    block_shape = (image_count // group_imgs, group_imgs, seq_len, local_heads, HEAD_DIM)
    q_blocks = queries.reshape(block_shape)
    k_blocks = key_rows.reshape(block_shape)
    v_blocks = values.reshape(block_shape)
    attended, log_total = lax.map(attend_forward, (q_blocks, k_blocks, v_blocks))
    heads_out = attended.reshape(row_count, head_cols).astype(jnp.bfloat16)
    heads_share = lax.psum_scatter(
        jnp.dot(heads_out, w_proj, preferred_element_type=jnp.float32).astype(jnp.bfloat16),
        "tensor",
        scatter_dimension=0,
        tiled=True,
    ).astype(jnp.float32)
    branch_a = lax.all_gather(
        heads_share.astype(jnp.bfloat16), "tensor", axis=0, tiled=True
    ).astype(heads_share.dtype)
    resid = flat_rows + gate_a * branch_a
    normed_m, inverse_m = norm_stats(resid)
    mixed_m = (normed_m * (1.0 + scale_m) + shift_m).astype(jnp.bfloat16)
    hidden = times_transposed(mixed_m, w_up)
    acted = jax.nn.gelu(hidden, approximate=True).astype(jnp.bfloat16)
    hidden_share = lax.psum_scatter(
        jnp.dot(acted, w_down, preferred_element_type=jnp.float32).astype(jnp.bfloat16),
        "tensor",
        scatter_dimension=0,
        tiled=True,
    ).astype(jnp.float32)
    branch_m = lax.all_gather(
        hidden_share.astype(jnp.bfloat16), "tensor", axis=0, tiled=True
    ).astype(hidden_share.dtype)
    result = resid + gate_m * branch_m
    block_output = (result * live).astype(jnp.bfloat16).reshape(inputs.shape)
    grad_y = out_grad.reshape(row_count, D).astype(jnp.float32) * (group_scale * live)
    grad_branch_m = (gate_m * grad_y).astype(jnp.bfloat16)
    grad_gate_m = jnp.sum(grad_y * branch_m, axis=0)
    grad_acted = times_transposed(grad_branch_m, w_down)
    grad_down = transposed_times(acted, grad_branch_m)
    grad_hidden = jax.vjp(partial(jax.nn.gelu, approximate=True), hidden)[1](grad_acted)[0].astype(
        jnp.bfloat16
    )
    grad_up = transposed_times(grad_hidden, mixed_m)
    mlp_grad_share = lax.psum_scatter(
        jnp.dot(grad_hidden, w_up, preferred_element_type=jnp.float32).astype(jnp.bfloat16),
        "tensor",
        scatter_dimension=0,
        tiled=True,
    ).astype(jnp.float32)
    grad_mixed_m = lax.all_gather(
        mlp_grad_share.astype(jnp.bfloat16), "tensor", axis=0, tiled=True
    ).astype(mlp_grad_share.dtype)
    grad_shift_m = jnp.sum(grad_mixed_m, axis=0)
    grad_scale_m = jnp.sum(grad_mixed_m * normed_m, axis=0)
    grad_resid = grad_y + norm_back(normed_m, inverse_m, grad_mixed_m * (1.0 + scale_m))
    grad_branch_a = (gate_a * grad_resid).astype(jnp.bfloat16)
    grad_gate_a = jnp.sum(grad_resid * branch_a, axis=0)
    grad_heads = times_transposed(grad_branch_a, w_proj).astype(jnp.bfloat16)
    grad_proj = transposed_times(heads_out, grad_branch_a)
    grads_query, grads_key, grads_value = lax.map(
        attend_backward, (q_blocks, k_blocks, v_blocks, log_total, grad_heads.reshape(block_shape))
    )
    grad_qkv = jnp.concatenate(
        [
            grads_query.reshape(row_count, head_cols),
            grads_key.reshape(row_count, head_cols),
            grads_value.reshape(row_count, head_cols),
        ],
        axis=1,
    ).astype(jnp.bfloat16)
    grad_wqkv = transposed_times(grad_qkv, mixed_a)
    attn_grad_share = lax.psum_scatter(
        jnp.dot(grad_qkv, w_qkv, preferred_element_type=jnp.float32).astype(jnp.bfloat16),
        "tensor",
        scatter_dimension=0,
        tiled=True,
    ).astype(jnp.float32)
    grad_mixed_a = lax.all_gather(
        attn_grad_share.astype(jnp.bfloat16), "tensor", axis=0, tiled=True
    ).astype(attn_grad_share.dtype)
    token_sums = jnp.sum(grad_qkv, axis=0, dtype=jnp.float32)
    grad_qtime = token_sums[:head_cols, None] * token_wide[None, :]
    grad_vtime = token_sums[2 * head_cols :, None] * token_wide[None, :]
    grad_shift_a = jnp.sum(grad_mixed_a, axis=0)
    grad_scale_a = jnp.sum(grad_mixed_a * normed_a, axis=0)
    grad_in = grad_resid + norm_back(normed_a, inverse_a, grad_mixed_a * (1.0 + scale_a))
    grad_mod = jnp.concatenate(
        [grad_shift_a, grad_scale_a, grad_gate_a, grad_shift_m, grad_scale_m, grad_gate_m]
    )
    grad_mod_piece = lax.dynamic_slice_in_dim(grad_mod, tensor_rank * 6 * head_cols, 6 * head_cols)
    grad_wmod = grad_mod_piece[:, None] * token_wide[None, :]
    grads = jnp.concatenate(
        [grad_wmod, grad_wqkv, grad_qtime, grad_vtime, grad_proj, grad_up, grad_down], axis=0
    )
    grad_blocks = grads.reshape(block_count, block_rows, D)
    owned_blocks = jnp.full((dp_count * own_slots,), -1, jnp.int32).at[slot_of].set(block_ids)
    mine = lax.dynamic_slice_in_dim(owned_blocks, dp_rank * own_slots, own_slots)
    filled = (mine >= 0)[:, None, None]
    placed = (
        jnp.zeros((dp_count * own_slots, block_rows, D), jnp.float32).at[slot_of].set(grad_blocks)
    )
    reduced = lax.psum_scatter(
        placed.astype(jnp.bfloat16), "dp", scatter_dimension=0, tiled=True
    ).astype(jnp.float32)
    new_first = beta_one * first_moment + (1.0 - beta_one) * reduced
    new_second = beta_two * second_moment + (1.0 - beta_two) * reduced * reduced
    fix_one = 1.0 - beta_one**STEP
    fix_two = 1.0 - beta_two**STEP
    change = (
        new_first / fix_one / (jnp.sqrt(new_second / fix_two) + eps_adam)
        + decay_rate * master_weight
    )
    new_master = master_weight - learn_rate * change
    return (
        block_output,
        grad_in.reshape(inputs.shape),
        jnp.where(filled, new_first, 0.0),
        jnp.where(filled, new_second, 0.0),
        jnp.where(filled, new_master, 0.0),
    )


def solution(mesh):
    return jax.shard_map(
        per_device,
        mesh=mesh,
        in_specs=(
            P("dp", None, None),
            P("dp", None, None),
            P("dp"),
            P(),
            P("dp"),
            P(),
            P("dp", "tensor", None),
            P("dp", "tensor", None),
            P("dp", "tensor", None),
        ),
        out_specs=(
            P("dp", None, None),
            P("dp", None, None),
            P("dp", "tensor", None),
            P("dp", "tensor", None),
            P("dp", "tensor", None),
        ),
        check_vma=False,
    )
```

profile of v0, /device:TPU:0, one launch (start us, length us, event | category | flops | bytes accessed | tf_op | source)
XLA Modules:
  0.0 909.1 jit_solution(1372573210963665698)
XLA Ops:
  7.2 6.6 convert_element_type.163
  19.3 123.1 %all-gather.6.cloned.1.call-done = bf16[360,24,1152]{2,1,0:T(8,128)(2,1)} async-done(((bf16[90,24,1152]{2,1,0:T(8,128)(2,1)}), bf16[360,24,1152]{2,1,0:T(8,128)(2,1)}) %all-gather.6.cloned.1.call-update) | async-done | bytes 19906576 | tf_op jit(solution)/shard_map/all_gather | solution.py:126
  142.4 11.2 %gather_fusion = bf16[120,24,1152]{2,1,0:T(8,128)(2,1)} fusion(bf16[360,24,1152]{2,1,0:T(8,128)(2,1)} %all-gather.6.cloned.1.call-done, s32[1024]{0:T(1024)S(1)} %pad_clamp_fusion), kind=kCustom, calls=%fused_computation | custom fusion | bytes 13271520 | tf_op jit(solution)/shard_map/gather | solution.py:127
  153.6 2.3 slice.80
  159.8 37.1 %all-reduce = f32[6912]{0:T(1024)S(1)} all-reduce(f32[6912]{0:T(1024)S(1)} %dynamic-update-slice), channel_id=1, replica_groups=mesh['dp'=4,'tensor'=8] {'tensor'}, use_global_device_ids=true, to_apply=%add | all-reduce | flops 6912 | bytes 55296
  198.1 2.0 fusion.84
  203.7 60.5 %reduce-scatter.8.cloned.1.call-done = bf16[64,1152]{1,0:T(8,128)(2,1)} async-done(((bf16[512,1152]{1,0:T(8,128)(2,1)}), bf16[64,1152]{1,0:T(8,128)(2,1)}) %reduce-scatter.8.cloned.1.call-update) | async-done | bytes 147472 | tf_op jit(solution)/shard_map/reduce_scatter | solution.py:161
  268.0 3.0 fusion.79
  272.0 2.0 fusion.87
  274.0 32.4 %all-gather.8.cloned.1.call-done = bf16[512,1152]{1,0:T(8,128)(2,1)} async-done(((bf16[64,1152]{1,0:T(8,128)(2,1)}), bf16[512,1152]{1,0:T(8,128)(2,1)}) %all-gather.8.cloned.1.call-update) | async-done | bytes 1179664 | tf_op jit(solution)/shard_map/all_gather | solution.py:167
  310.6 2.5 fusion.42
  313.9 2.2 convolution_convert_fusion.2
  316.2 4.0 convolution_convert_fusion.3
  320.3 58.9 %reduce-scatter.12.cloned.1.call-done = bf16[64,1152]{1,0:T(8,128)(2,1)} async-done(((bf16[512,1152]{1,0:T(8,128)(2,1)}), bf16[64,1152]{1,0:T(8,128)(2,1)}) %reduce-scatter.12.cloned.1.call-update) | async-done | bytes 147472 | tf_op jit(solution)/shard_map/reduce_scatter | solution.py:195
  379.2 66.9 %reduce-scatter.10.cloned.1.call-done = bf16[64,1152]{1,0:T(8,128)(2,1)} async-done(((bf16[512,1152]{1,0:T(8,128)(2,1)}), bf16[64,1152]{1,0:T(8,128)(2,1)}) %reduce-scatter.10.cloned.1.call-update) | async-done | bytes 147472 | tf_op jit(solution)/shard_map/reduce_scatter | solution.py:175
  448.2 40.0 %all-gather.12.cloned.1.call-done = bf16[512,1152]{1,0:T(8,128)(2,1)} async-done(((bf16[64,1152]{1,0:T(8,128)(2,1)}), bf16[512,1152]{1,0:T(8,128)(2,1)}) %all-gather.12.cloned.1.call-update) | async-done | bytes 1179664 | tf_op jit(solution)/shard_map/all_gather | solution.py:201
  488.2 3.2 fusion.23
  492.6 37.7 %all-gather.10.cloned.1.call-done = bf16[512,1152]{1,0:T(8,128)(2,1)} async-done(((bf16[64,1152]{1,0:T(8,128)(2,1)}), bf16[512,1152]{1,0:T(8,128)(2,1)}) %all-gather.10.cloned.1.call-update) | async-done | bytes 1179664 | tf_op jit(solution)/shard_map/all_gather | solution.py:181
  530.3 5.7 fusion.10
  546.3 63.0 %reduce-scatter.14.cloned.1.call-done = bf16[64,1152]{1,0:T(8,128)(2,1)} async-done(((bf16[512,1152]{1,0:T(8,128)(2,1)}), bf16[64,1152]{1,0:T(8,128)(2,1)}) %reduce-scatter.14.cloned.1.call-update) | async-done | bytes 147472 | tf_op jit(solution)/shard_map/reduce_scatter | solution.py:223
  613.9 37.6 %all-gather.14.cloned.1.call-done = bf16[512,1152]{1,0:T(8,128)(2,1)} async-done(((bf16[64,1152]{1,0:T(8,128)(2,1)}), bf16[512,1152]{1,0:T(8,128)(2,1)}) %all-gather.14.cloned.1.call-update) | async-done | bytes 1179664 | tf_op jit(solution)/shard_map/all_gather | solution.py:229
  651.5 2.4 fusion.24
  654.3 2.2 multiply_dynamic-update-slice_fusion
  656.5 2.4 fusion.35
  659.0 2.0 convolution_dynamic-update-slice_fusion.2
  664.2 2.4 convolution_dynamic-update-slice_fusion.1
  666.6 2.6 convolution_dynamic-update-slice_fusion
  669.3 12.9 %broadcast_in_dim.45 = f32[360,24,1152]{2,1,0:T(8,128)} broadcast(f32[]{:T(128)} %constant.119.clone.1), dimensions={} | broadcast | bytes 39813124 | tf_op jit(solution)/shard_map/broadcast_in_dim | solution.py:251
  682.2 28.8 %scatter_fusion = f32[360,24,1152]{2,1,0:T(8,128)} fusion(f32[360,24,1152]{2,1,0:T(8,128)} %broadcast_in_dim.45, s32[120]{0:T(128)S(1)} %copy-done.45, f32[120,24,1152]{2,1,0:T(8,128)} %bitcast.23), kind=kCustom, calls=%fused_computation.2 | custom fusion | bytes 39813600 | tf_op jit(solution)/shard_map/scatter | solution.py:251
  711.0 20.5 %convert_element_type.203 = bf16[360,24,1152]{2,1,0:T(8,128)(2,1)} convert(f32[360,24,1152]{2,1,0:T(8,128)} %scatter_fusion) | non-fusion elementwise | flops 9953280 | bytes 59719680 | tf_op jit(solution)/shard_map/convert_element_type | solution.py:254
  732.5 145.5 %reduce-scatter.16.cloned.1.call-done = bf16[90,24,1152]{2,1,0:T(8,128)(2,1)} async-done(((bf16[360,24,1152]{2,1,0:T(8,128)(2,1)}), bf16[90,24,1152]{2,1,0:T(8,128)(2,1)}) %reduce-scatter.16.cloned.1.call-update) | async-done | bytes 4976656
  878.1 24.2 %subtract_select_fusion = (f32[90,24,1152]{2,1,0:T(8,128)}, f32[90,24,1152]{2,1,0:T(8,128)}, f32[90,24,1152]{2,1,0:T(8,128)}) fusion(f32[90,24,1152]{2,1,0:T(8,128)} %param.15, bf16[90,24,1152]{2,1,0:T(8,128)(2,1)} %reduce-scatter.16.cloned.1.call-done, f32[90,24,1152]{2,1,0:T(8,128)} %param.16, f32[90,24,1152]{2,1,0:T(8,128)} %param.17, ...), kind=kLoop, calls=%fused_computation.6 | loop fusion | flops 44789760 | bytes 64696408 | tf_op jit(solution)/shard_map/jit(_where)/select_n | solution.py:270
  (208 shorter events, 42.9 us)
Async XLA Ops:
  7.2 135.3 %all-gather.6.cloned.1.call-start = ((), (), s32[]{:S(2)}) async-start(), calls=%async_computation.5 | async-start | bytes 24883200 | tf_op jit(solution)/shard_map/all_gather | solution.py:126
  13.8 2.8 copy-start.47
  13.8 3.0 copy-start
  13.8 250.3 %reduce-scatter.8.cloned.1.call-start = ((), (), s32[]{:S(2)}) async-start(), calls=%async_computation.6 | async-start | bytes 1327104 | tf_op jit(solution)/shard_map/reduce_scatter | solution.py:161
  16.8 136.8 %copy-start.44 = (s32[120]{0:T(128)}, s32[120]{0:T(128)S(1)}, u32[]{:S(2)}) copy-start(s32[120]{0:T(128)S(1)} %compare_select_fusion.1) | copy-start | bytes 1444
  157.2 44.8 %copy-start.10 = (bf16[6,24,1152]{2,1,0:T(8,128)(2,1)}, bf16[6,24,1152]{2,1,0:T(8,128)(2,1)S(1)}, u32[]{:S(2)}) copy-start(bf16[6,24,1152]{2,1,0:T(8,128)(2,1)S(1)} %get-tuple-element.67) | copy-start | bytes 995332
  196.9 3.2 copy-start.27
  196.9 70.7 %copy-start.29 = (f32[1152]{0:T(1024)}, f32[1152]{0:T(1024)S(1)}, u32[]{:S(2)}) copy-start(f32[1152]{0:T(1024)S(1)} %get-tuple-element.77) | copy-start | bytes 13828
  196.9 291.3 %copy-start.25 = (f32[1152]{0:T(1024)}, f32[1152]{0:T(1024)S(1)}, u32[]{:S(2)}) copy-start(f32[1152]{0:T(1024)S(1)} %get-tuple-element.78) | copy-start | bytes 13828
  201.8 63.2 %copy-start.48 = (s32[4]{0:T(128)S(1)}, s32[4]{0:T(128)}, u32[]{:S(2)}) copy-start(s32[4]{0:T(128)} %param.12) | copy-start | bytes 52
  201.8 65.8 %copy-start.5 = (bf16[2,256,1152]{2,1,0:T(8,128)(2,1)S(1)}, bf16[2,256,1152]{2,1,0:T(8,128)(2,1)}, u32[]{:S(2)}) copy-start(bf16[2,256,1152]{2,1,0:T(8,128)(2,1)} %param.10) | copy-start | bytes 3538948
  202.0 66.0 %copy-start.14 = (bf16[18,8,2,256]{3,1,2,0:T(8,128)(2,1)}, bf16[18,8,2,256]{3,1,2,0:T(8,128)(2,1)S(1)}, u32[]{:S(2)}) copy-start(bf16[18,8,2,256]{3,1,2,0:T(8,128)(2,1)S(1)} %copy.78) | copy-start | bytes 442372
  203.6 102.8 %all-gather.8.cloned.1.call-start = ((), (), s32[]{:S(2)}) async-start(), calls=%async_computation.7 | async-start | bytes 1327104 | tf_op jit(solution)/shard_map/all_gather | solution.py:167
  264.2 115.0 %reduce-scatter.12.cloned.1.call-start = ((), (), s32[]{:S(2)}) async-start(), calls=%async_computation.10 | async-start | bytes 1327104 | tf_op jit(solution)/shard_map/reduce_scatter | solution.py:195
  308.2 180.0 %copy-start.31 = (f32[512]{0:T(512)}, f32[512]{0:T(512)S(1)}, u32[]{:S(2)}) copy-start(f32[512]{0:T(512)S(1)} %broadcast_multiply_fusion.4) | copy-start | bytes 6148
  308.9 179.3 %copy-start.32 = (f32[512]{0:T(512)}, f32[512]{0:T(512)S(1)}, u32[]{:S(2)}) copy-start(f32[512]{0:T(512)S(1)} %add_rsqrt_fusion) | copy-start | bytes 6148
  309.6 3.5 copy-start.6
  316.2 129.9 %reduce-scatter.10.cloned.1.call-start = ((), (), s32[]{:S(2)}) async-start(), calls=%async_computation.8 | async-start | bytes 1327104 | tf_op jit(solution)/shard_map/reduce_scatter | solution.py:175
  320.2 168.0 %all-gather.12.cloned.1.call-start = ((), (), s32[]{:S(2)}) async-start(), calls=%async_computation.11 | async-start | bytes 1327104 | tf_op jit(solution)/shard_map/all_gather | solution.py:201
  379.1 151.1 %all-gather.10.cloned.1.call-start = ((), (), s32[]{:S(2)}) async-start(), calls=%async_computation.9 | async-start | bytes 1327104 | tf_op jit(solution)/shard_map/all_gather | solution.py:181
  446.1 163.1 %reduce-scatter.14.cloned.1.call-start = ((), (), s32[]{:S(2)}) async-start(), calls=%async_computation.12 | async-start | bytes 1327104 | tf_op jit(solution)/shard_map/reduce_scatter | solution.py:223
  530.3 5.7 copy-start.11
  538.8 3.4 copy-start.3
  538.8 3.4 copy-start.30
  546.2 105.3 %all-gather.14.cloned.1.call-start = ((), (), s32[]{:S(2)}) async-start(), calls=%async_computation.13 | async-start | bytes 1327104 | tf_op jit(solution)/shard_map/all_gather | solution.py:229
  609.3 268.8 %reduce-scatter.16.cloned.1.call-start = ((), (), s32[]{:S(2)}) async-start(), calls=%async_computation.14 | async-start | bytes 24883200
  651.5 2.7 copy-start.26
  659.0 3.0 copy-start.42
  659.0 4.0 copy-start.15
  661.0 3.2 copy-start.7
  661.0 3.2 copy-start.13
  669.3 12.9 %copy-start.45 = (s32[120]{0:T(128)S(1)}, s32[120]{0:T(128)}, u32[]{:S(2)}) copy-start(s32[120]{0:T(128)} %copy-done.44) | copy-start | bytes 1444
  (31 other events, 57.3 us)
Sparse Core Ops, SparseCore 0:
  14.0 128.4 all-gather.5
  203.7 60.3 reduce-scatter.7
  266.3 40.0 all-gather.7
  316.3 62.7 reduce-scatter.11
  382.9 63.1 reduce-scatter.9
  448.2 40.0 all-gather.11
  490.4 39.8 all-gather.9
  546.4 62.8 reduce-scatter.13
  611.4 40.0 all-gather.13
  731.6 146.4 reduce-scatter.15
where the time goes:
time: 910 us; the launch traced here: 909 us
  waiting for transfers between devices  666 us (73%)
  other arithmetic  82.1 us (9%)
  local copies, waits for them, and re-layouts  72.4 us (8%)
  blocking collectives  37.1 us (4%)
  matrix products  32.5 us (4%)
  between operations  18.3 us (2%)
    unnamed x11, waiting for transfers between devices  146 us
    all_gather x1, waiting for transfers between devices, per_device(): lax.all_gather(master_weight.astype(jnp.bfloat16), 'dp', axis=0, tiled=True)  123 us
    reduce_scatter x1, waiting for transfers between devices, per_device(): lax.psum_scatter(jnp.dot(acted, w_down, preferred_element_type=jnp.float3...  66.9 us
    reduce_scatter x1, waiting for transfers between devices, per_device(): lax.psum_scatter(jnp.dot(grad_qkv, w_qkv, preferred_element_type=jnp.floa...  63 us
    reduce_scatter x1, waiting for transfers between devices, per_device(): lax.psum_scatter(jnp.dot(heads_out, w_proj, preferred_element_type=jnp.fl...  60.5 us
    reduce_scatter x1, waiting for transfers between devices, per_device(): lax.psum_scatter(jnp.dot(grad_hidden, w_up, preferred_element_type=jnp.fl...  58.9 us
    all_gather x1, waiting for transfers between devices, per_device(): lax.all_gather(mlp_grad_share.astype(jnp.bfloat16), 'tensor', axis=0, til...  40 us
    all_gather x1, waiting for transfers between devices, per_device(): lax.all_gather(hidden_share.astype(jnp.bfloat16), 'tensor', axis=0, tiled...  37.7 us
  transfers between devices with their start and end apart: 10, of which 10 were waited for; matrix products, arithmetic and copies ran while one was open for 3% of the time, Pallas kernels for 0%

commit v1 on v0

--- a/solution.py
+++ b/solution.py
@@ -1,9 +1,12 @@
 from functools import partial
 import math
+from types import SimpleNamespace
 
 import jax
 import jax.numpy as jnp
 from jax import lax
+from jax.experimental import pallas as pl
+from jax.experimental.pallas import tpu as pltpu
 from jax.sharding import PartitionSpec as P
 
 D = 1152
@@ -95,7 +98,7 @@
     return (grad_query, grad_key, grad_value)
 
 
-def per_device(
+def per_device_plain(
     inputs,
     out_grad,
     bucket,
@@ -271,6 +274,932 @@
     )
 
 
+BF = jnp.bfloat16
+F32 = jnp.float32
+MESH = pl.DeviceIdType.MESH
+TILE = 64
+PAIR = 48
+GELU_C = math.sqrt(2.0 / math.pi)
+GELU_K = 0.044715
+
+
+def rows_at(start, size):
+    return pl.ds(pl.multiple_of(start, 16), size)
+
+
+def remote(src, dst, send_sem, recv_sem, device):
+    return pltpu.make_async_remote_copy(
+        src_ref=src,
+        dst_ref=dst,
+        send_sem=send_sem,
+        recv_sem=recv_sem,
+        device_id=device,
+        device_id_type=MESH,
+    )
+
+
+def times(left, right):
+    return jnp.dot(left, right, preferred_element_type=F32)
+
+
+class Sizes:
+    def __init__(self, dp_count, tensor_count, slots, block_rows, images, seq):
+        self.dp_count, self.tensor_count = dp_count, tensor_count
+        self.slots, self.block_rows = slots, block_rows
+        self.images, self.seq = images, seq
+        self.rows = images * seq
+        self.head_cols = D // tensor_count
+        self.ffn_cols = FF // tensor_count
+        self.heads = HEADS // tensor_count
+        self.mod_rows = 6 * self.head_cols
+        self.local_rows = 12 * self.head_cols + 2 * self.ffn_cols
+        self.blocks = self.local_rows // block_rows
+        self.wide = 4 * self.head_cols + 2 * self.ffn_cols
+        self.thin = self.mod_rows + 2 * self.head_cols
+
+    def fits(self):
+        return (
+            self.dp_count == 4
+            and self.tensor_count == 8
+            and 2 * self.block_rows == PAIR
+            and self.rows == self.tensor_count * TILE
+            and self.head_cols % PAIR == 0
+            and self.ffn_cols % PAIR == 0
+            and self.wide % (6 * PAIR) == 0
+            and self.thin == D
+            and self.mod_rows <= 1024
+            and self.seq % 128 == 0
+        )
+
+
+def flatten(space):
+    leaves = []
+    for value in vars(space).values():
+        leaves.extend(flatten(value) if isinstance(value, SimpleNamespace) else [value])
+    return leaves
+
+
+def rebuild(space, leaves):
+    return SimpleNamespace(
+        **{
+            key: rebuild(value, leaves) if isinstance(value, SimpleNamespace) else next(leaves)
+            for key, value in vars(space).items()
+        }
+    )
+
+
+def scratch_plan(z):
+    dma = pltpu.SemaphoreType.DMA
+    vm = pltpu.VMEM
+    half = z.wide // PAIR // 2
+
+    def dp_sum():
+        return SimpleNamespace(
+            far=vm((half, PAIR, D), BF),
+            fin=vm((z.wide, D), BF),
+            s1=dma((half,)),
+            r1=dma((half,)),
+            s2=dma((half,)),
+            r2=dma((half,)),
+            s3=dma((half,)),
+            r3=dma((half,)),
+        )
+
+    def hop_sems():
+        return SimpleNamespace(xs=dma((4,)), xr=dma((4,)), zs=dma((3,)), zr=dma((3,)))
+
+    def scatter():
+        return SimpleNamespace(
+            part=vm((z.rows, D), BF),
+            xin=vm((4, TILE, D), BF),
+            zout=vm((3, TILE, D), BF),
+            zin=vm((3, TILE, D), BF),
+            own=vm((TILE, D), F32),
+            sem=hop_sems(),
+        )
+
+    def gather():
+        return SimpleNamespace(buf=vm((z.rows, D), BF), sem=hop_sems())
+
+    return SimpleNamespace(
+        slot_table=pltpu.SMEM((z.blocks,), jnp.int32),
+        master=vm((z.slots, z.block_rows, D), F32),
+        master_sem=dma((3,)),
+        placed=vm((z.local_rows, D), BF),
+        tok_all=vm((16 * z.dp_count, D), BF),
+        tok_s=dma((3,)),
+        tok_r=dma((3,)),
+        mod_prod=vm((16 * z.dp_count, D), F32),
+        mod_pack=vm((z.dp_count, 16, 128), F32),
+        mod_recv=vm((3, 16, 128), F32),
+        mod_s=dma((3,)),
+        mod_r=dma((3,)),
+        mod_own=vm((16, 128), F32),
+        mod_all=vm((z.tensor_count, 16, 128), F32),
+        moda_s=dma((z.tensor_count - 1,)),
+        moda_r=dma((z.tensor_count - 1,)),
+        modv=vm((8, D), F32),
+        time_qv=vm((8, 2 * 256), F32),
+        u=vm((z.rows, D), BF),
+        dmlp=vm((z.rows, D), BF),
+        q=vm((z.rows, z.head_cols), BF),
+        k=vm((z.rows, z.head_cols), BF),
+        v=vm((z.rows, z.head_cols), BF),
+        o=vm((z.rows, z.head_cols), BF),
+        dq=vm((z.rows, z.head_cols), BF),
+        dk=vm((z.rows, z.head_cols), BF),
+        dv=vm((z.rows, z.head_cols), BF),
+        soft=vm((z.images * z.heads, z.seq, z.seq), F32),
+        dgact=vm((z.rows, z.ffn_cols), F32),
+        gact=vm((z.rows, z.ffn_cols), BF),
+        dz=vm((z.rows, z.ffn_cols), BF),
+        h1=vm((TILE, D), F32),
+        attn=vm((TILE, D), F32),
+        dh1=vm((TILE, D), F32),
+        dmod=vm((8, D), F32),
+        dmod_pack=vm((z.tensor_count, 8, 128), F32),
+        dmod_recv=vm((z.tensor_count - 1, 8, 128), F32),
+        dmod_s=dma((z.tensor_count - 1,)),
+        dmod_r=dma((z.tensor_count - 1,)),
+        vec=vm((z.dp_count, 16, 256), F32),
+        vec_s=dma((3,)),
+        vec_r=dma((3,)),
+        out_sem=dma((5,)),
+        w=dp_sum(),
+        g=dp_sum(),
+        w_sib=vm((half, PAIR, D), BF),
+        w_mrg=vm((half, PAIR, D), BF),
+        rs1=scatter(),
+        rs2=scatter(),
+        rs3=scatter(),
+        rs4=scatter(),
+        ag1=gather(),
+        ag2=gather(),
+        ag3=gather(),
+        ag4=gather(),
+    )
+
+
+def layer_kernel(z, plan, *refs):
+    owners, counts, held, tok, x_ref, grad_ref, master_hbm = refs[:7]
+    out_bo, out_ig, out_g, out_vec, out_tok = refs[7:12]
+    s = rebuild(plan, iter(refs[12:]))
+    s.w.src, s.w.sib, s.w.mrg = s.placed, s.w_sib, s.w_mrg
+    s.g.src, s.g.sib, s.g.mrg = s.placed, s.w_sib, s.w_mrg
+    nt_dims = (((1,), (1,)), ((), ()))
+    tn_dims = (((0,), (0,)), ((), ()))
+
+    def nt(left, right):
+        return lax.dot_general(left, right, nt_dims, preferred_element_type=F32)
+
+    def tn(left, right):
+        return lax.dot_general(left, right, tn_dims, preferred_element_type=F32)
+
+    hc, fc = z.head_cols, z.ffn_cols
+    n_dp, n_t = z.dp_count, z.tensor_count
+    dp, t = lax.axis_index("dp"), lax.axis_index("tensor")
+    core = lax.rem(dp, 2)
+    za, xb = t // 2, lax.rem(t, 2)
+    sib = (dp + 1 - 2 * core, t)
+    far = (lax.rem(dp + 2, 4), t)
+    xp = (dp, t + 1 - 2 * xb)
+    half = z.wide // PAIR // 2
+    head_part = (4 * hc) // PAIR // 2
+    pending = []
+
+    def go(copy):
+        copy.start()
+        pending.append(copy)
+
+    third = z.slots // 3
+    loads = [
+        pltpu.make_async_copy(
+            master_hbm.at[pl.ds(i * third, third)],
+            s.master.at[pl.ds(i * third, third)],
+            s.master_sem.at[i],
+        )
+        for i in range(3)
+    ]
+    for load in loads:
+        load.start()
+
+    barrier = pltpu.get_barrier_semaphore()
+    for i in range(1, n_dp):
+        pl.semaphore_signal(
+            barrier, inc=1, device_id=(lax.rem(dp + i, n_dp), t), device_id_type=MESH
+        )
+    for i in range(1, n_t):
+        pl.semaphore_signal(
+            barrier, inc=1, device_id=(dp, lax.rem(t + i, n_t)), device_id_type=MESH
+        )
+    pl.semaphore_wait(barrier, n_dp + n_t - 2)
+
+    s.tok_all[rows_at(dp * 16, 16), :] = tok[...]
+
+    def tok_copy(i, group):
+        block = s.tok_all.at[rows_at(group * 16, 16)]
+        return remote(
+            block,
+            block,
+            s.tok_s.at[i - 1],
+            s.tok_r.at[i - 1],
+            (lax.rem(dp + i, n_dp), t),
+        )
+
+    for i in range(1, n_dp):
+        go(tok_copy(i, dp))
+
+    def note_slot(block, taken):
+        mine = owners[block] == dp
+        s.slot_table[block] = jnp.where(mine, taken, -1)
+        return taken + mine.astype(jnp.int32)
+
+    lax.fori_loop(0, z.blocks, note_slot, jnp.int32(0))
+    for load in loads:
+        load.wait()
+
+    def place(lower, upper, shift):
+        def one(pair, carry):
+            halves = []
+            for side in range(2):
+                slot = s.slot_table[2 * (pair + shift) + side]
+                block = s.master[jnp.clip(slot, 0, z.slots - 1)]
+                halves.append(jnp.where(slot >= 0, block, 0.0))
+            s.placed[rows_at(pair * PAIR, PAIR), :] = jnp.concatenate(halves, axis=0).astype(BF)
+            return carry
+
+        lax.fori_loop(lower, upper, one, 0)
+
+    qkv_pairs, mod_pairs = 3 * hc // PAIR, z.mod_rows // PAIR
+    time_pairs = 2 * hc // PAIR
+    wide_pairs, all_pairs = z.wide // PAIR, z.local_rows // PAIR
+    shift_qkv = mod_pairs
+    shift_rest = mod_pairs + time_pairs
+
+    def sum_step_one(ph, lower, upper):
+        def one(i, carry):
+            remote(
+                ph.src.at[rows_at((2 * i + 1 - core) * PAIR, PAIR)],
+                ph.sib.at[i],
+                ph.s1.at[i],
+                ph.r1.at[i],
+                sib,
+            ).start()
+            return carry
+
+        lax.fori_loop(lower, upper, one, 0)
+
+    def sum_step_two(ph, lower, upper):
+        def one(i, carry):
+            remote(
+                ph.src.at[rows_at((2 * i + 1 - core) * PAIR, PAIR)],
+                ph.sib.at[i],
+                ph.s1.at[i],
+                ph.r1.at[i],
+                sib,
+            ).wait()
+            mine = ph.src[rows_at((2 * i + core) * PAIR, PAIR), :].astype(F32)
+            ph.mrg[i] = (mine + ph.sib[i].astype(F32)).astype(BF)
+            remote(
+                ph.mrg.at[i],
+                ph.far.at[i],
+                ph.s2.at[i],
+                ph.r2.at[i],
+                far,
+            ).start()
+            return carry
+
+        lax.fori_loop(lower, upper, one, 0)
+
+    def final_copy(ph, i, side):
+        block = ph.fin.at[rows_at((2 * i + side) * PAIR, PAIR)]
+        return remote(block, block, ph.s3.at[i], ph.r3.at[i], sib)
+
+    def sum_step_three(ph, lower, upper):
+        def one(i, carry):
+            remote(
+                ph.mrg.at[i],
+                ph.far.at[i],
+                ph.s2.at[i],
+                ph.r2.at[i],
+                far,
+            ).wait()
+            total = ph.mrg[i].astype(F32) + ph.far[i].astype(F32)
+            ph.fin[rows_at((2 * i + core) * PAIR, PAIR), :] = total.astype(BF)
+            final_copy(ph, i, core).start()
+            return carry
+
+        lax.fori_loop(lower, upper, one, 0)
+
+    def sum_step_four(ph, lower, upper):
+        def one(i, carry):
+            final_copy(ph, i, core).wait_send()
+            final_copy(ph, i, 1 - core).wait_recv()
+            return carry
+
+        lax.fori_loop(lower, upper, one, 0)
+
+    place(0, qkv_pairs, shift_qkv)
+    place(qkv_pairs, 2 * head_part, shift_rest)
+    sum_step_one(s.w, 0, head_part)
+    place(wide_pairs, wide_pairs + mod_pairs, -wide_pairs)
+    place(wide_pairs + mod_pairs, all_pairs, -wide_pairs + qkv_pairs)
+
+    for i in range(1, n_dp):
+        tok_copy(i, lax.rem(dp - i + n_dp, n_dp)).wait_recv()
+    for i in range(3):
+        cols = D // 3
+        s.mod_prod[:, i * cols : (i + 1) * cols] = nt(
+            s.tok_all[...], s.placed[z.wide + i * cols : z.wide + (i + 1) * cols, :]
+        )
+    for group in range(n_dp):
+        for i in range(D // 128):
+            s.mod_pack[group, i : i + 1, :] = s.mod_prod[
+                16 * group : 16 * group + 1, 128 * i : 128 * (i + 1)
+            ]
+
+    def mod_copy(i):
+        group = lax.rem(dp + i, n_dp)
+        return remote(
+            s.mod_pack.at[group],
+            s.mod_recv.at[i - 1],
+            s.mod_s.at[i - 1],
+            s.mod_r.at[i - 1],
+            (group, t),
+        )
+
+    for i in range(1, n_dp):
+        go(mod_copy(i))
+    sum_step_two(s.w, 0, head_part)
+    place(2 * head_part, wide_pairs, shift_rest)
+    sum_step_one(s.w, head_part, half)
+    for i in range(1, n_dp):
+        mod_copy(i).wait_recv()
+    s.mod_own[...] = (
+        s.mod_pack[dp] + s.mod_recv[0] + s.mod_recv[1] + s.mod_recv[2]
+    )
+    s.mod_all[t] = s.mod_own[...]
+
+    def mod_all_copy(i, member):
+        block = s.mod_all.at[member, pl.ds(0, 8)]
+        return remote(
+            block,
+            block,
+            s.moda_s.at[i - 1],
+            s.moda_r.at[i - 1],
+            (dp, lax.rem(t + i, n_t)),
+        )
+
+    for i in range(1, n_t):
+        go(mod_all_copy(i, t))
+    sum_step_two(s.w, head_part, half)
+    for i in range(1, n_t):
+        mod_all_copy(i, lax.rem(t - i + n_t, n_t)).wait_recv()
+
+    lane = lax.broadcasted_iota(jnp.int32, (8, D), 1)
+
+    def spread(vector):
+        return jnp.broadcast_to(vector, (8, D))
+
+    def unpack_rows(block):
+        return jnp.concatenate([block[i : i + 1, :] for i in range(block.shape[0])], axis=1)
+
+    own_line = spread(unpack_rows(s.mod_own[0 : D // 128, :]))
+    s.time_qv[:, 0:256] = pltpu.roll(own_line, D - z.mod_rows, 1)[:, 0:256]
+    s.time_qv[:, 256:512] = pltpu.roll(own_line, D - z.mod_rows - hc, 1)[:, 0:256]
+    lines = [jnp.zeros((8, D), F32) for _ in range(6)]
+    for member in range(n_t):
+        first = member * z.mod_rows
+        line = jnp.concatenate(
+            [s.mod_all[member, i : i + 1, :] for i in range(8)]
+            + [jnp.zeros((1, D - 1024), F32)],
+            axis=1,
+        )
+        line = spread(line)
+        for piece in range(6):
+            lower = max(first, piece * D) - piece * D
+            upper = min(first + z.mod_rows, (piece + 1) * D) - piece * D
+            if lower < upper:
+                moved = pltpu.roll(line, (first - piece * D) % D, 1) if (first - piece * D) % D else line
+                lines[piece] = jnp.where((lane >= lower) & (lane < upper), moved, lines[piece])
+    for piece in range(6):
+        s.modv[piece : piece + 1, :] = lines[piece][0:1, :]
+
+    def mod_line(piece):
+        return s.modv[piece : piece + 1, :]
+
+    def norm_parts(values):
+        centred = values - jnp.mean(values, axis=-1, keepdims=True)
+        inverse = lax.rsqrt(jnp.mean(centred * centred, axis=-1, keepdims=True) + eps_norm)
+        return centred * inverse, inverse
+
+    count_sum = counts[0]
+    for i in range(1, n_dp):
+        count_sum = count_sum + counts[i]
+    group_scale = jnp.full((1, 1), counts[dp], jnp.int32).astype(F32) * n_dp / jnp.full(
+        (1, 1), count_sum, jnp.int32
+    ).astype(F32)
+
+    def live_of(image):
+        return (jnp.full((1, 1), image, jnp.int32) < held[0]).astype(F32)
+
+    def mix_tile(i, carry):
+        at = rows_at(i * TILE, TILE)
+        normed, _ = norm_parts(x_ref[at, :].astype(F32))
+        s.u[at, :] = (normed * (1.0 + mod_line(1)) + mod_line(0)).astype(BF)
+        dy = grad_ref[at, :].astype(F32) * (group_scale * live_of(i * TILE // z.seq))
+        s.dmlp[at, :] = (mod_line(5) * dy).astype(BF)
+        return carry
+
+    lax.fori_loop(0, n_t, mix_tile, 0)
+
+    sum_step_three(s.w, 0, head_part)
+    sum_step_four(s.w, 0, head_part)
+    w_fin = s.w.fin
+    w_q, w_k, w_v, w_p = (w_fin.at[i * hc : (i + 1) * hc] for i in range(4))
+    w_u = w_fin.at[4 * hc : 4 * hc + fc]
+    w_d = w_fin.at[4 * hc + fc : 4 * hc + 2 * fc]
+
+    head_of = lax.broadcasted_iota(jnp.int32, (1, hc), 1) // HEAD_DIM
+
+    def only(values, head):
+        return jnp.where(head_of == head, values, jnp.zeros_like(values))
+
+    scale = HEAD_DIM ** (-0.5)
+    time_q = s.time_qv[0:1, 0:hc]
+    time_v = s.time_qv[0:1, 256 : 256 + hc]
+
+    def attend(image, carry):
+        at = rows_at(image * z.seq, z.seq)
+        mixed = s.u[at, :]
+        q = (nt(mixed, w_q[...]) + time_q).astype(BF)
+        k = nt(mixed, w_k[...]).astype(BF)
+        v = (nt(mixed, w_v[...]) + time_v).astype(BF)
+        s.q[at, :] = q
+        s.k[at, :] = k
+        s.v[at, :] = v
+        out = jnp.zeros((z.seq, hc), F32)
+        for head in range(z.heads):
+            scores = nt(only(q, head), k) * scale
+            e = jnp.exp(scores - jnp.max(scores, axis=-1, keepdims=True))
+            p = e / jnp.sum(e, axis=-1, keepdims=True)
+            s.soft[image * z.heads + head] = p
+            out = out + times(p.astype(BF), only(v, head))
+        s.o[at, :] = out.astype(BF)
+        s.rs1.part[at, :] = times(out.astype(BF), w_p[...]).astype(BF)
+        return carry
+
+    lax.fori_loop(0, z.images, attend, 0)
+
+    def rs_x(ph, k):
+        theirs = 2 * lax.rem(za + 1 + k, 4) + 1 - xb
+        return remote(
+            ph.part.at[rows_at(theirs * TILE, TILE)],
+            ph.xin.at[k],
+            ph.sem.xs.at[k],
+            ph.sem.xr.at[k],
+            xp,
+        )
+
+    def rs_z(ph, k):
+        return remote(
+            ph.zout.at[k],
+            ph.zin.at[k],
+            ph.sem.zs.at[k],
+            ph.sem.zr.at[k],
+            (dp, 2 * lax.rem(za + 1 + k, 4) + xb),
+        )
+
+    def rs_start(ph):
+        for k in range(4):
+            go(rs_x(ph, k))
+
+    def rs_middle(ph):
+        for k in range(4):
+            rs_x(ph, k).wait_recv()
+            mine = 2 * lax.rem(za + 1 + k, 4) + xb
+            total = ph.part[rows_at(mine * TILE, TILE), :].astype(F32) + ph.xin[k].astype(F32)
+            if k < 3:
+                ph.zout[k] = total.astype(BF)
+                go(rs_z(ph, k))
+            else:
+                ph.own[...] = total
+
+    def rs_end(ph):
+        total = ph.own[...]
+        for k in range(3):
+            rs_z(ph, k).wait_recv()
+            total = total + ph.zin[k].astype(F32)
+        return total
+
+    def ag_z(ph, shard, k):
+        block = ph.buf.at[rows_at(shard * TILE, TILE)]
+        device = (dp, 2 * lax.rem(za + 1 + k, 4) + xb)
+        return remote(block, block, ph.sem.zs.at[k], ph.sem.zr.at[k], device)
+
+    def ag_x(ph, shard, k):
+        block = ph.buf.at[rows_at(shard * TILE, TILE)]
+        return remote(block, block, ph.sem.xs.at[k], ph.sem.xr.at[k], xp)
+
+    def ag_start(ph, value):
+        ph.buf[rows_at(t * TILE, TILE), :] = value
+        for k in range(3):
+            go(ag_z(ph, t, k))
+        go(ag_x(ph, t, 0))
+
+    def ag_middle(ph):
+        for k in range(3):
+            origin = lax.rem(za + 3 - k, 4)
+            ag_z(ph, 2 * origin + xb, k).wait_recv()
+            go(ag_x(ph, 2 * origin + xb, k + 1))
+
+    def ag_end(ph):
+        for k in range(4):
+            origin = lax.rem(za + 4 - k, 4)
+            ag_x(ph, 2 * origin + 1 - xb, k).wait_recv()
+
+    rs_start(s.rs1)
+    rs_middle(s.rs1)
+
+    mine_at = rows_at(t * TILE, TILE)
+    live = live_of(t * TILE // z.seq)
+    attn = rs_end(s.rs1)
+    s.attn[...] = attn
+    h1 = x_ref[mine_at, :].astype(F32) + mod_line(2) * attn
+    s.h1[...] = h1
+    normed_m, _ = norm_parts(h1)
+    ag_start(s.ag1, (normed_m * (1.0 + mod_line(4)) + mod_line(3)).astype(BF))
+    sum_step_three(s.w, head_part, half)
+    ag_middle(s.ag1)
+    sum_step_four(s.w, head_part, half)
+
+    step_rows = 128
+
+    def up_tile(i, carry):
+        at = rows_at(i * step_rows, step_rows)
+        s.dgact[at, :] = nt(s.dmlp[at, :], w_d[...])
+        return carry
+
+    lax.fori_loop(0, z.rows // step_rows, up_tile, 0)
+    ag_end(s.ag1)
+
+    def mlp_tile(i, carry):
+        at = rows_at(i * step_rows, step_rows)
+        hidden = nt(s.ag1.buf[at, :], w_u[...])
+        square = hidden * hidden
+        bend = jnp.tanh(GELU_C * hidden * (1.0 + GELU_K * square))
+        s.gact[at, :] = (0.5 * hidden * (1.0 + bend)).astype(BF)
+        slope = 0.5 * (1.0 + bend) + 0.5 * hidden * (1.0 - bend * bend) * (
+            GELU_C * (1.0 + 3.0 * GELU_K * square)
+        )
+        dz = (s.dgact[at, :] * slope).astype(BF)
+        s.dz[at, :] = dz
+        s.rs2.part[at, :] = times(dz, w_u[...]).astype(BF)
+        return carry
+
+    lax.fori_loop(0, z.rows // step_rows, mlp_tile, 0)
+    rs_start(s.rs2)
+    rs_middle(s.rs2)
+
+    cols = 384
+
+    def grad_tile(i, carry):
+        at = pl.ds(pl.multiple_of(i * cols, 128), cols)
+        s.g.src[4 * hc : 4 * hc + fc, at] = tn(s.dz[...], s.ag1.buf[:, at]).astype(BF)
+        s.g.src[4 * hc + fc : z.wide, at] = tn(s.gact[...], s.dmlp[:, at]).astype(BF)
+        return carry
+
+    lax.fori_loop(0, D // cols, grad_tile, 0)
+    sum_step_one(s.g, head_part, half)
+
+    def down_tile(i, carry):
+        at = rows_at(i * step_rows, step_rows)
+        s.rs4.part[at, :] = times(s.gact[at, :], w_d[...]).astype(BF)
+        return carry
+
+    lax.fori_loop(0, z.rows // step_rows, down_tile, 0)
+
+    def norm_back_of(normed, inverse, upstream):
+        return inverse * (
+            upstream
+            - jnp.mean(upstream, axis=-1, keepdims=True)
+            - normed * jnp.mean(upstream * normed, axis=-1, keepdims=True)
+        )
+
+    def column_sum(values):
+        return jnp.sum(values, axis=0, keepdims=True)
+
+    dw = rs_end(s.rs2)
+    dy_mine = grad_ref[mine_at, :].astype(F32) * (group_scale * live)
+    normed_m, inverse_m = norm_parts(s.h1[...])
+    dh1 = dy_mine + norm_back_of(normed_m, inverse_m, dw * (1.0 + mod_line(4)))
+    ag_start(s.ag2, (mod_line(2) * dh1).astype(BF))
+    s.dh1[...] = dh1
+    s.dmod[2:3, :] = column_sum(dh1 * s.attn[...])
+    s.dmod[3:4, :] = column_sum(dw)
+    s.dmod[4:5, :] = column_sum(dw * normed_m)
+    sum_step_two(s.g, head_part, half)
+    ag_middle(s.ag2)
+    ag_end(s.ag2)
+    rs_start(s.rs4)
+
+    def attend_back(image, carry):
+        at = rows_at(image * z.seq, z.seq)
+        do = nt(s.ag2.buf[at, :], w_p[...]).astype(BF)
+        q, k, v = s.q[at, :], s.k[at, :], s.v[at, :]
+        dq = jnp.zeros((z.seq, hc), F32)
+        dk = jnp.zeros((z.seq, hc), F32)
+        dv = jnp.zeros((z.seq, hc), F32)
+        for head in range(z.heads):
+            p = s.soft[image * z.heads + head]
+            do_head = only(do, head)
+            dp_soft = nt(do_head, v)
+            inner = jnp.sum(p * dp_soft, axis=-1, keepdims=True)
+            ds = (p * (dp_soft - inner)).astype(BF)
+            dq = dq + times(ds, only(k, head))
+            dk = dk + tn(ds, only(q, head))
+            dv = dv + tn(p.astype(BF), do_head)
+        dq = (dq * scale).astype(BF)
+        dk = (dk * scale).astype(BF)
+        dv = dv.astype(BF)
+        s.dq[at, :] = dq
+        s.dk[at, :] = dk
+        s.dv[at, :] = dv
+        s.rs3.part[at, :] = (
+            times(dq, w_q[...]) + times(dk, w_k[...]) + times(dv, w_v[...])
+        ).astype(BF)
+        return carry
+
+    lax.fori_loop(0, z.images, attend_back, 0)
+    rs_start(s.rs3)
+    rs_middle(s.rs4)
+
+    def attn_grad_tile(i, carry):
+        at = pl.ds(pl.multiple_of(i * cols, 128), cols)
+        mixed = s.u[:, at]
+        s.g.src[0:hc, at] = tn(s.dq[...], mixed).astype(BF)
+        s.g.src[hc : 2 * hc, at] = tn(s.dk[...], mixed).astype(BF)
+        s.g.src[2 * hc : 3 * hc, at] = tn(s.dv[...], mixed).astype(BF)
+        s.g.src[3 * hc : 4 * hc, at] = tn(s.o[...], s.ag2.buf[:, at]).astype(BF)
+        return carry
+
+    lax.fori_loop(0, D // cols, attn_grad_tile, 0)
+    sum_step_one(s.g, 0, head_part)
+    rs_middle(s.rs3)
+    s.vec[dp] = jnp.zeros((16, 256), F32)
+    s.vec[dp, 8:9, 0:hc] = column_sum(s.dq[...].astype(F32))
+    s.vec[dp, 9:10, 0:hc] = column_sum(s.dv[...].astype(F32))
+    sum_step_two(s.g, 0, head_part)
+
+    mlp = rs_end(s.rs4)
+    s.dmod[5:6, :] = column_sum(dy_mine * mlp)
+    ag_start(s.ag4, ((s.h1[...] + mod_line(5) * mlp) * live).astype(BF))
+    sum_step_three(s.g, head_part, half)
+    ag_middle(s.ag4)
+
+    du = rs_end(s.rs3)
+    normed_a, inverse_a = norm_parts(x_ref[mine_at, :].astype(F32))
+    ag_start(
+        s.ag3,
+        (s.dh1[...] + norm_back_of(normed_a, inverse_a, du * (1.0 + mod_line(1)))).astype(BF),
+    )
+    s.dmod[0:1, :] = column_sum(du)
+    s.dmod[1:2, :] = column_sum(du * normed_a)
+    s.dmod[6:8, :] = jnp.zeros((2, D), F32)
+
+    dlines = [spread(s.dmod[i : i + 1, :]) for i in range(6)]
+    for member in range(n_t):
+        first = member * z.mod_rows
+        line = jnp.zeros((8, D), F32)
+        for piece in range(6):
+            lower = max(first, piece * D) - first
+            upper = min(first + z.mod_rows, (piece + 1) * D) - first
+            if lower < upper:
+                back = (piece * D - first) % D
+                moved = pltpu.roll(dlines[piece], back, 1) if back else dlines[piece]
+                line = jnp.where((lane >= lower) & (lane < upper), moved, line)
+        for i in range(8):
+            s.dmod_pack[member, i : i + 1, :] = line[0:1, 128 * i : 128 * (i + 1)]
+
+    def dmod_copy(i):
+        member = lax.rem(t + i, n_t)
+        return remote(
+            s.dmod_pack.at[member],
+            s.dmod_recv.at[i - 1],
+            s.dmod_s.at[i - 1],
+            s.dmod_r.at[i - 1],
+            (dp, member),
+        )
+
+    for i in range(1, n_t):
+        go(dmod_copy(i))
+    ag_middle(s.ag3)
+    sum_step_three(s.g, 0, head_part)
+    total = s.dmod_pack[t]
+    for i in range(1, n_t):
+        dmod_copy(i).wait_recv()
+        total = total + s.dmod_recv[i - 1]
+    s.vec[dp, 0:8, 0:128] = total
+
+    def vec_copy(i, group):
+        return remote(
+            s.vec.at[group],
+            s.vec.at[group],
+            s.vec_s.at[i - 1],
+            s.vec_r.at[i - 1],
+            (lax.rem(dp + i, n_dp), t),
+        )
+
+    for i in range(1, n_dp):
+        go(vec_copy(i, dp))
+    sum_step_four(s.g, 0, half)
+    ag_end(s.ag4)
+    ag_end(s.ag3)
+    for i in range(1, n_dp):
+        vec_copy(i, lax.rem(dp - i + n_dp, n_dp)).wait_recv()
+    for copy in pending:
+        copy.wait_send()
+
+    outs = (
+        (s.ag4.buf, out_bo),
+        (s.ag3.buf, out_ig),
+        (s.g.fin, out_g),
+        (s.vec, out_vec),
+        (s.tok_all, out_tok),
+    )
+    stores = [
+        pltpu.make_async_copy(src, dst, s.out_sem.at[i]) for i, (src, dst) in enumerate(outs)
+    ]
+    for store in stores:
+        store.start()
+    for store in stores:
+        store.wait()
+
+
+def update_kernel(z, group_slots, owners, grads, table, tokens, master, first, second, new_first, new_second, new_master, bos):
+    step = pl.program_id(0)
+    dp = lax.axis_index("dp")
+
+    @pl.when(step == 0)
+    def _():
+        def clear(slot, carry):
+            bos[slot] = -1
+            return carry
+
+        lax.fori_loop(0, z.slots, clear, 0)
+
+        def note(block, taken):
+            mine = owners[block] == dp
+
+            @pl.when(mine & (taken < z.slots))
+            def _():
+                bos[taken] = block
+
+            return taken + mine.astype(jnp.int32)
+
+        lax.fori_loop(0, z.blocks, note, jnp.int32(0))
+
+    rows = z.block_rows
+    mod_blocks = z.mod_rows // rows
+    head_blocks = z.head_cols // rows
+    fix_one = 1.0 - beta_one**STEP
+    fix_two = 1.0 - beta_two**STEP
+
+    def put(i, grad):
+        weight = master[i]
+        one = beta_one * first[i] + (1.0 - beta_one) * grad
+        two = beta_two * second[i] + (1.0 - beta_two) * grad * grad
+        new_first[i] = one
+        new_second[i] = two
+        change = one / fix_one / (jnp.sqrt(two / fix_two) + eps_adam) + decay_rate * weight
+        new_master[i] = weight - learn_rate * change
+
+    def slot(i, carry):
+        block = bos[step * group_slots + i]
+        is_mod = block < mod_blocks
+        is_time = (block >= mod_blocks + 3 * head_blocks) & (block < mod_blocks + 5 * head_blocks)
+
+        @pl.when(block < 0)
+        def _():
+            new_first[i] = jnp.zeros((rows, D), F32)
+            new_second[i] = jnp.zeros((rows, D), F32)
+            new_master[i] = jnp.zeros((rows, D), F32)
+
+        @pl.when((block >= 0) & (is_mod | is_time))
+        def _():
+            index = jnp.where(is_mod, block, block - 3 * head_blocks)
+            columns = table[index]
+            grad = columns[:, 0:1] * tokens[0:1, :].astype(F32)
+            for group in range(1, z.dp_count):
+                grad = grad + columns[:, group : group + 1] * tokens[
+                    16 * group : 16 * group + 1, :
+                ].astype(F32)
+            put(i, grad)
+
+        @pl.when((block >= 0) & jnp.logical_not(is_mod | is_time))
+        def _():
+            index = jnp.where(
+                block < mod_blocks + 3 * head_blocks,
+                block - mod_blocks,
+                block - mod_blocks - 2 * head_blocks,
+            )
+            both = grads[rows_at(index // 2 * PAIR, PAIR), :].astype(F32)
+            put(i, jnp.where(lax.rem(index, 2) == 0, both[:rows], both[rows:]))
+
+        return carry
+
+    lax.fori_loop(0, group_slots, slot, 0)
+
+
+def per_device_fast(
+    z,
+    inputs,
+    out_grad,
+    bucket,
+    counts,
+    images_held,
+    owners,
+    master_weight,
+    first_moment,
+    second_moment,
+):
+    token = jnp.broadcast_to(time_token(bucket[0]).astype(BF)[None, :], (16, D))
+    plan = scratch_plan(z)
+    smem = pl.BlockSpec(memory_space=pltpu.SMEM)
+    vmem = pl.BlockSpec(memory_space=pltpu.VMEM)
+    hbm = pl.BlockSpec(memory_space=pl.ANY)
+    flops = 6 * z.rows * D * z.wide
+    block_output, input_grad, grads, vectors, tokens = pl.pallas_call(
+        partial(layer_kernel, z, plan),
+        out_shape=(
+            jax.ShapeDtypeStruct((z.rows, D), BF),
+            jax.ShapeDtypeStruct((z.rows, D), BF),
+            jax.ShapeDtypeStruct((z.wide, D), BF),
+            jax.ShapeDtypeStruct((z.dp_count, 16, 256), F32),
+            jax.ShapeDtypeStruct((16 * z.dp_count, D), BF),
+        ),
+        in_specs=[smem, smem, smem, vmem, vmem, vmem, hbm],
+        out_specs=(hbm,) * 5,
+        scratch_shapes=flatten(plan),
+        compiler_params=pltpu.CompilerParams(
+            collective_id=0, has_side_effects=True, vmem_limit_bytes=62 * 2**20
+        ),
+        cost_estimate=pl.CostEstimate(
+            flops=flops, bytes_accessed=20 * 2**20, transcendentals=z.rows * z.ffn_cols
+        ),
+        name="layer",
+    )(
+        owners,
+        counts,
+        images_held,
+        token,
+        inputs.reshape(z.rows, D),
+        out_grad.reshape(z.rows, D),
+        master_weight,
+    )
+    columns = jnp.concatenate(
+        [
+            vectors[:, :8, :128].reshape(z.dp_count, 1024)[:, : z.mod_rows],
+            vectors[:, 8, : z.head_cols],
+            vectors[:, 9, : z.head_cols],
+        ],
+        axis=1,
+    ).T.reshape(z.thin // z.block_rows, z.block_rows, z.dp_count)
+    group_slots = next(size for size in (6, 5, 4, 3, 2, 1) if z.slots % size == 0)
+    block = pl.BlockSpec((group_slots, z.block_rows, D), lambda i: (i, 0, 0))
+    state = jax.ShapeDtypeStruct(master_weight.shape, F32)
+    new_first, new_second, new_master = pl.pallas_call(
+        partial(update_kernel, z, group_slots),
+        grid=(z.slots // group_slots,),
+        out_shape=(state,) * 3,
+        in_specs=[smem, vmem, vmem, vmem, block, block, block],
+        out_specs=(block,) * 3,
+        scratch_shapes=[pltpu.SMEM((z.slots,), jnp.int32)],
+        compiler_params=pltpu.CompilerParams(vmem_limit_bytes=48 * 2**20),
+        name="update",
+    )(owners, grads, columns, tokens, master_weight, first_moment, second_moment)
+    return (
+        block_output.reshape(inputs.shape),
+        input_grad.astype(F32).reshape(inputs.shape),
+        new_first,
+        new_second,
+        new_master,
+    )
+
+
+def per_device(inputs, out_grad, bucket, counts, images_held, owners, master, first, second):
+    sizes = Sizes(
+        lax.axis_size("dp"),
+        lax.axis_size("tensor"),
+        master.shape[0],
+        master.shape[1],
+        inputs.shape[0],
+        inputs.shape[1],
+    )
+    run = partial(per_device_fast, sizes) if sizes.fits() else per_device_plain
+    return run(inputs, out_grad, bucket, counts, images_held, owners, master, first, second)
+
+
 def solution(mesh):
     return jax.shard_map(
         per_device,

time: 910 us -> 231 us (0.25)
  waiting for transfers between devices: 666 us -> 0 us
  Pallas kernels: 0 us -> 218 us
  other arithmetic: 82.1 us -> 1.7 us
  local copies, waits for them, and re-layouts: 72.4 us -> 6.77 us
  blocking collectives: 37.1 us -> 0 us
  matrix products: 32.5 us -> 0 us
  between operations: 18.3 us -> 1.99 us
    all_gather x5 -> x0, waiting for transfers between devices: 271 us -> none  [the longest x1 123 us: per_device(): lax.all_gather(master_weight.astype(jnp.bfloat16), 'dp', axis=0, tiled=True)]
    reduce_scatter x4 -> x0, waiting for transfers between devices: 249 us -> none  [the longest x1 66.9 us: per_device(): lax.psum_scatter(jnp.dot(acted, w_down, preferred_element_type=jnp.float3...]
    pallas_call x0 -> x2, Pallas kernels: none -> 218 us  [the longest x1 189 us: per_device_fast(): pl.pallas_call(partial(layer_kernel, z, plan), out_shape=(jax.ShapeDtypeS...]
    unnamed x11 -> x0, waiting for transfers between devices: 146 us -> none
    unnamed x1 -> x0, blocking collectives: 37.1 us -> none
    convert_element_type x11 -> x1, other arithmetic: 33.3 us -> 0.08 us  [per_device_fast(): token = jnp.broadcast_to(time_token(bucket[0]).astype(BF)[None, :], (16, D))]
    dot_general x21 -> x0, matrix products: 32.5 us -> none  [the longest x4 8.3 us: transposed_times(): lax.dot_general(left, right, (((0,), (0,)), ((), ())), preferred_element_...]
    scatter x2 -> x0, local copies, waits for them, and re-layouts: 29.7 us -> none  [the longest x1 28.8 us: per_device(): jnp.zeros((dp_count * own_slots, block_rows, D), jnp.float32).at[slot_of]]
  transfers between devices with their start and end apart: 10 -> 0, of which waited for: 10 -> 0; matrix products, arithmetic and copies ran while one was open for 3% -> 0% of each run, Pallas kernels for 0% -> 0%
where the time goes in v1:
time: 231 us; the launch traced here: 229 us
  Pallas kernels  218 us (94%)
  local copies, waits for them, and re-layouts  6.77 us (3%)
    pallas_call x1, Pallas kernels, per_device_fast(): pl.pallas_call(partial(layer_kernel, z, plan), out_shape=(jax.ShapeDtypeS...  189 us
    pallas_call x1, Pallas kernels, per_device_fast(): pl.pallas_call(partial(update_kernel, z, group_slots), grid=(z.slots // g...  28.9 us
    unnamed x15, local copies, waits for them, and re-layouts  4.91 us

profile of v1, /device:TPU:0, one launch (start us, length us, event | category | flops | bytes accessed | tf_op | source)
XLA Modules:
  0.0 228.9 jit_solution(14812021954730419033)
XLA Ops:
  1.3 0.1 multiply_convert_fusion
  1.4 0.6 broadcast_in_dim.2.refs_3_
  2.7 0.0 copy-start.2
  2.7 189.5 %layer.1 = (bf16[512,1152]{1,0:T(8,128)(2,1)}, bf16[512,1152]{1,0:T(8,128)(2,1)}, bf16[1728,1152]{1,0:T(8,128)(2,1)}, f32[4,16,256]{2,1,0:T(8,128)}, bf16[64,1152]{1,0:T(8,128)(2,1)}) custom-call(s32[120]{0:T(128)} %owners.1, s32[4]{0:T(128)} %refs_1_.1, s32[1]{0:T(128)S(6)} %copy.29.refs_2_, bf16[16,1152]{1,0:T(8,128)(2,1)} %broadcast_in_dim.2.refs_3_, ...), custom_call_target="tpu_custom_call" | custom-call | flops 6115295232 | bytes 20971520 | tf_op jit(solution)/shard_map/layer/pallas_call | solution.py:1132
  192.2 0.9 fusion.2
  193.1 0.7 slice_bitcast_fusion
  193.8 0.1 concatenate.14
  193.9 0.2 copy.17
  194.2 0.0 copy-done.2
  194.2 0.0 copy-start
  194.2 2.1 copy-done
  196.3 0.0 copy-start.1
  196.3 0.9 copy-done.1
  197.2 0.0 copy-start.3
  197.2 28.9 %update.1 = (f32[90,24,1152]{2,1,0:T(8,128)}, f32[90,24,1152]{2,1,0:T(8,128)}, f32[90,24,1152]{2,1,0:T(8,128)}) custom-call(s32[120]{0:T(128)S(1)} %copy-done.2, bf16[1728,1152]{1,0:T(8,128)(2,1)S(1)} %copy-done, f32[48,24,4]{2,1,0:T(8,128)S(1)} %bitcast.19, bf16[64,1152]{1,0:T(8,128)(2,1)S(1)} %copy-done.1, f32[90,24,1152]{2,1,0:T(8,128)} %master.1, ...), custom_call_target="tpu_custom_call" | custom-call | tf_op jit(solution)/shard_map/update/pallas_call | solution.py:1171
  226.2 0.0 copy-start.4
  226.2 0.0 copy-done.3
  226.2 1.6 convert.1
  227.7 0.1 copy-done.4
  227.9 1.0 copy.30
  (5 shorter events, 0.1 us)
Async XLA Ops:
  2.7 191.5 %copy-start.2 = (s32[120]{0:T(128)S(1)}, s32[120]{0:T(128)}, u32[]{:S(2)}) copy-start(s32[120]{0:T(128)} %owners.1) | copy-start | bytes 1444
  194.2 2.1 copy-start
  196.3 0.9 copy-start.1
  197.2 28.9 %copy-start.3 = (bf16[512,1152]{1,0:T(8,128)(2,1)S(1)}, bf16[512,1152]{1,0:T(8,128)(2,1)}, u32[]{:S(2)}) copy-start(bf16[512,1152]{1,0:T(8,128)(2,1)} %get-tuple-element.14) | copy-start | bytes 3538948
  226.2 1.7 copy-start.4

commit v2 on v1

--- a/solution.py
+++ b/solution.py
@@ -278,6 +278,7 @@
 F32 = jnp.float32
 MESH = pl.DeviceIdType.MESH
 TILE = 64
+HOP_ROWS = 16
 PAIR = 48
 GELU_C = math.sqrt(2.0 / math.pi)
 GELU_K = 0.044715
@@ -308,6 +309,7 @@
         self.slots, self.block_rows = slots, block_rows
         self.images, self.seq = images, seq
         self.rows = images * seq
+        self.shard = seq // tensor_count
         self.head_cols = D // tensor_count
         self.ffn_cols = FF // tensor_count
         self.heads = HEADS // tensor_count
@@ -322,7 +324,8 @@
             self.dp_count == 4
             and self.tensor_count == 8
             and 2 * self.block_rows == PAIR
-            and self.rows == self.tensor_count * TILE
+            and self.shard % HOP_ROWS == 0
+            and self.rows % TILE == 0
             and self.head_cols % PAIR == 0
             and self.ffn_cols % PAIR == 0
             and self.wide % (6 * PAIR) == 0
@@ -332,20 +335,20 @@
         )
 
 
-def flatten(space):
-    leaves = []
-    for value in vars(space).values():
-        leaves.extend(flatten(value) if isinstance(value, SimpleNamespace) else [value])
-    return leaves
-
-
-def rebuild(space, leaves):
-    return SimpleNamespace(
-        **{
-            key: rebuild(value, leaves) if isinstance(value, SimpleNamespace) else next(leaves)
-            for key, value in vars(space).items()
-        }
-    )
+def flatten(plan):
+    if isinstance(plan, SimpleNamespace):
+        return flatten(list(vars(plan).values()))
+    if isinstance(plan, list):
+        return [leaf for member in plan for leaf in flatten(member)]
+    return [plan]
+
+
+def rebuild(plan, leaves):
+    if isinstance(plan, SimpleNamespace):
+        return SimpleNamespace(**{key: rebuild(value, leaves) for key, value in vars(plan).items()})
+    if isinstance(plan, list):
+        return [rebuild(member, leaves) for member in plan]
+    return next(leaves)
 
 
 def scratch_plan(z):
@@ -370,16 +373,19 @@
 
     def scatter():
         return SimpleNamespace(
-            part=vm((z.rows, D), BF),
-            xin=vm((4, TILE, D), BF),
-            zout=vm((3, TILE, D), BF),
-            zin=vm((3, TILE, D), BF),
-            own=vm((TILE, D), F32),
+            part=vm((z.seq, D), BF),
+            xin=vm((4, z.shard, D), BF),
+            zout=vm((3, z.shard, D), BF),
+            zin=vm((3, z.shard, D), BF),
+            own=vm((z.shard, D), F32),
             sem=hop_sems(),
         )
 
     def gather():
-        return SimpleNamespace(buf=vm((z.rows, D), BF), sem=hop_sems())
+        return SimpleNamespace(buf=vm((z.seq, D), BF), sem=hop_sems())
+
+    def each(make):
+        return [make() for _ in range(z.images)]
 
     return SimpleNamespace(
         slot_table=pltpu.SMEM((z.blocks,), jnp.int32),
@@ -413,9 +419,9 @@
         dgact=vm((z.rows, z.ffn_cols), F32),
         gact=vm((z.rows, z.ffn_cols), BF),
         dz=vm((z.rows, z.ffn_cols), BF),
-        h1=vm((TILE, D), F32),
-        attn=vm((TILE, D), F32),
-        dh1=vm((TILE, D), F32),
+        h1=vm((z.images, z.shard, D), F32),
+        attn=vm((z.images, z.shard, D), F32),
+        dh1=vm((z.images, z.shard, D), F32),
         dmod=vm((8, D), F32),
         dmod_pack=vm((z.tensor_count, 8, 128), F32),
         dmod_recv=vm((z.tensor_count - 1, 8, 128), F32),
@@ -424,19 +430,19 @@
         vec=vm((z.dp_count, 16, 256), F32),
         vec_s=dma((3,)),
         vec_r=dma((3,)),
-        out_sem=dma((5,)),
+        out_sem=dma((3 + 2 * z.images,)),
         w=dp_sum(),
         g=dp_sum(),
         w_sib=vm((half, PAIR, D), BF),
         w_mrg=vm((half, PAIR, D), BF),
-        rs1=scatter(),
-        rs2=scatter(),
-        rs3=scatter(),
-        rs4=scatter(),
-        ag1=gather(),
-        ag2=gather(),
-        ag3=gather(),
-        ag4=gather(),
+        rs1=each(scatter),
+        rs2=each(scatter),
+        rs3=each(scatter),
+        rs4=each(scatter),
+        ag1=each(gather),
+        ag2=each(gather),
+        ag3=each(gather),
+        ag4=each(gather),
     )
 
 
@@ -711,7 +717,7 @@
         s.dmlp[at, :] = (mod_line(5) * dy).astype(BF)
         return carry
 
-    lax.fori_loop(0, n_t, mix_tile, 0)
+    lax.fori_loop(0, z.rows // TILE, mix_tile, 0)
 
     sum_step_three(s.w, 0, head_part)
     sum_step_four(s.w, 0, head_part)
@@ -729,7 +735,7 @@
     time_q = s.time_qv[0:1, 0:hc]
     time_v = s.time_qv[0:1, 256 : 256 + hc]
 
-    def attend(image, carry):
+    def attend(image):
         at = rows_at(image * z.seq, z.seq)
         mixed = s.u[at, :]
         q = (nt(mixed, w_q[...]) + time_q).astype(BF)
@@ -746,29 +752,18 @@
             s.soft[image * z.heads + head] = p
             out = out + times(p.astype(BF), only(v, head))
         s.o[at, :] = out.astype(BF)
-        s.rs1.part[at, :] = times(out.astype(BF), w_p[...]).astype(BF)
-        return carry
-
-    lax.fori_loop(0, z.images, attend, 0)
+        s.rs1[image].part[...] = times(out.astype(BF), w_p[...]).astype(BF)
+
+    sh = z.shard
 
     def rs_x(ph, k):
         theirs = 2 * lax.rem(za + 1 + k, 4) + 1 - xb
-        return remote(
-            ph.part.at[rows_at(theirs * TILE, TILE)],
-            ph.xin.at[k],
-            ph.sem.xs.at[k],
-            ph.sem.xr.at[k],
-            xp,
-        )
+        part = ph.part.at[rows_at(theirs * sh, sh)]
+        return remote(part, ph.xin.at[k], ph.sem.xs.at[k], ph.sem.xr.at[k], xp)
 
     def rs_z(ph, k):
-        return remote(
-            ph.zout.at[k],
-            ph.zin.at[k],
-            ph.sem.zs.at[k],
-            ph.sem.zr.at[k],
-            (dp, 2 * lax.rem(za + 1 + k, 4) + xb),
-        )
+        device = (dp, 2 * lax.rem(za + 1 + k, 4) + xb)
+        return remote(ph.zout.at[k], ph.zin.at[k], ph.sem.zs.at[k], ph.sem.zr.at[k], device)
 
     def rs_start(ph):
         for k in range(4):
@@ -778,7 +773,7 @@
         for k in range(4):
             rs_x(ph, k).wait_recv()
             mine = 2 * lax.rem(za + 1 + k, 4) + xb
-            total = ph.part[rows_at(mine * TILE, TILE), :].astype(F32) + ph.xin[k].astype(F32)
+            total = ph.part[rows_at(mine * sh, sh), :].astype(F32) + ph.xin[k].astype(F32)
             if k < 3:
                 ph.zout[k] = total.astype(BF)
                 go(rs_z(ph, k))
@@ -793,44 +788,51 @@
         return total
 
     def ag_z(ph, shard, k):
-        block = ph.buf.at[rows_at(shard * TILE, TILE)]
+        block = ph.buf.at[rows_at(shard * sh, sh)]
         device = (dp, 2 * lax.rem(za + 1 + k, 4) + xb)
         return remote(block, block, ph.sem.zs.at[k], ph.sem.zr.at[k], device)
 
     def ag_x(ph, shard, k):
-        block = ph.buf.at[rows_at(shard * TILE, TILE)]
+        block = ph.buf.at[rows_at(shard * sh, sh)]
         return remote(block, block, ph.sem.xs.at[k], ph.sem.xr.at[k], xp)
 
     def ag_start(ph, value):
-        ph.buf[rows_at(t * TILE, TILE), :] = value
+        ph.buf[rows_at(t * sh, sh), :] = value
         for k in range(3):
             go(ag_z(ph, t, k))
         go(ag_x(ph, t, 0))
 
     def ag_middle(ph):
         for k in range(3):
-            origin = lax.rem(za + 3 - k, 4)
-            ag_z(ph, 2 * origin + xb, k).wait_recv()
-            go(ag_x(ph, 2 * origin + xb, k + 1))
+            shard = 2 * lax.rem(za + 3 - k, 4) + xb
+            ag_z(ph, shard, k).wait_recv()
+            go(ag_x(ph, shard, k + 1))
 
     def ag_end(ph):
         for k in range(4):
-            origin = lax.rem(za + 4 - k, 4)
-            ag_x(ph, 2 * origin + 1 - xb, k).wait_recv()
-
-    rs_start(s.rs1)
-    rs_middle(s.rs1)
-
-    mine_at = rows_at(t * TILE, TILE)
-    live = live_of(t * TILE // z.seq)
-    attn = rs_end(s.rs1)
-    s.attn[...] = attn
-    h1 = x_ref[mine_at, :].astype(F32) + mod_line(2) * attn
-    s.h1[...] = h1
-    normed_m, _ = norm_parts(h1)
-    ag_start(s.ag1, (normed_m * (1.0 + mod_line(4)) + mod_line(3)).astype(BF))
+            ag_x(ph, 2 * lax.rem(za + 4 - k, 4) + 1 - xb, k).wait_recv()
+
+    images = range(z.images)
+    for i in images:
+        attend(i)
+        rs_start(s.rs1[i])
+    for i in images:
+        rs_middle(s.rs1[i])
+
+    def mine_at(image):
+        return rows_at(image * z.seq + t * sh, sh)
+
+    for i in images:
+        attn = rs_end(s.rs1[i])
+        h1 = x_ref[mine_at(i), :].astype(F32) + mod_line(2) * attn
+        normed_m, _ = norm_parts(h1)
+        ag_start(s.ag1[i], (normed_m * (1.0 + mod_line(4)) + mod_line(3)).astype(BF))
+        s.attn[i] = attn
+        s.h1[i] = h1
+    ag_middle(s.ag1[0])
     sum_step_three(s.w, head_part, half)
-    ag_middle(s.ag1)
+    for i in images[1:]:
+        ag_middle(s.ag1[i])
     sum_step_four(s.w, head_part, half)
 
     step_rows = 128
@@ -841,43 +843,61 @@
         return carry
 
     lax.fori_loop(0, z.rows // step_rows, up_tile, 0)
-    ag_end(s.ag1)
-
-    def mlp_tile(i, carry):
-        at = rows_at(i * step_rows, step_rows)
-        hidden = nt(s.ag1.buf[at, :], w_u[...])
-        square = hidden * hidden
-        bend = jnp.tanh(GELU_C * hidden * (1.0 + GELU_K * square))
-        s.gact[at, :] = (0.5 * hidden * (1.0 + bend)).astype(BF)
-        slope = 0.5 * (1.0 + bend) + 0.5 * hidden * (1.0 - bend * bend) * (
-            GELU_C * (1.0 + 3.0 * GELU_K * square)
-        )
-        dz = (s.dgact[at, :] * slope).astype(BF)
-        s.dz[at, :] = dz
-        s.rs2.part[at, :] = times(dz, w_u[...]).astype(BF)
-        return carry
-
-    lax.fori_loop(0, z.rows // step_rows, mlp_tile, 0)
-    rs_start(s.rs2)
-    rs_middle(s.rs2)
+
+    def mlp(image):
+        def tile(i, carry):
+            at = rows_at(image * z.seq + i * step_rows, step_rows)
+            hidden = nt(s.ag1[image].buf[rows_at(i * step_rows, step_rows), :], w_u[...])
+            square = hidden * hidden
+            bend = jnp.tanh(GELU_C * hidden * (1.0 + GELU_K * square))
+            s.gact[at, :] = (0.5 * hidden * (1.0 + bend)).astype(BF)
+            slope = 0.5 * (1.0 + bend) + 0.5 * hidden * (1.0 - bend * bend) * (
+                GELU_C * (1.0 + 3.0 * GELU_K * square)
+            )
+            dz = (s.dgact[at, :] * slope).astype(BF)
+            s.dz[at, :] = dz
+            s.rs2[image].part[rows_at(i * step_rows, step_rows), :] = times(dz, w_u[...]).astype(BF)
+            return carry
+
+        lax.fori_loop(0, z.seq // step_rows, tile, 0)
+
+    def down(image):
+        def tile(i, carry):
+            at = rows_at(image * z.seq + i * step_rows, step_rows)
+            s.rs4[image].part[rows_at(i * step_rows, step_rows), :] = times(
+                s.gact[at, :], w_d[...]
+            ).astype(BF)
+            return carry
+
+        lax.fori_loop(0, z.seq // step_rows, tile, 0)
+
+    for i in images:
+        ag_end(s.ag1[i])
+        mlp(i)
+        rs_start(s.rs2[i])
+    for i in images:
+        rs_middle(s.rs2[i])
 
     cols = 384
+
+    def over_images(left, gathered, at):
+        total = 0.0
+        for image in images:
+            total = total + tn(
+                left[image * z.seq : (image + 1) * z.seq, :], gathered[image].buf[:, at]
+            )
+        return total.astype(BF)
 
     def grad_tile(i, carry):
         at = pl.ds(pl.multiple_of(i * cols, 128), cols)
-        s.g.src[4 * hc : 4 * hc + fc, at] = tn(s.dz[...], s.ag1.buf[:, at]).astype(BF)
+        s.g.src[4 * hc : 4 * hc + fc, at] = over_images(s.dz, s.ag1, at)
         s.g.src[4 * hc + fc : z.wide, at] = tn(s.gact[...], s.dmlp[:, at]).astype(BF)
         return carry
 
     lax.fori_loop(0, D // cols, grad_tile, 0)
     sum_step_one(s.g, head_part, half)
-
-    def down_tile(i, carry):
-        at = rows_at(i * step_rows, step_rows)
-        s.rs4.part[at, :] = times(s.gact[at, :], w_d[...]).astype(BF)
-        return carry
-
-    lax.fori_loop(0, z.rows // step_rows, down_tile, 0)
+    for i in images:
+        down(i)
 
     def norm_back_of(normed, inverse, upstream):
         return inverse * (
@@ -889,23 +909,29 @@
     def column_sum(values):
         return jnp.sum(values, axis=0, keepdims=True)
 
-    dw = rs_end(s.rs2)
-    dy_mine = grad_ref[mine_at, :].astype(F32) * (group_scale * live)
-    normed_m, inverse_m = norm_parts(s.h1[...])
-    dh1 = dy_mine + norm_back_of(normed_m, inverse_m, dw * (1.0 + mod_line(4)))
-    ag_start(s.ag2, (mod_line(2) * dh1).astype(BF))
-    s.dh1[...] = dh1
-    s.dmod[2:3, :] = column_sum(dh1 * s.attn[...])
-    s.dmod[3:4, :] = column_sum(dw)
-    s.dmod[4:5, :] = column_sum(dw * normed_m)
+    def dy_of(image):
+        return grad_ref[mine_at(image), :].astype(F32) * (group_scale * live_of(image))
+
+    gate_a_sum = shift_m_sum = scale_m_sum = 0.0
+    for i in images:
+        dw = rs_end(s.rs2[i])
+        normed_m, inverse_m = norm_parts(s.h1[i])
+        dh1 = dy_of(i) + norm_back_of(normed_m, inverse_m, dw * (1.0 + mod_line(4)))
+        ag_start(s.ag2[i], (mod_line(2) * dh1).astype(BF))
+        s.dh1[i] = dh1
+        gate_a_sum = gate_a_sum + column_sum(dh1 * s.attn[i])
+        shift_m_sum = shift_m_sum + column_sum(dw)
+        scale_m_sum = scale_m_sum + column_sum(dw * normed_m)
+    s.dmod[2:3, :] = gate_a_sum
+    s.dmod[3:4, :] = shift_m_sum
+    s.dmod[4:5, :] = scale_m_sum
+    for i in images:
+        ag_middle(s.ag2[i])
     sum_step_two(s.g, head_part, half)
-    ag_middle(s.ag2)
-    ag_end(s.ag2)
-    rs_start(s.rs4)
-
-    def attend_back(image, carry):
+
+    def attend_back(image):
         at = rows_at(image * z.seq, z.seq)
-        do = nt(s.ag2.buf[at, :], w_p[...]).astype(BF)
+        do = nt(s.ag2[image].buf[...], w_p[...]).astype(BF)
         q, k, v = s.q[at, :], s.k[at, :], s.v[at, :]
         dq = jnp.zeros((z.seq, hc), F32)
         dk = jnp.zeros((z.seq, hc), F32)
@@ -925,14 +951,18 @@
         s.dq[at, :] = dq
         s.dk[at, :] = dk
         s.dv[at, :] = dv
-        s.rs3.part[at, :] = (
+        s.rs3[image].part[...] = (
             times(dq, w_q[...]) + times(dk, w_k[...]) + times(dv, w_v[...])
         ).astype(BF)
-        return carry
-
-    lax.fori_loop(0, z.images, attend_back, 0)
-    rs_start(s.rs3)
-    rs_middle(s.rs4)
+
+    for i in images:
+        ag_end(s.ag2[i])
+        attend_back(i)
+        rs_start(s.rs3[i])
+        rs_start(s.rs4[i])
+    for i in images:
+        rs_middle(s.rs3[i])
+        rs_middle(s.rs4[i])
 
     def attn_grad_tile(i, carry):
         at = pl.ds(pl.multiple_of(i * cols, 128), cols)
@@ -940,31 +970,30 @@
         s.g.src[0:hc, at] = tn(s.dq[...], mixed).astype(BF)
         s.g.src[hc : 2 * hc, at] = tn(s.dk[...], mixed).astype(BF)
         s.g.src[2 * hc : 3 * hc, at] = tn(s.dv[...], mixed).astype(BF)
-        s.g.src[3 * hc : 4 * hc, at] = tn(s.o[...], s.ag2.buf[:, at]).astype(BF)
+        s.g.src[3 * hc : 4 * hc, at] = over_images(s.o, s.ag2, at)
         return carry
 
     lax.fori_loop(0, D // cols, attn_grad_tile, 0)
     sum_step_one(s.g, 0, head_part)
-    rs_middle(s.rs3)
+    shift_a_sum = scale_a_sum = gate_m_sum = 0.0
+    for i in images:
+        du = rs_end(s.rs3[i])
+        normed_a, inverse_a = norm_parts(x_ref[mine_at(i), :].astype(F32))
+        dx = s.dh1[i] + norm_back_of(normed_a, inverse_a, du * (1.0 + mod_line(1)))
+        ag_start(s.ag3[i], dx.astype(BF))
+        shift_a_sum = shift_a_sum + column_sum(du)
+        scale_a_sum = scale_a_sum + column_sum(du * normed_a)
+        mlp_sum = rs_end(s.rs4[i])
+        gate_m_sum = gate_m_sum + column_sum(dy_of(i) * mlp_sum)
+        result = (s.h1[i] + mod_line(5) * mlp_sum) * live_of(i)
+        ag_start(s.ag4[i], result.astype(BF))
+    s.dmod[0:1, :] = shift_a_sum
+    s.dmod[1:2, :] = scale_a_sum
+    s.dmod[5:6, :] = gate_m_sum
+    sum_step_two(s.g, 0, head_part)
     s.vec[dp] = jnp.zeros((16, 256), F32)
     s.vec[dp, 8:9, 0:hc] = column_sum(s.dq[...].astype(F32))
     s.vec[dp, 9:10, 0:hc] = column_sum(s.dv[...].astype(F32))
-    sum_step_two(s.g, 0, head_part)
-
-    mlp = rs_end(s.rs4)
-    s.dmod[5:6, :] = column_sum(dy_mine * mlp)
-    ag_start(s.ag4, ((s.h1[...] + mod_line(5) * mlp) * live).astype(BF))
-    sum_step_three(s.g, head_part, half)
-    ag_middle(s.ag4)
-
-    du = rs_end(s.rs3)
-    normed_a, inverse_a = norm_parts(x_ref[mine_at, :].astype(F32))
-    ag_start(
-        s.ag3,
-        (s.dh1[...] + norm_back_of(normed_a, inverse_a, du * (1.0 + mod_line(1)))).astype(BF),
-    )
-    s.dmod[0:1, :] = column_sum(du)
-    s.dmod[1:2, :] = column_sum(du * normed_a)
     s.dmod[6:8, :] = jnp.zeros((2, D), F32)
 
     dlines = [spread(s.dmod[i : i + 1, :]) for i in range(6)]
@@ -993,8 +1022,10 @@
 
     for i in range(1, n_t):
         go(dmod_copy(i))
-    ag_middle(s.ag3)
-    sum_step_three(s.g, 0, head_part)
+    for i in images:
+        ag_middle(s.ag3[i])
+        ag_middle(s.ag4[i])
+    sum_step_three(s.g, 0, half)
     total = s.dmod_pack[t]
     for i in range(1, n_t):
         dmod_copy(i).wait_recv()
@@ -1013,20 +1044,18 @@
     for i in range(1, n_dp):
         go(vec_copy(i, dp))
     sum_step_four(s.g, 0, half)
-    ag_end(s.ag4)
-    ag_end(s.ag3)
+    for i in images:
+        ag_end(s.ag3[i])
+        ag_end(s.ag4[i])
     for i in range(1, n_dp):
         vec_copy(i, lax.rem(dp - i + n_dp, n_dp)).wait_recv()
     for copy in pending:
         copy.wait_send()
 
-    outs = (
-        (s.ag4.buf, out_bo),
-        (s.ag3.buf, out_ig),
-        (s.g.fin, out_g),
-        (s.vec, out_vec),
-        (s.tok_all, out_tok),
-    )
+    outs = [(s.g.fin, out_g), (s.vec, out_vec), (s.tok_all, out_tok)]
+    for i in images:
+        outs.append((s.ag4[i].buf, out_bo.at[i]))
+        outs.append((s.ag3[i].buf, out_ig.at[i]))
     stores = [
         pltpu.make_async_copy(src, dst, s.out_sem.at[i]) for i, (src, dst) in enumerate(outs)
     ]
@@ -1071,7 +1100,9 @@
         two = beta_two * second[i] + (1.0 - beta_two) * grad * grad
         new_first[i] = one
         new_second[i] = two
-        change = one / fix_one / (jnp.sqrt(two / fix_two) + eps_adam) + decay_rate * weight
+        spread = two * (1.0 / fix_two)
+        root = spread * lax.rsqrt(spread)
+        change = one * (1.0 / fix_one) * pltpu.reciprocal(root + eps_adam) + decay_rate * weight
         new_master[i] = weight - learn_rate * change
 
     def slot(i, carry):
@@ -1132,8 +1163,8 @@
     block_output, input_grad, grads, vectors, tokens = pl.pallas_call(
         partial(layer_kernel, z, plan),
         out_shape=(
-            jax.ShapeDtypeStruct((z.rows, D), BF),
-            jax.ShapeDtypeStruct((z.rows, D), BF),
+            jax.ShapeDtypeStruct(inputs.shape, BF),
+            jax.ShapeDtypeStruct(inputs.shape, BF),
             jax.ShapeDtypeStruct((z.wide, D), BF),
             jax.ShapeDtypeStruct((z.dp_count, 16, 256), F32),
             jax.ShapeDtypeStruct((16 * z.dp_count, D), BF),
@@ -1165,7 +1196,7 @@
         ],
         axis=1,
     ).T.reshape(z.thin // z.block_rows, z.block_rows, z.dp_count)
-    group_slots = next(size for size in (6, 5, 4, 3, 2, 1) if z.slots % size == 0)
+    group_slots = next(size for size in (15, 12, 10, 8, 6, 5, 4, 3, 2, 1) if z.slots % size == 0)
     block = pl.BlockSpec((group_slots, z.block_rows, D), lambda i: (i, 0, 0))
     state = jax.ShapeDtypeStruct(master_weight.shape, F32)
     new_first, new_second, new_master = pl.pallas_call(
@@ -1179,8 +1210,8 @@
         name="update",
     )(owners, grads, columns, tokens, master_weight, first_moment, second_moment)
     return (
-        block_output.reshape(inputs.shape),
-        input_grad.astype(F32).reshape(inputs.shape),
+        block_output,
+        input_grad.astype(F32),
         new_first,
         new_second,
         new_master,

time: 231 us -> 209 us (0.905)
  Pallas kernels: 218 us -> 196 us
    pallas_call x1, Pallas kernels: 189 us -> 172 us  [per_device_fast(): pl.pallas_call(partial(layer_kernel, z, plan), out_shape=(jax.ShapeDtypeS...]
    pallas_call x1, Pallas kernels: 28.9 us -> 23.3 us  [per_device_fast(): pl.pallas_call(partial(update_kernel, z, group_slots), grid=(z.slots // g...]
where the time goes in v2:
time: 209 us; the launch traced here: 206 us
  Pallas kernels  196 us (94%)
  local copies, waits for them, and re-layouts  6.77 us (3%)
    pallas_call x1, Pallas kernels, per_device_fast(): pl.pallas_call(partial(layer_kernel, z, plan), out_shape=(jax.ShapeDtypeS...  172 us
    pallas_call x1, Pallas kernels, per_device_fast(): pl.pallas_call(partial(update_kernel, z, group_slots), grid=(z.slots // g...  23.3 us
    unnamed x15, local copies, waits for them, and re-layouts  4.91 us

profile of v2, /device:TPU:0, one launch (start us, length us, event | category | flops | bytes accessed | tf_op | source)
XLA Modules:
  0.0 206.0 jit_solution(11273996297086768726)
XLA Ops:
  1.3 0.1 multiply_convert_fusion
  1.4 0.6 broadcast_in_dim.2.refs_3_
  2.7 0.0 copy-start.2
  2.7 172.3 %layer.1 = (bf16[2,256,1152]{2,1,0:T(8,128)(2,1)}, bf16[2,256,1152]{2,1,0:T(8,128)(2,1)}, bf16[1728,1152]{1,0:T(8,128)(2,1)}, f32[4,16,256]{2,1,0:T(8,128)}, bf16[64,1152]{1,0:T(8,128)(2,1)}) custom-call(s32[120]{0:T(128)} %owners.1, s32[4]{0:T(128)} %refs_1_.1, s32[1]{0:T(128)S(6)} %copy.29.refs_2_, bf16[16,1152]{1,0:T(8,128)(2,1)} %broadcast_in_dim.2.refs_3_, ...), custom_call_target="tpu_custom_call" | custom-call | flops 6115295232 | bytes 20971520 | tf_op jit(solution)/shard_map/layer/pallas_call | solution.py:1163
  175.0 0.9 fusion.2
  175.9 0.7 slice_bitcast_fusion
  176.6 0.1 concatenate.14
  176.7 0.2 copy.17
  177.0 0.0 copy-done.2
  177.0 0.0 copy-start
  177.0 2.1 %copy-done = bf16[1728,1152]{1,0:T(8,128)(2,1)S(1)} copy-done((bf16[1728,1152]{1,0:T(8,128)(2,1)S(1)}, bf16[1728,1152]{1,0:T(8,128)(2,1)}, u32[]{:S(2)}) %copy-start) | copy-done | bytes 3981336
  179.1 0.0 copy-start.1
  179.1 0.9 copy-done.1
  180.0 0.0 copy-start.3
  180.0 23.3 %update.1 = (f32[90,24,1152]{2,1,0:T(8,128)}, f32[90,24,1152]{2,1,0:T(8,128)}, f32[90,24,1152]{2,1,0:T(8,128)}) custom-call(s32[120]{0:T(128)S(1)} %copy-done.2, bf16[1728,1152]{1,0:T(8,128)(2,1)S(1)} %copy-done, f32[48,24,4]{2,1,0:T(8,128)S(1)} %bitcast.16, bf16[64,1152]{1,0:T(8,128)(2,1)S(1)} %copy-done.1, f32[90,24,1152]{2,1,0:T(8,128)} %master.1, ...), custom_call_target="tpu_custom_call" | custom-call | tf_op jit(solution)/shard_map/update/pallas_call | solution.py:1202
  203.3 0.0 copy-start.4
  203.3 0.0 copy-done.3
  203.3 1.6 convert_element_type.16
  204.9 0.1 copy-done.4
  205.0 1.0 copy.30
  (5 shorter events, 0.1 us)
Async XLA Ops:
  2.7 174.3 %copy-start.2 = (s32[120]{0:T(128)S(1)}, s32[120]{0:T(128)}, u32[]{:S(2)}) copy-start(s32[120]{0:T(128)} %owners.1) | copy-start | bytes 1444
  177.0 2.1 %copy-start = (bf16[1728,1152]{1,0:T(8,128)(2,1)S(1)}, bf16[1728,1152]{1,0:T(8,128)(2,1)}, u32[]{:S(2)}) copy-start(bf16[1728,1152]{1,0:T(8,128)(2,1)} %get-tuple-element.15.grads) | copy-start | bytes 11943940
  179.1 0.9 copy-start.1
  180.0 23.3 %copy-start.3 = (bf16[2,256,1152]{2,1,0:T(8,128)(2,1)S(1)}, bf16[2,256,1152]{2,1,0:T(8,128)(2,1)}, u32[]{:S(2)}) copy-start(bf16[2,256,1152]{2,1,0:T(8,128)(2,1)} %get-tuple-element.14) | copy-start | bytes 3538948
  203.3 1.7 copy-start.4

commit v3 on v2

--- a/solution.py
+++ b/solution.py
@@ -278,7 +278,6 @@
 F32 = jnp.float32
 MESH = pl.DeviceIdType.MESH
 TILE = 64
-HOP_ROWS = 16
 PAIR = 48
 GELU_C = math.sqrt(2.0 / math.pi)
 GELU_K = 0.044715
@@ -308,8 +307,9 @@
         self.dp_count, self.tensor_count = dp_count, tensor_count
         self.slots, self.block_rows = slots, block_rows
         self.images, self.seq = images, seq
-        self.rows = images * seq
-        self.shard = seq // tensor_count
+        self.parts = 2
+        self.part_rows = seq // self.parts
+        self.shard = self.part_rows // 4
         self.head_cols = D // tensor_count
         self.ffn_cols = FF // tensor_count
         self.heads = HEADS // tensor_count
@@ -323,15 +323,16 @@
         return (
             self.dp_count == 4
             and self.tensor_count == 8
+            and self.images == 2
             and 2 * self.block_rows == PAIR
-            and self.shard % HOP_ROWS == 0
-            and self.rows % TILE == 0
+            and self.slots % 3 == 0
+            and self.seq % 128 == 0
             and self.head_cols % PAIR == 0
             and self.ffn_cols % PAIR == 0
             and self.wide % (6 * PAIR) == 0
             and self.thin == D
+            and self.thin == 2 * self.ffn_cols
             and self.mod_rows <= 1024
-            and self.seq % 128 == 0
         )
 
 
@@ -356,42 +357,55 @@
     vm = pltpu.VMEM
     half = z.wide // PAIR // 2
 
-    def dp_sum():
+    def pairs():
+        return vm((half, PAIR, D), BF)
+
+    def attention():
+        names = 7
+        q, k, v, o, dq, dk, dv = (vm((z.seq, z.head_cols), BF) for _ in range(names))
+        return SimpleNamespace(q=q, k=k, v=v, o=o, dq=dq, dk=dk, dv=dv)
+
+    def hidden():
         return SimpleNamespace(
-            far=vm((half, PAIR, D), BF),
-            fin=vm((z.wide, D), BF),
-            s1=dma((half,)),
-            r1=dma((half,)),
-            s2=dma((half,)),
-            r2=dma((half,)),
-            s3=dma((half,)),
-            r3=dma((half,)),
-        )
-
-    def hop_sems():
-        return SimpleNamespace(xs=dma((4,)), xr=dma((4,)), zs=dma((3,)), zr=dma((3,)))
+            dgact=vm((z.seq, z.ffn_cols), F32),
+            gact=vm((z.seq, z.ffn_cols), BF),
+            dz=vm((z.seq, z.ffn_cols), BF),
+        )
 
     def scatter():
         return SimpleNamespace(
-            part=vm((z.seq, D), BF),
-            xin=vm((4, z.shard, D), BF),
-            zout=vm((3, z.shard, D), BF),
+            part=vm((z.part_rows, D), BF),
+            zout=vm((z.shard, D), BF),
             zin=vm((3, z.shard, D), BF),
-            own=vm((z.shard, D), F32),
-            sem=hop_sems(),
+            zs=dma((3,)),
+            zr=dma((3,)),
         )
 
     def gather():
-        return SimpleNamespace(buf=vm((z.seq, D), BF), sem=hop_sems())
+        return SimpleNamespace(buf=vm((z.part_rows, D), BF), zs=dma((3,)), zr=dma((3,)))
+
+    def gather_x():
+        return SimpleNamespace(
+            buf=vm((z.part_rows, D), BF),
+            xbuf=vm((z.part_rows, D), BF),
+            zs=dma((3,)),
+            zr=dma((3,)),
+            xs=dma((4,)),
+            xr=dma((4,)),
+        )
 
     def each(make):
-        return [make() for _ in range(z.images)]
+        return [make() for _ in range(z.parts)]
 
     return SimpleNamespace(
         slot_table=pltpu.SMEM((z.blocks,), jnp.int32),
         master=vm((z.slots, z.block_rows, D), F32),
         master_sem=dma((3,)),
+        x=vm((z.seq, D), BF),
+        grad=vm((z.seq, D), BF),
+        in_sem=dma((2,)),
         placed=vm((z.local_rows, D), BF),
+        extra=vm((4 * z.head_cols, D), BF),
         tok_all=vm((16 * z.dp_count, D), BF),
         tok_s=dma((3,)),
         tok_r=dma((3,)),
@@ -400,58 +414,81 @@
         mod_recv=vm((3, 16, 128), F32),
         mod_s=dma((3,)),
         mod_r=dma((3,)),
-        mod_own=vm((16, 128), F32),
         mod_all=vm((z.tensor_count, 16, 128), F32),
         moda_s=dma((z.tensor_count - 1,)),
         moda_r=dma((z.tensor_count - 1,)),
         modv=vm((8, D), F32),
-        time_qv=vm((8, 2 * 256), F32),
-        u=vm((z.rows, D), BF),
-        dmlp=vm((z.rows, D), BF),
-        q=vm((z.rows, z.head_cols), BF),
-        k=vm((z.rows, z.head_cols), BF),
-        v=vm((z.rows, z.head_cols), BF),
-        o=vm((z.rows, z.head_cols), BF),
-        dq=vm((z.rows, z.head_cols), BF),
-        dk=vm((z.rows, z.head_cols), BF),
-        dv=vm((z.rows, z.head_cols), BF),
-        soft=vm((z.images * z.heads, z.seq, z.seq), F32),
-        dgact=vm((z.rows, z.ffn_cols), F32),
-        gact=vm((z.rows, z.ffn_cols), BF),
-        dz=vm((z.rows, z.ffn_cols), BF),
-        h1=vm((z.images, z.shard, D), F32),
-        attn=vm((z.images, z.shard, D), F32),
-        dh1=vm((z.images, z.shard, D), F32),
+        time_qv=vm((8, 4 * 256), F32),
+        u=vm((z.seq, D), BF),
+        dmlp=vm((z.seq, D), BF),
+        heads=[attention(), attention()],
+        soft=vm((2 * z.heads, z.seq, z.seq), F32),
+        hid=[hidden(), hidden()],
+        h1=vm((z.parts, z.shard, D), F32),
+        attn=vm((z.parts, z.shard, D), F32),
+        dh1=vm((z.parts, z.shard, D), F32),
         dmod=vm((8, D), F32),
         dmod_pack=vm((z.tensor_count, 8, 128), F32),
         dmod_recv=vm((z.tensor_count - 1, 8, 128), F32),
         dmod_s=dma((z.tensor_count - 1,)),
         dmod_r=dma((z.tensor_count - 1,)),
+        dsum=vm((8, 256), F32),
+        dsum_in=vm((8, 256), F32),
+        dsum_s=dma((1,)),
+        dsum_r=dma((1,)),
         vec=vm((z.dp_count, 16, 256), F32),
         vec_s=dma((3,)),
         vec_r=dma((3,)),
-        out_sem=dma((3 + 2 * z.images,)),
-        w=dp_sum(),
-        g=dp_sum(),
-        w_sib=vm((half, PAIR, D), BF),
-        w_mrg=vm((half, PAIR, D), BF),
+        out_sem=dma((3 + 4 * z.parts,)),
+        sib=pairs(),
+        mrg=pairs(),
+        w=SimpleNamespace(
+            far=pairs(),
+            fin=vm((z.wide, D), BF),
+            oth=vm((z.wide, D), BF),
+            s1=dma((half,)),
+            r1=dma((half,)),
+            s2=dma((half,)),
+            r2=dma((half,)),
+            s3=dma((half,)),
+            r3=dma((half,)),
+            s4=dma((half,)),
+            r4=dma((half,)),
+            s5=dma((half,)),
+            r5=dma((half,)),
+        ),
+        g=SimpleNamespace(
+            far=pairs(),
+            fin=vm((z.wide, D), BF),
+            sib1=pairs(),
+            mrg1=pairs(),
+            xin=pairs(),
+            s0=dma((half,)),
+            r0=dma((half,)),
+            s1=dma((half,)),
+            r1=dma((half,)),
+            s2=dma((half,)),
+            r2=dma((half,)),
+            s3=dma((half,)),
+            r3=dma((half,)),
+            s4=dma((half,)),
+            r4=dma((half,)),
+        ),
         rs1=each(scatter),
         rs2=each(scatter),
         rs3=each(scatter),
         rs4=each(scatter),
         ag1=each(gather),
         ag2=each(gather),
-        ag3=each(gather),
-        ag4=each(gather),
+        ag3=each(gather_x),
+        ag4=each(gather_x),
     )
 
 
 def layer_kernel(z, plan, *refs):
-    owners, counts, held, tok, x_ref, grad_ref, master_hbm = refs[:7]
+    owners, counts, held, tok, x_hbm, grad_hbm, master_hbm = refs[:7]
     out_bo, out_ig, out_g, out_vec, out_tok = refs[7:12]
     s = rebuild(plan, iter(refs[12:]))
-    s.w.src, s.w.sib, s.w.mrg = s.placed, s.w_sib, s.w_mrg
-    s.g.src, s.g.sib, s.g.mrg = s.placed, s.w_sib, s.w_mrg
     nt_dims = (((1,), (1,)), ((), ()))
     tn_dims = (((0,), (0,)), ((), ()))
 
@@ -466,9 +503,13 @@
     dp, t = lax.axis_index("dp"), lax.axis_index("tensor")
     core = lax.rem(dp, 2)
     za, xb = t // 2, lax.rem(t, 2)
+    near_z = za + 1 - 2 * lax.rem(za, 2)
+    far_z = lax.rem(za + 2, 4)
+    cross_z = 3 - za
     sib = (dp + 1 - 2 * core, t)
     far = (lax.rem(dp + 2, 4), t)
     xp = (dp, t + 1 - 2 * xb)
+    near, across = (dp, 2 * near_z + xb), (dp, 2 * far_z + xb)
     half = z.wide // PAIR // 2
     head_part = (4 * hc) // PAIR // 2
     pending = []
@@ -486,7 +527,11 @@
         )
         for i in range(3)
     ]
-    for load in loads:
+    image_loads = [
+        pltpu.make_async_copy(x_hbm.at[xb], s.x, s.in_sem.at[0]),
+        pltpu.make_async_copy(grad_hbm.at[xb], s.grad, s.in_sem.at[1]),
+    ]
+    for load in loads + image_loads:
         load.start()
 
     barrier = pltpu.get_barrier_semaphore()
@@ -542,72 +587,142 @@
     shift_qkv = mod_pairs
     shift_rest = mod_pairs + time_pairs
 
-    def sum_step_one(ph, lower, upper):
-        def one(i, carry):
-            remote(
-                ph.src.at[rows_at((2 * i + 1 - core) * PAIR, PAIR)],
-                ph.sib.at[i],
-                ph.s1.at[i],
-                ph.r1.at[i],
-                sib,
-            ).start()
-            return carry
-
-        lax.fori_loop(lower, upper, one, 0)
-
-    def sum_step_two(ph, lower, upper):
-        def one(i, carry):
-            remote(
-                ph.src.at[rows_at((2 * i + 1 - core) * PAIR, PAIR)],
-                ph.sib.at[i],
-                ph.s1.at[i],
-                ph.r1.at[i],
-                sib,
-            ).wait()
-            mine = ph.src[rows_at((2 * i + core) * PAIR, PAIR), :].astype(F32)
-            ph.mrg[i] = (mine + ph.sib[i].astype(F32)).astype(BF)
-            remote(
-                ph.mrg.at[i],
-                ph.far.at[i],
-                ph.s2.at[i],
-                ph.r2.at[i],
-                far,
-            ).start()
-            return carry
-
-        lax.fori_loop(lower, upper, one, 0)
-
-    def final_copy(ph, i, side):
-        block = ph.fin.at[rows_at((2 * i + side) * PAIR, PAIR)]
-        return remote(block, block, ph.s3.at[i], ph.r3.at[i], sib)
-
-    def sum_step_three(ph, lower, upper):
-        def one(i, carry):
-            remote(
-                ph.mrg.at[i],
-                ph.far.at[i],
-                ph.s2.at[i],
-                ph.r2.at[i],
-                far,
-            ).wait()
-            total = ph.mrg[i].astype(F32) + ph.far[i].astype(F32)
-            ph.fin[rows_at((2 * i + core) * PAIR, PAIR), :] = total.astype(BF)
-            final_copy(ph, i, core).start()
-            return carry
-
-        lax.fori_loop(lower, upper, one, 0)
-
-    def sum_step_four(ph, lower, upper):
-        def one(i, carry):
-            final_copy(ph, i, core).wait_send()
-            final_copy(ph, i, 1 - core).wait_recv()
-            return carry
-
-        lax.fori_loop(lower, upper, one, 0)
+    def loop(lower, upper, body):
+        lax.fori_loop(lower, upper, lambda i, carry: (body(i), carry)[1], 0)
+
+    def pair_at(ref, i, side, first=0):
+        return ref.at[rows_at(first + (2 * i + side) * PAIR, PAIR)]
+
+    def w_core(i):
+        return remote(
+            pair_at(s.placed, i, 1 - core), s.sib.at[i], s.w.s1.at[i], s.w.r1.at[i], sib
+        )
+
+    def w_far(i):
+        return remote(s.mrg.at[i], s.w.far.at[i], s.w.s2.at[i], s.w.r2.at[i], far)
+
+    def w_back(i, side):
+        block = pair_at(s.w.fin, i, side)
+        return remote(block, block, s.w.s3.at[i], s.w.r3.at[i], sib)
+
+    def w_x(i):
+        return remote(
+            pair_at(s.w.fin, i, core),
+            pair_at(s.w.oth, i, core),
+            s.w.s4.at[i],
+            s.w.r4.at[i],
+            xp,
+        )
+
+    def w_pass(i, side):
+        block = pair_at(s.w.oth, i, side)
+        return remote(block, block, s.w.s5.at[i], s.w.r5.at[i], sib)
+
+    def w_one(lower, upper):
+        loop(lower, upper, lambda i: w_core(i).start())
+
+    def w_two(lower, upper):
+        def one(i):
+            w_core(i).wait()
+            mine = s.placed[rows_at((2 * i + core) * PAIR, PAIR), :].astype(F32)
+            s.mrg[i] = (mine + s.sib[i].astype(F32)).astype(BF)
+            w_far(i).start()
+
+        loop(lower, upper, one)
+
+    def w_three(lower, upper):
+        def one(i):
+            w_far(i).wait()
+            total = s.mrg[i].astype(F32) + s.w.far[i].astype(F32)
+            s.w.fin[rows_at((2 * i + core) * PAIR, PAIR), :] = total.astype(BF)
+            w_x(i).start()
+            w_back(i, core).start()
+
+        loop(lower, upper, one)
+
+    def w_four(lower, upper):
+        def one(i):
+            w_x(i).wait()
+            w_pass(i, core).start()
+
+        loop(lower, upper, one)
+
+    def w_end_own(lower, upper):
+        def one(i):
+            w_back(i, core).wait_send()
+            w_back(i, 1 - core).wait_recv()
+
+        loop(lower, upper, one)
+
+    def w_end_other(lower, upper):
+        def one(i):
+            w_pass(i, core).wait_send()
+            w_pass(i, 1 - core).wait_recv()
+
+        loop(lower, upper, one)
+
+    def g_core(i, index, src, first):
+        into, send, recv = ((s.sib, s.g.s0, s.g.r0), (s.g.sib1, s.g.s1, s.g.r1))[index]
+        return remote(
+            pair_at(src, i, 1 - core, first), into.at[i], send.at[i], recv.at[i], sib
+        )
+
+    def g_x(i):
+        return remote(s.g.mrg1.at[i], s.g.xin.at[i], s.g.s2.at[i], s.g.r2.at[i], xp)
+
+    def g_far(i):
+        return remote(s.mrg.at[i], s.g.far.at[i], s.g.s3.at[i], s.g.r3.at[i], far)
+
+    def g_back(i, side):
+        block = pair_at(s.g.fin, i, side)
+        return remote(block, block, s.g.s4.at[i], s.g.r4.at[i], sib)
+
+    def g_one(lower, upper, src, first):
+        def one(i):
+            g_core(i, 1, src, first).start()
+            g_core(i, 0, s.placed, 0).start()
+
+        loop(lower, upper, one)
+
+    def g_two(lower, upper, src, first):
+        def one(i):
+            g_core(i, 1, src, first).wait()
+            g_core(i, 0, s.placed, 0).wait()
+            mine = src[rows_at(first + (2 * i + core) * PAIR, PAIR), :].astype(F32)
+            s.g.mrg1[i] = (mine + s.g.sib1[i].astype(F32)).astype(BF)
+            g_x(i).start()
+
+        loop(lower, upper, one)
+
+    def g_three(lower, upper):
+        def one(i):
+            g_x(i).wait()
+            mine = s.placed[rows_at((2 * i + core) * PAIR, PAIR), :].astype(F32)
+            total = mine + s.sib[i].astype(F32) + s.g.xin[i].astype(F32)
+            s.mrg[i] = total.astype(BF)
+            g_far(i).start()
+
+        loop(lower, upper, one)
+
+    def g_four(lower, upper):
+        def one(i):
+            g_far(i).wait()
+            total = s.mrg[i].astype(F32) + s.g.far[i].astype(F32)
+            s.g.fin[rows_at((2 * i + core) * PAIR, PAIR), :] = total.astype(BF)
+            g_back(i, core).start()
+
+        loop(lower, upper, one)
+
+    def g_end(lower, upper):
+        def one(i):
+            g_back(i, core).wait_send()
+            g_back(i, 1 - core).wait_recv()
+
+        loop(lower, upper, one)
 
     place(0, qkv_pairs, shift_qkv)
     place(qkv_pairs, 2 * head_part, shift_rest)
-    sum_step_one(s.w, 0, head_part)
+    w_one(0, head_part)
     place(wide_pairs, wide_pairs + mod_pairs, -wide_pairs)
     place(wide_pairs + mod_pairs, all_pairs, -wide_pairs + qkv_pairs)
 
@@ -636,18 +751,15 @@
 
     for i in range(1, n_dp):
         go(mod_copy(i))
-    sum_step_two(s.w, 0, head_part)
+    w_two(0, head_part)
     place(2 * head_part, wide_pairs, shift_rest)
-    sum_step_one(s.w, head_part, half)
+    w_one(head_part, half)
     for i in range(1, n_dp):
         mod_copy(i).wait_recv()
-    s.mod_own[...] = (
-        s.mod_pack[dp] + s.mod_recv[0] + s.mod_recv[1] + s.mod_recv[2]
-    )
-    s.mod_all[t] = s.mod_own[...]
+    s.mod_all[t] = s.mod_pack[dp] + s.mod_recv[0] + s.mod_recv[1] + s.mod_recv[2]
 
     def mod_all_copy(i, member):
-        block = s.mod_all.at[member, pl.ds(0, 8)]
+        block = s.mod_all.at[member]
         return remote(
             block,
             block,
@@ -658,7 +770,7 @@
 
     for i in range(1, n_t):
         go(mod_all_copy(i, t))
-    sum_step_two(s.w, head_part, half)
+    w_two(head_part, half)
     for i in range(1, n_t):
         mod_all_copy(i, lax.rem(t - i + n_t, n_t)).wait_recv()
 
@@ -670,9 +782,12 @@
     def unpack_rows(block):
         return jnp.concatenate([block[i : i + 1, :] for i in range(block.shape[0])], axis=1)
 
-    own_line = spread(unpack_rows(s.mod_own[0 : D // 128, :]))
-    s.time_qv[:, 0:256] = pltpu.roll(own_line, D - z.mod_rows, 1)[:, 0:256]
-    s.time_qv[:, 256:512] = pltpu.roll(own_line, D - z.mod_rows - hc, 1)[:, 0:256]
+    for index, member in enumerate((t, t + 1 - 2 * xb)):
+        line = spread(unpack_rows(s.mod_all[member][0 : D // 128, :]))
+        moved = pltpu.roll(line, D - z.mod_rows, 1)
+        s.time_qv[:, 512 * index : 512 * index + 256] = moved[:, 0:256]
+        moved = pltpu.roll(line, D - z.mod_rows - hc, 1)
+        s.time_qv[:, 512 * index + 256 : 512 * index + 512] = moved[:, 0:256]
     lines = [jnp.zeros((8, D), F32) for _ in range(6)]
     for member in range(n_t):
         first = member * z.mod_rows
@@ -706,25 +821,27 @@
         (1, 1), count_sum, jnp.int32
     ).astype(F32)
 
-    def live_of(image):
-        return (jnp.full((1, 1), image, jnp.int32) < held[0]).astype(F32)
+    live = (jnp.full((1, 1), xb, jnp.int32) < held[0]).astype(F32)
+    for load in image_loads:
+        load.wait()
 
     def mix_tile(i, carry):
         at = rows_at(i * TILE, TILE)
-        normed, _ = norm_parts(x_ref[at, :].astype(F32))
+        normed, _ = norm_parts(s.x[at, :].astype(F32))
         s.u[at, :] = (normed * (1.0 + mod_line(1)) + mod_line(0)).astype(BF)
-        dy = grad_ref[at, :].astype(F32) * (group_scale * live_of(i * TILE // z.seq))
+        dy = s.grad[at, :].astype(F32) * (group_scale * live)
         s.dmlp[at, :] = (mod_line(5) * dy).astype(BF)
         return carry
 
-    lax.fori_loop(0, z.rows // TILE, mix_tile, 0)
-
-    sum_step_three(s.w, 0, head_part)
-    sum_step_four(s.w, 0, head_part)
-    w_fin = s.w.fin
-    w_q, w_k, w_v, w_p = (w_fin.at[i * hc : (i + 1) * hc] for i in range(4))
-    w_u = w_fin.at[4 * hc : 4 * hc + fc]
-    w_d = w_fin.at[4 * hc + fc : 4 * hc + 2 * fc]
+    lax.fori_loop(0, z.seq // TILE, mix_tile, 0)
+
+    sets = range(2)
+    weights = []
+    for ref in (s.w.fin, s.w.oth):
+        q, k, v, p = (ref.at[i * hc : (i + 1) * hc] for i in range(4))
+        up = ref.at[4 * hc : 4 * hc + fc]
+        down = ref.at[4 * hc + fc : 4 * hc + 2 * fc]
+        weights.append(SimpleNamespace(q=q, k=k, v=v, p=p, up=up, down=down))
 
     head_of = lax.broadcasted_iota(jnp.int32, (1, hc), 1) // HEAD_DIM
 
@@ -732,171 +849,183 @@
         return jnp.where(head_of == head, values, jnp.zeros_like(values))
 
     scale = HEAD_DIM ** (-0.5)
-    time_q = s.time_qv[0:1, 0:hc]
-    time_v = s.time_qv[0:1, 256 : 256 + hc]
-
-    def attend(image):
-        at = rows_at(image * z.seq, z.seq)
-        mixed = s.u[at, :]
-        q = (nt(mixed, w_q[...]) + time_q).astype(BF)
-        k = nt(mixed, w_k[...]).astype(BF)
-        v = (nt(mixed, w_v[...]) + time_v).astype(BF)
-        s.q[at, :] = q
-        s.k[at, :] = k
-        s.v[at, :] = v
+
+    def attend(index):
+        own, at = weights[index], s.heads[index]
+        mixed = s.u[...]
+        q_bias = s.time_qv[0:1, 512 * index : 512 * index + hc]
+        v_bias = s.time_qv[0:1, 512 * index + 256 : 512 * index + 256 + hc]
+        q = (nt(mixed, own.q[...]) + q_bias).astype(BF)
+        k = nt(mixed, own.k[...]).astype(BF)
+        v = (nt(mixed, own.v[...]) + v_bias).astype(BF)
+        at.q[...] = q
+        at.k[...] = k
+        at.v[...] = v
         out = jnp.zeros((z.seq, hc), F32)
         for head in range(z.heads):
             scores = nt(only(q, head), k) * scale
             e = jnp.exp(scores - jnp.max(scores, axis=-1, keepdims=True))
             p = e / jnp.sum(e, axis=-1, keepdims=True)
-            s.soft[image * z.heads + head] = p
+            s.soft[index * z.heads + head] = p
             out = out + times(p.astype(BF), only(v, head))
-        s.o[at, :] = out.astype(BF)
-        s.rs1[image].part[...] = times(out.astype(BF), w_p[...]).astype(BF)
+        at.o[...] = out.astype(BF)
 
     sh = z.shard
 
-    def rs_x(ph, k):
-        theirs = 2 * lax.rem(za + 1 + k, 4) + 1 - xb
-        part = ph.part.at[rows_at(theirs * sh, sh)]
-        return remote(part, ph.xin.at[k], ph.sem.xs.at[k], ph.sem.xr.at[k], xp)
+    def shard_of(ref, chip):
+        return ref.at[rows_at(chip * sh, sh)]
 
     def rs_z(ph, k):
-        device = (dp, 2 * lax.rem(za + 1 + k, 4) + xb)
-        return remote(ph.zout.at[k], ph.zin.at[k], ph.sem.zs.at[k], ph.sem.zr.at[k], device)
+        if k == 2:
+            return remote(ph.zout, ph.zin.at[2], ph.zs.at[2], ph.zr.at[2], across)
+        block = shard_of(ph.part, (cross_z, near_z)[k])
+        return remote(block, ph.zin.at[k], ph.zs.at[k], ph.zr.at[k], near)
 
     def rs_start(ph):
-        for k in range(4):
-            go(rs_x(ph, k))
+        go(rs_z(ph, 0))
+        go(rs_z(ph, 1))
 
     def rs_middle(ph):
-        for k in range(4):
-            rs_x(ph, k).wait_recv()
-            mine = 2 * lax.rem(za + 1 + k, 4) + xb
-            total = ph.part[rows_at(mine * sh, sh), :].astype(F32) + ph.xin[k].astype(F32)
-            if k < 3:
-                ph.zout[k] = total.astype(BF)
-                go(rs_z(ph, k))
-            else:
-                ph.own[...] = total
+        rs_z(ph, 0).wait_recv()
+        to_far = ph.part[rows_at(far_z * sh, sh), :].astype(F32)
+        ph.zout[...] = (to_far + ph.zin[0].astype(F32)).astype(BF)
+        go(rs_z(ph, 2))
 
     def rs_end(ph):
-        total = ph.own[...]
-        for k in range(3):
+        total = ph.part[rows_at(za * sh, sh), :].astype(F32)
+        for k in (1, 2):
             rs_z(ph, k).wait_recv()
             total = total + ph.zin[k].astype(F32)
         return total
 
-    def ag_z(ph, shard, k):
-        block = ph.buf.at[rows_at(shard * sh, sh)]
-        device = (dp, 2 * lax.rem(za + 1 + k, 4) + xb)
-        return remote(block, block, ph.sem.zs.at[k], ph.sem.zr.at[k], device)
-
-    def ag_x(ph, shard, k):
-        block = ph.buf.at[rows_at(shard * sh, sh)]
-        return remote(block, block, ph.sem.xs.at[k], ph.sem.xr.at[k], xp)
-
-    def ag_start(ph, value):
-        ph.buf[rows_at(t * sh, sh), :] = value
-        for k in range(3):
-            go(ag_z(ph, t, k))
-        go(ag_x(ph, t, 0))
-
-    def ag_middle(ph):
-        for k in range(3):
-            shard = 2 * lax.rem(za + 3 - k, 4) + xb
-            ag_z(ph, shard, k).wait_recv()
-            go(ag_x(ph, shard, k + 1))
-
-    def ag_end(ph):
-        for k in range(4):
-            ag_x(ph, 2 * lax.rem(za + 4 - k, 4) + 1 - xb, k).wait_recv()
-
-    images = range(z.images)
-    for i in images:
-        attend(i)
+    def ag_z(ph, chip, k):
+        block = shard_of(ph.buf, chip)
+        return remote(block, block, ph.zs.at[k], ph.zr.at[k], across if k == 0 else near)
+
+    def ag_x(ph, chip, k):
+        source, target = shard_of(ph.buf, chip), shard_of(ph.xbuf, chip)
+        return remote(source, target, ph.xs.at[k], ph.xr.at[k], xp)
+
+    def ag_start(ph, value, out=False):
+        ph.buf[rows_at(za * sh, sh), :] = value
+        go(ag_z(ph, za, 0))
+        go(ag_z(ph, za, 1))
+        if out:
+            go(ag_x(ph, za, 0))
+
+    def ag_middle(ph, out=False):
+        ag_z(ph, far_z, 0).wait_recv()
+        go(ag_z(ph, far_z, 2))
+        if out:
+            go(ag_x(ph, far_z, 1))
+
+    def ag_end(ph, out=False):
+        ag_z(ph, near_z, 1).wait_recv()
+        if out:
+            go(ag_x(ph, near_z, 2))
+        ag_z(ph, cross_z, 2).wait_recv()
+        if out:
+            go(ag_x(ph, cross_z, 3))
+
+    def ag_end_x(ph):
+        for k, chip in enumerate((za, far_z, near_z, cross_z)):
+            ag_x(ph, chip, k).wait_recv()
+
+    parts = range(z.parts)
+    quarter = (half - head_part) // 4
+
+    def part_at(part):
+        return slice(part * z.part_rows, (part + 1) * z.part_rows)
+
+    w_three(0, head_part)
+    w_end_own(0, head_part)
+    attend(0)
+    w_four(0, head_part)
+    w_end_other(0, head_part)
+    attend(1)
+    for i in parts:
+        total = 0.0
+        for index in sets:
+            total = total + times(s.heads[index].o[part_at(i), :], weights[index].p[...])
+        s.rs1[i].part[...] = total.astype(BF)
         rs_start(s.rs1[i])
-    for i in images:
+    w_three(head_part, head_part + 2 * quarter)
+    for i in parts:
         rs_middle(s.rs1[i])
 
-    def mine_at(image):
-        return rows_at(image * z.seq + t * sh, sh)
-
-    for i in images:
+    def mine_at(part):
+        return rows_at(part * z.part_rows + za * sh, sh)
+
+    w_four(head_part, head_part + quarter)
+    for i in parts:
         attn = rs_end(s.rs1[i])
-        h1 = x_ref[mine_at(i), :].astype(F32) + mod_line(2) * attn
+        h1 = s.x[mine_at(i), :].astype(F32) + mod_line(2) * attn
         normed_m, _ = norm_parts(h1)
         ag_start(s.ag1[i], (normed_m * (1.0 + mod_line(4)) + mod_line(3)).astype(BF))
         s.attn[i] = attn
         s.h1[i] = h1
-    ag_middle(s.ag1[0])
-    sum_step_three(s.w, head_part, half)
-    for i in images[1:]:
+    w_three(head_part + 2 * quarter, half)
+    for i in parts:
         ag_middle(s.ag1[i])
-    sum_step_four(s.w, head_part, half)
-
-    step_rows = 128
-
-    def up_tile(i, carry):
-        at = rows_at(i * step_rows, step_rows)
-        s.dgact[at, :] = nt(s.dmlp[at, :], w_d[...])
-        return carry
-
-    lax.fori_loop(0, z.rows // step_rows, up_tile, 0)
-
-    def mlp(image):
-        def tile(i, carry):
-            at = rows_at(image * z.seq + i * step_rows, step_rows)
-            hidden = nt(s.ag1[image].buf[rows_at(i * step_rows, step_rows), :], w_u[...])
+    w_four(head_part + quarter, half)
+    w_end_own(head_part, half)
+    w_end_other(head_part, half)
+
+    for index in sets:
+        s.hid[index].dgact[...] = nt(s.dmlp[...], weights[index].down[...])
+
+    def mlp(part):
+        at = part_at(part)
+        total = 0.0
+        for index in sets:
+            hid = s.hid[index]
+            hidden = nt(s.ag1[part].buf[...], weights[index].up[...])
             square = hidden * hidden
             bend = jnp.tanh(GELU_C * hidden * (1.0 + GELU_K * square))
-            s.gact[at, :] = (0.5 * hidden * (1.0 + bend)).astype(BF)
+            hid.gact[at, :] = (0.5 * hidden * (1.0 + bend)).astype(BF)
             slope = 0.5 * (1.0 + bend) + 0.5 * hidden * (1.0 - bend * bend) * (
                 GELU_C * (1.0 + 3.0 * GELU_K * square)
             )
-            dz = (s.dgact[at, :] * slope).astype(BF)
-            s.dz[at, :] = dz
-            s.rs2[image].part[rows_at(i * step_rows, step_rows), :] = times(dz, w_u[...]).astype(BF)
-            return carry
-
-        lax.fori_loop(0, z.seq // step_rows, tile, 0)
-
-    def down(image):
-        def tile(i, carry):
-            at = rows_at(image * z.seq + i * step_rows, step_rows)
-            s.rs4[image].part[rows_at(i * step_rows, step_rows), :] = times(
-                s.gact[at, :], w_d[...]
-            ).astype(BF)
-            return carry
-
-        lax.fori_loop(0, z.seq // step_rows, tile, 0)
-
-    for i in images:
+            dz = (hid.dgact[at, :] * slope).astype(BF)
+            hid.dz[at, :] = dz
+            total = total + times(dz, weights[index].up[...])
+        s.rs2[part].part[...] = total.astype(BF)
+
+    def down(part):
+        total = 0.0
+        for index in sets:
+            total = total + times(s.hid[index].gact[part_at(part), :], weights[index].down[...])
+        s.rs4[part].part[...] = total.astype(BF)
+
+    for i in parts:
         ag_end(s.ag1[i])
         mlp(i)
         rs_start(s.rs2[i])
-    for i in images:
-        rs_middle(s.rs2[i])
 
     cols = 384
 
-    def over_images(left, gathered, at):
+    def over_parts(left, gathered, at):
         total = 0.0
-        for image in images:
-            total = total + tn(
-                left[image * z.seq : (image + 1) * z.seq, :], gathered[image].buf[:, at]
-            )
+        for part in parts:
+            total = total + tn(left[part_at(part), :], gathered[part].buf[:, at])
         return total.astype(BF)
 
     def grad_tile(i, carry):
         at = pl.ds(pl.multiple_of(i * cols, 128), cols)
-        s.g.src[4 * hc : 4 * hc + fc, at] = over_images(s.dz, s.ag1, at)
-        s.g.src[4 * hc + fc : z.wide, at] = tn(s.gact[...], s.dmlp[:, at]).astype(BF)
+        for index, first in ((1, z.wide), (0, 4 * hc)):
+            hid = s.hid[index]
+            s.placed[first : first + fc, at] = over_parts(hid.dz, s.ag1, at)
+            down_grad = tn(hid.gact[...], s.dmlp[:, at]).astype(BF)
+            s.placed[first + fc : first + 2 * fc, at] = down_grad
         return carry
 
     lax.fori_loop(0, D // cols, grad_tile, 0)
-    sum_step_one(s.g, head_part, half)
-    for i in images:
+    first_one = z.wide - 4 * hc
+    g_one(head_part, half, s.placed, first_one)
+    for i in parts:
+        rs_middle(s.rs2[i])
+    g_two(head_part, half, s.placed, first_one)
+    for i in parts:
         down(i)
 
     def norm_back_of(normed, inverse, upstream):
@@ -909,11 +1038,13 @@
     def column_sum(values):
         return jnp.sum(values, axis=0, keepdims=True)
 
-    def dy_of(image):
-        return grad_ref[mine_at(image), :].astype(F32) * (group_scale * live_of(image))
-
+    def dy_of(part):
+        return s.grad[mine_at(part), :].astype(F32) * (group_scale * live)
+
+    step = (half - head_part) // 6
+    g_three(head_part, head_part + step)
     gate_a_sum = shift_m_sum = scale_m_sum = 0.0
-    for i in images:
+    for i in parts:
         dw = rs_end(s.rs2[i])
         normed_m, inverse_m = norm_parts(s.h1[i])
         dh1 = dy_of(i) + norm_back_of(normed_m, inverse_m, dw * (1.0 + mod_line(4)))
@@ -925,19 +1056,23 @@
     s.dmod[2:3, :] = gate_a_sum
     s.dmod[3:4, :] = shift_m_sum
     s.dmod[4:5, :] = scale_m_sum
-    for i in images:
+    g_three(head_part + step, head_part + 2 * step)
+    for i in parts:
         ag_middle(s.ag2[i])
-    sum_step_two(s.g, head_part, half)
-
-    def attend_back(image):
-        at = rows_at(image * z.seq, z.seq)
-        do = nt(s.ag2[image].buf[...], w_p[...]).astype(BF)
-        q, k, v = s.q[at, :], s.k[at, :], s.v[at, :]
+    for i in parts:
+        rs_start(s.rs4[i])
+    g_three(head_part + 2 * step, head_part + 3 * step)
+
+    def attend_back(index):
+        own, at = weights[index], s.heads[index]
+        do = jnp.concatenate([nt(s.ag2[i].buf[...], own.p[...]) for i in parts], axis=0)
+        do = do.astype(BF)
+        q, k, v = at.q[...], at.k[...], at.v[...]
         dq = jnp.zeros((z.seq, hc), F32)
         dk = jnp.zeros((z.seq, hc), F32)
         dv = jnp.zeros((z.seq, hc), F32)
         for head in range(z.heads):
-            p = s.soft[image * z.heads + head]
+            p = s.soft[index * z.heads + head]
             do_head = only(do, head)
             dp_soft = nt(do_head, v)
             inner = jnp.sum(p * dp_soft, axis=-1, keepdims=True)
@@ -945,55 +1080,69 @@
             dq = dq + times(ds, only(k, head))
             dk = dk + tn(ds, only(q, head))
             dv = dv + tn(p.astype(BF), do_head)
-        dq = (dq * scale).astype(BF)
-        dk = (dk * scale).astype(BF)
-        dv = dv.astype(BF)
-        s.dq[at, :] = dq
-        s.dk[at, :] = dk
-        s.dv[at, :] = dv
-        s.rs3[image].part[...] = (
-            times(dq, w_q[...]) + times(dk, w_k[...]) + times(dv, w_v[...])
-        ).astype(BF)
-
-    for i in images:
+        at.dq[...] = (dq * scale).astype(BF)
+        at.dk[...] = (dk * scale).astype(BF)
+        at.dv[...] = dv.astype(BF)
+
+    for i in parts:
         ag_end(s.ag2[i])
-        attend_back(i)
+    for index in sets:
+        attend_back(index)
+    for i in parts:
+        total = 0.0
+        for index in sets:
+            own, at = weights[index], s.heads[index]
+            rows = part_at(i)
+            total = total + times(at.dq[rows, :], own.q[...])
+            total = total + times(at.dk[rows, :], own.k[...])
+            total = total + times(at.dv[rows, :], own.v[...])
+        s.rs3[i].part[...] = total.astype(BF)
         rs_start(s.rs3[i])
-        rs_start(s.rs4[i])
-    for i in images:
-        rs_middle(s.rs3[i])
+    for i in parts:
         rs_middle(s.rs4[i])
 
     def attn_grad_tile(i, carry):
         at = pl.ds(pl.multiple_of(i * cols, 128), cols)
         mixed = s.u[:, at]
-        s.g.src[0:hc, at] = tn(s.dq[...], mixed).astype(BF)
-        s.g.src[hc : 2 * hc, at] = tn(s.dk[...], mixed).astype(BF)
-        s.g.src[2 * hc : 3 * hc, at] = tn(s.dv[...], mixed).astype(BF)
-        s.g.src[3 * hc : 4 * hc, at] = over_images(s.o, s.ag2, at)
+        for index, target in ((1, s.extra), (0, s.placed)):
+            own = s.heads[index]
+            target[0:hc, at] = tn(own.dq[...], mixed).astype(BF)
+            target[hc : 2 * hc, at] = tn(own.dk[...], mixed).astype(BF)
+            target[2 * hc : 3 * hc, at] = tn(own.dv[...], mixed).astype(BF)
+            target[3 * hc : 4 * hc, at] = over_parts(own.o, s.ag2, at)
         return carry
 
     lax.fori_loop(0, D // cols, attn_grad_tile, 0)
-    sum_step_one(s.g, 0, head_part)
+    g_one(0, head_part, s.extra, 0)
+    for i in parts:
+        rs_middle(s.rs3[i])
+    g_two(0, head_part, s.extra, 0)
+
+    def dsum_copy():
+        return remote(s.dsum, s.dsum_in, s.dsum_s.at[0], s.dsum_r.at[0], xp)
+
+    s.dsum[...] = jnp.zeros((8, 256), F32)
+    s.dsum[0:1, 0:hc] = column_sum(s.heads[1].dq[...].astype(F32))
+    s.dsum[1:2, 0:hc] = column_sum(s.heads[1].dv[...].astype(F32))
+    go(dsum_copy())
+    g_three(head_part + 3 * step, head_part + 5 * step)
+
     shift_a_sum = scale_a_sum = gate_m_sum = 0.0
-    for i in images:
+    for i in parts:
         du = rs_end(s.rs3[i])
-        normed_a, inverse_a = norm_parts(x_ref[mine_at(i), :].astype(F32))
+        normed_a, inverse_a = norm_parts(s.x[mine_at(i), :].astype(F32))
         dx = s.dh1[i] + norm_back_of(normed_a, inverse_a, du * (1.0 + mod_line(1)))
-        ag_start(s.ag3[i], dx.astype(BF))
+        ag_start(s.ag3[i], dx.astype(BF), True)
         shift_a_sum = shift_a_sum + column_sum(du)
         scale_a_sum = scale_a_sum + column_sum(du * normed_a)
+    for i in parts:
         mlp_sum = rs_end(s.rs4[i])
         gate_m_sum = gate_m_sum + column_sum(dy_of(i) * mlp_sum)
-        result = (s.h1[i] + mod_line(5) * mlp_sum) * live_of(i)
-        ag_start(s.ag4[i], result.astype(BF))
+        result = (s.h1[i] + mod_line(5) * mlp_sum) * live
+        ag_start(s.ag4[i], result.astype(BF), True)
     s.dmod[0:1, :] = shift_a_sum
     s.dmod[1:2, :] = scale_a_sum
     s.dmod[5:6, :] = gate_m_sum
-    sum_step_two(s.g, 0, head_part)
-    s.vec[dp] = jnp.zeros((16, 256), F32)
-    s.vec[dp, 8:9, 0:hc] = column_sum(s.dq[...].astype(F32))
-    s.vec[dp, 9:10, 0:hc] = column_sum(s.dv[...].astype(F32))
     s.dmod[6:8, :] = jnp.zeros((2, D), F32)
 
     dlines = [spread(s.dmod[i : i + 1, :]) for i in range(6)]
@@ -1022,15 +1171,25 @@
 
     for i in range(1, n_t):
         go(dmod_copy(i))
-    for i in images:
-        ag_middle(s.ag3[i])
-        ag_middle(s.ag4[i])
-    sum_step_three(s.g, 0, half)
+    g_three(head_part + 5 * step, half)
+    for i in parts:
+        ag_middle(s.ag3[i], True)
+        ag_middle(s.ag4[i], True)
+    g_three(0, head_part)
+    g_four(head_part, half)
+    for i in parts:
+        ag_end(s.ag3[i], True)
+        ag_end(s.ag4[i], True)
+    dsum_copy().wait_recv()
     total = s.dmod_pack[t]
     for i in range(1, n_t):
         dmod_copy(i).wait_recv()
         total = total + s.dmod_recv[i - 1]
+    s.vec[dp] = jnp.zeros((16, 256), F32)
     s.vec[dp, 0:8, 0:128] = total
+    own_sums = (column_sum(s.heads[0].dq[...].astype(F32)), column_sum(s.heads[0].dv[...].astype(F32)))
+    s.vec[dp, 8:9, 0:hc] = own_sums[0] + s.dsum_in[0:1, 0:hc]
+    s.vec[dp, 9:10, 0:hc] = own_sums[1] + s.dsum_in[1:2, 0:hc]
 
     def vec_copy(i, group):
         return remote(
@@ -1043,19 +1202,22 @@
 
     for i in range(1, n_dp):
         go(vec_copy(i, dp))
-    sum_step_four(s.g, 0, half)
-    for i in images:
-        ag_end(s.ag3[i])
-        ag_end(s.ag4[i])
+    g_four(0, head_part)
+    g_end(0, half)
+    for i in parts:
+        ag_end_x(s.ag3[i])
+        ag_end_x(s.ag4[i])
     for i in range(1, n_dp):
         vec_copy(i, lax.rem(dp - i + n_dp, n_dp)).wait_recv()
     for copy in pending:
         copy.wait_send()
 
     outs = [(s.g.fin, out_g), (s.vec, out_vec), (s.tok_all, out_tok)]
-    for i in images:
-        outs.append((s.ag4[i].buf, out_bo.at[i]))
-        outs.append((s.ag3[i].buf, out_ig.at[i]))
+    for i in parts:
+        at = pl.ds(i * z.part_rows, z.part_rows)
+        for ph, out in ((s.ag4[i], out_bo), (s.ag3[i], out_ig)):
+            outs.append((ph.buf, out.at[xb, at]))
+            outs.append((ph.xbuf, out.at[1 - xb, at]))
     stores = [
         pltpu.make_async_copy(src, dst, s.out_sem.at[i]) for i, (src, dst) in enumerate(outs)
     ]
@@ -1159,7 +1321,7 @@
     smem = pl.BlockSpec(memory_space=pltpu.SMEM)
     vmem = pl.BlockSpec(memory_space=pltpu.VMEM)
     hbm = pl.BlockSpec(memory_space=pl.ANY)
-    flops = 6 * z.rows * D * z.wide
+    flops = 12 * z.seq * D * z.wide
     block_output, input_grad, grads, vectors, tokens = pl.pallas_call(
         partial(layer_kernel, z, plan),
         out_shape=(
@@ -1169,14 +1331,14 @@
             jax.ShapeDtypeStruct((z.dp_count, 16, 256), F32),
             jax.ShapeDtypeStruct((16 * z.dp_count, D), BF),
         ),
-        in_specs=[smem, smem, smem, vmem, vmem, vmem, hbm],
+        in_specs=[smem, smem, smem, vmem, hbm, hbm, hbm],
         out_specs=(hbm,) * 5,
         scratch_shapes=flatten(plan),
         compiler_params=pltpu.CompilerParams(
             collective_id=0, has_side_effects=True, vmem_limit_bytes=62 * 2**20
         ),
         cost_estimate=pl.CostEstimate(
-            flops=flops, bytes_accessed=20 * 2**20, transcendentals=z.rows * z.ffn_cols
+            flops=flops, bytes_accessed=20 * 2**20, transcendentals=2 * z.seq * z.ffn_cols
         ),
         name="layer",
     )(
@@ -1184,8 +1346,8 @@
         counts,
         images_held,
         token,
-        inputs.reshape(z.rows, D),
-        out_grad.reshape(z.rows, D),
+        inputs,
+        out_grad,
         master_weight,
     )
     columns = jnp.concatenate(

time: 209 us -> 196 us (0.938)
  Pallas kernels: 196 us -> 184 us
    pallas_call x1, Pallas kernels: 172 us -> 161 us  [per_device_fast(): pl.pallas_call(partial(layer_kernel, z, plan), out_shape=(jax.ShapeDtypeS...]
where the time goes in v3:
time: 196 us; the launch traced here: 194 us
  Pallas kernels  184 us (94%)
  local copies, waits for them, and re-layouts  6.77 us (3%)
  between operations  2 us (1%)
    pallas_call x1, Pallas kernels, per_device_fast(): pl.pallas_call(partial(layer_kernel, z, plan), out_shape=(jax.ShapeDtypeS...  161 us
    pallas_call x1, Pallas kernels, per_device_fast(): pl.pallas_call(partial(update_kernel, z, group_slots), grid=(z.slots // g...  23 us
    unnamed x15, local copies, waits for them, and re-layouts  4.91 us

profile of v3, /device:TPU:0, one launch (start us, length us, event | category | flops | bytes accessed | tf_op | source)
XLA Modules:
  0.0 194.3 jit_solution(1293029449649635303)
XLA Ops:
  1.3 0.1 multiply_convert_fusion
  1.4 0.6 broadcast_in_dim.2.refs_3_
  2.7 0.0 copy-start.2
  2.7 160.8 %layer.1 = (bf16[2,256,1152]{2,1,0:T(8,128)(2,1)}, bf16[2,256,1152]{2,1,0:T(8,128)(2,1)}, bf16[1728,1152]{1,0:T(8,128)(2,1)}, f32[4,16,256]{2,1,0:T(8,128)}, bf16[64,1152]{1,0:T(8,128)(2,1)}) custom-call(s32[120]{0:T(128)} %owners.1, s32[4]{0:T(128)} %refs_1_.1, s32[1]{0:T(128)S(6)} %copy.29.refs_2_, bf16[16,1152]{1,0:T(8,128)(2,1)} %broadcast_in_dim.2.refs_3_, ...), custom_call_target="tpu_custom_call" | custom-call | flops 6115295232 | bytes 20971520 | tf_op jit(solution)/shard_map/layer/pallas_call | solution.py:1325
  163.6 0.9 fusion.2
  164.5 0.7 slice_bitcast_fusion
  165.2 0.1 concatenate.14
  165.3 0.2 copy.17
  165.5 0.0 copy-done.2
  165.6 0.0 copy-start
  165.6 2.1 %copy-done = bf16[1728,1152]{1,0:T(8,128)(2,1)S(1)} copy-done((bf16[1728,1152]{1,0:T(8,128)(2,1)S(1)}, bf16[1728,1152]{1,0:T(8,128)(2,1)}, u32[]{:S(2)}) %copy-start) | copy-done | bytes 3981336
  167.7 0.0 copy-start.1
  167.7 0.9 copy-done.1
  168.6 0.0 copy-start.3
  168.6 23.0 %update.1 = (f32[90,24,1152]{2,1,0:T(8,128)}, f32[90,24,1152]{2,1,0:T(8,128)}, f32[90,24,1152]{2,1,0:T(8,128)}) custom-call(s32[120]{0:T(128)S(1)} %copy-done.2, bf16[1728,1152]{1,0:T(8,128)(2,1)S(1)} %copy-done, f32[48,24,4]{2,1,0:T(8,128)S(1)} %bitcast.14, bf16[64,1152]{1,0:T(8,128)(2,1)S(1)} %copy-done.1, f32[90,24,1152]{2,1,0:T(8,128)} %master.1, ...), custom_call_target="tpu_custom_call" | custom-call | tf_op jit(solution)/shard_map/update/pallas_call | solution.py:1364
  191.6 0.0 copy-start.4
  191.6 0.0 copy-done.3
  191.6 1.6 convert_element_type.16
  193.1 0.1 copy-done.4
  193.3 1.0 copy.30
  (5 shorter events, 0.1 us)
Async XLA Ops:
  2.7 162.8 %copy-start.2 = (s32[120]{0:T(128)S(1)}, s32[120]{0:T(128)}, u32[]{:S(2)}) copy-start(s32[120]{0:T(128)} %owners.1) | copy-start | bytes 1444
  165.6 2.1 %copy-start = (bf16[1728,1152]{1,0:T(8,128)(2,1)S(1)}, bf16[1728,1152]{1,0:T(8,128)(2,1)}, u32[]{:S(2)}) copy-start(bf16[1728,1152]{1,0:T(8,128)(2,1)} %get-tuple-element.15.grads) | copy-start | bytes 11943940
  167.7 0.9 copy-start.1
  168.6 23.0 %copy-start.3 = (bf16[2,256,1152]{2,1,0:T(8,128)(2,1)S(1)}, bf16[2,256,1152]{2,1,0:T(8,128)(2,1)}, u32[]{:S(2)}) copy-start(bf16[2,256,1152]{2,1,0:T(8,128)(2,1)} %get-tuple-element.14) | copy-start | bytes 3538948
  191.6 1.7 copy-start.4

commit v4 on v3

--- a/solution.py
+++ b/solution.py
@@ -277,7 +277,9 @@
 BF = jnp.bfloat16
 F32 = jnp.float32
 MESH = pl.DeviceIdType.MESH
+axes = ("dp", "tensor")
 TILE = 64
+LAG = 2
 PAIR = 48
 GELU_C = math.sqrt(2.0 / math.pi)
 GELU_K = 0.044715
@@ -367,7 +369,7 @@
 
     def hidden():
         return SimpleNamespace(
-            dgact=vm((z.seq, z.ffn_cols), F32),
+            slope=vm((z.seq, z.ffn_cols), F32),
             gact=vm((z.seq, z.ffn_cols), BF),
             dz=vm((z.seq, z.ffn_cols), BF),
         )
@@ -384,16 +386,6 @@
     def gather():
         return SimpleNamespace(buf=vm((z.part_rows, D), BF), zs=dma((3,)), zr=dma((3,)))
 
-    def gather_x():
-        return SimpleNamespace(
-            buf=vm((z.part_rows, D), BF),
-            xbuf=vm((z.part_rows, D), BF),
-            zs=dma((3,)),
-            zr=dma((3,)),
-            xs=dma((4,)),
-            xr=dma((4,)),
-        )
-
     def each(make):
         return [make() for _ in range(z.parts)]
 
@@ -404,7 +396,8 @@
         x=vm((z.seq, D), BF),
         grad=vm((z.seq, D), BF),
         in_sem=dma((2,)),
-        placed=vm((z.local_rows, D), BF),
+        placed=vm((z.wide, D), BF),
+        thin=vm((z.thin, D), BF),
         extra=vm((4 * z.head_cols, D), BF),
         tok_all=vm((16 * z.dp_count, D), BF),
         tok_s=dma((3,)),
@@ -439,7 +432,7 @@
         vec=vm((z.dp_count, 16, 256), F32),
         vec_s=dma((3,)),
         vec_r=dma((3,)),
-        out_sem=dma((3 + 4 * z.parts,)),
+        out_sem=dma((3 + 2 * z.parts,)),
         sib=pairs(),
         mrg=pairs(),
         w=SimpleNamespace(
@@ -480,15 +473,15 @@
         rs4=each(scatter),
         ag1=each(gather),
         ag2=each(gather),
-        ag3=each(gather_x),
-        ag4=each(gather_x),
+        ag3=each(gather),
+        ag4=each(gather),
     )
 
 
 def layer_kernel(z, plan, *refs):
     owners, counts, held, tok, x_hbm, grad_hbm, master_hbm = refs[:7]
-    out_bo, out_ig, out_g, out_vec, out_tok = refs[7:12]
-    s = rebuild(plan, iter(refs[12:]))
+    out_own, out_g, out_vec, out_tok = refs[7:11]
+    s = rebuild(plan, iter(refs[11:]))
     nt_dims = (((1,), (1,)), ((), ()))
     tn_dims = (((0,), (0,)), ((), ()))
 
@@ -569,21 +562,21 @@
     for load in loads:
         load.wait()
 
-    def place(lower, upper, shift):
+    def place(into, lower, upper, shift):
         def one(pair, carry):
             halves = []
             for side in range(2):
                 slot = s.slot_table[2 * (pair + shift) + side]
                 block = s.master[jnp.clip(slot, 0, z.slots - 1)]
                 halves.append(jnp.where(slot >= 0, block, 0.0))
-            s.placed[rows_at(pair * PAIR, PAIR), :] = jnp.concatenate(halves, axis=0).astype(BF)
+            into[rows_at(pair * PAIR, PAIR), :] = jnp.concatenate(halves, axis=0).astype(BF)
             return carry
 
         lax.fori_loop(lower, upper, one, 0)
 
     qkv_pairs, mod_pairs = 3 * hc // PAIR, z.mod_rows // PAIR
     time_pairs = 2 * hc // PAIR
-    wide_pairs, all_pairs = z.wide // PAIR, z.local_rows // PAIR
+    wide_pairs = z.wide // PAIR
     shift_qkv = mod_pairs
     shift_rest = mod_pairs + time_pairs
 
@@ -630,22 +623,23 @@
 
         loop(lower, upper, one)
 
-    def w_three(lower, upper):
-        def one(i):
-            w_far(i).wait()
-            total = s.mrg[i].astype(F32) + s.w.far[i].astype(F32)
-            s.w.fin[rows_at((2 * i + core) * PAIR, PAIR), :] = total.astype(BF)
-            w_x(i).start()
-            w_back(i, core).start()
-
-        loop(lower, upper, one)
-
-    def w_four(lower, upper):
-        def one(i):
-            w_x(i).wait()
-            w_pass(i, core).start()
-
-        loop(lower, upper, one)
+    def w_three(i):
+        w_far(i).wait()
+        total = s.mrg[i].astype(F32) + s.w.far[i].astype(F32)
+        s.w.fin[rows_at((2 * i + core) * PAIR, PAIR), :] = total.astype(BF)
+        w_x(i).start()
+        w_back(i, core).start()
+
+    def w_four(i):
+        w_x(i).wait()
+        w_pass(i, core).start()
+
+    def w_steps(lower, upper):
+        for i in range(lower, upper):
+            if i < half:
+                w_three(i)
+            if 0 <= i - LAG < half:
+                w_four(i - LAG)
 
     def w_end_own(lower, upper):
         def one(i):
@@ -677,41 +671,45 @@
         block = pair_at(s.g.fin, i, side)
         return remote(block, block, s.g.s4.at[i], s.g.r4.at[i], sib)
 
-    def g_one(lower, upper, src, first):
-        def one(i):
-            g_core(i, 1, src, first).start()
-            g_core(i, 0, s.placed, 0).start()
-
-        loop(lower, upper, one)
+    def g_one(index, lower, upper, src, first):
+        loop(lower, upper, lambda i: g_core(i, index, src, first).start())
 
     def g_two(lower, upper, src, first):
         def one(i):
             g_core(i, 1, src, first).wait()
-            g_core(i, 0, s.placed, 0).wait()
             mine = src[rows_at(first + (2 * i + core) * PAIR, PAIR), :].astype(F32)
             s.g.mrg1[i] = (mine + s.g.sib1[i].astype(F32)).astype(BF)
-            g_x(i).start()
 
         loop(lower, upper, one)
 
-    def g_three(lower, upper):
-        def one(i):
-            g_x(i).wait()
-            mine = s.placed[rows_at((2 * i + core) * PAIR, PAIR), :].astype(F32)
-            total = mine + s.sib[i].astype(F32) + s.g.xin[i].astype(F32)
-            s.mrg[i] = total.astype(BF)
-            g_far(i).start()
-
-        loop(lower, upper, one)
-
-    def g_four(lower, upper):
-        def one(i):
-            g_far(i).wait()
-            total = s.mrg[i].astype(F32) + s.g.far[i].astype(F32)
-            s.g.fin[rows_at((2 * i + core) * PAIR, PAIR), :] = total.astype(BF)
-            g_back(i, core).start()
-
-        loop(lower, upper, one)
+    def g_two_own(lower, upper):
+        loop(lower, upper, lambda i: g_core(i, 0, s.placed, 0).wait())
+
+    def g_three(i):
+        g_x(i).wait()
+        mine = s.placed[rows_at((2 * i + core) * PAIR, PAIR), :].astype(F32)
+        total = mine + s.sib[i].astype(F32) + s.g.xin[i].astype(F32)
+        s.mrg[i] = total.astype(BF)
+        g_far(i).start()
+
+    def g_four(i):
+        g_far(i).wait()
+        total = s.mrg[i].astype(F32) + s.g.far[i].astype(F32)
+        s.g.fin[rows_at((2 * i + core) * PAIR, PAIR), :] = total.astype(BF)
+        g_back(i, core).start()
+
+    thirds = head_part, head_part + (half - head_part) // 2, half
+    g_order = list(range(thirds[1], half)) + list(range(head_part, thirds[1]))
+    g_order += list(range(head_part))
+
+    def g_steps(lower, upper):
+        for k in range(lower, upper):
+            if k < half:
+                g_three(g_order[k])
+            if k + LAG < half:
+                g_x(g_order[k + LAG]).start()
+            if 0 <= k - LAG < half:
+                g_four(g_order[k - LAG])
 
     def g_end(lower, upper):
         def one(i):
@@ -720,18 +718,19 @@
 
         loop(lower, upper, one)
 
-    place(0, qkv_pairs, shift_qkv)
-    place(qkv_pairs, 2 * head_part, shift_rest)
+    place(s.placed, 0, qkv_pairs, shift_qkv)
+    place(s.placed, qkv_pairs, 2 * head_part, shift_rest)
     w_one(0, head_part)
-    place(wide_pairs, wide_pairs + mod_pairs, -wide_pairs)
-    place(wide_pairs + mod_pairs, all_pairs, -wide_pairs + qkv_pairs)
+    place(s.thin, 0, mod_pairs, 0)
+    place(s.thin, mod_pairs, mod_pairs + time_pairs, qkv_pairs)
+
 
     for i in range(1, n_dp):
         tok_copy(i, lax.rem(dp - i + n_dp, n_dp)).wait_recv()
     for i in range(3):
         cols = D // 3
         s.mod_prod[:, i * cols : (i + 1) * cols] = nt(
-            s.tok_all[...], s.placed[z.wide + i * cols : z.wide + (i + 1) * cols, :]
+            s.tok_all[...], s.thin[i * cols : (i + 1) * cols, :]
         )
     for group in range(n_dp):
         for i in range(D // 128):
@@ -752,7 +751,7 @@
     for i in range(1, n_dp):
         go(mod_copy(i))
     w_two(0, head_part)
-    place(2 * head_part, wide_pairs, shift_rest)
+    place(s.placed, 2 * head_part, wide_pairs, shift_rest)
     w_one(head_part, half)
     for i in range(1, n_dp):
         mod_copy(i).wait_recv()
@@ -771,6 +770,7 @@
     for i in range(1, n_t):
         go(mod_all_copy(i, t))
     w_two(head_part, half)
+    w_steps(0, 1)
     for i in range(1, n_t):
         mod_all_copy(i, lax.rem(t - i + n_t, n_t)).wait_recv()
 
@@ -833,6 +833,7 @@
         s.dmlp[at, :] = (mod_line(5) * dy).astype(BF)
         return carry
 
+    w_steps(1, 2)
     lax.fori_loop(0, z.seq // TILE, mix_tile, 0)
 
     sets = range(2)
@@ -902,45 +903,28 @@
         block = shard_of(ph.buf, chip)
         return remote(block, block, ph.zs.at[k], ph.zr.at[k], across if k == 0 else near)
 
-    def ag_x(ph, chip, k):
-        source, target = shard_of(ph.buf, chip), shard_of(ph.xbuf, chip)
-        return remote(source, target, ph.xs.at[k], ph.xr.at[k], xp)
-
-    def ag_start(ph, value, out=False):
+    def ag_start(ph, value):
         ph.buf[rows_at(za * sh, sh), :] = value
         go(ag_z(ph, za, 0))
         go(ag_z(ph, za, 1))
-        if out:
-            go(ag_x(ph, za, 0))
-
-    def ag_middle(ph, out=False):
+
+    def ag_middle(ph):
         ag_z(ph, far_z, 0).wait_recv()
         go(ag_z(ph, far_z, 2))
-        if out:
-            go(ag_x(ph, far_z, 1))
-
-    def ag_end(ph, out=False):
+
+    def ag_end(ph):
         ag_z(ph, near_z, 1).wait_recv()
-        if out:
-            go(ag_x(ph, near_z, 2))
         ag_z(ph, cross_z, 2).wait_recv()
-        if out:
-            go(ag_x(ph, cross_z, 3))
-
-    def ag_end_x(ph):
-        for k, chip in enumerate((za, far_z, near_z, cross_z)):
-            ag_x(ph, chip, k).wait_recv()
 
     parts = range(z.parts)
-    quarter = (half - head_part) // 4
 
     def part_at(part):
         return slice(part * z.part_rows, (part + 1) * z.part_rows)
 
-    w_three(0, head_part)
+    w_steps(2, head_part)
     w_end_own(0, head_part)
     attend(0)
-    w_four(0, head_part)
+    w_steps(head_part, head_part + LAG)
     w_end_other(0, head_part)
     attend(1)
     for i in parts:
@@ -949,44 +933,49 @@
             total = total + times(s.heads[index].o[part_at(i), :], weights[index].p[...])
         s.rs1[i].part[...] = total.astype(BF)
         rs_start(s.rs1[i])
-    w_three(head_part, head_part + 2 * quarter)
+    w_steps(head_part + LAG, head_part + LAG + 2)
     for i in parts:
         rs_middle(s.rs1[i])
+        w_steps(head_part + LAG + 2 + i, head_part + LAG + 3 + i)
 
     def mine_at(part):
         return rows_at(part * z.part_rows + za * sh, sh)
 
-    w_four(head_part, head_part + quarter)
     for i in parts:
         attn = rs_end(s.rs1[i])
+        if i:
+            w_steps(head_part + LAG + 4, head_part + LAG + 5)
         h1 = s.x[mine_at(i), :].astype(F32) + mod_line(2) * attn
         normed_m, _ = norm_parts(h1)
         ag_start(s.ag1[i], (normed_m * (1.0 + mod_line(4)) + mod_line(3)).astype(BF))
         s.attn[i] = attn
         s.h1[i] = h1
-    w_three(head_part + 2 * quarter, half)
+    w_steps(head_part + LAG + 5, half - 3)
     for i in parts:
         ag_middle(s.ag1[i])
-    w_four(head_part + quarter, half)
-    w_end_own(head_part, half)
-    w_end_other(head_part, half)
-
-    for index in sets:
-        s.hid[index].dgact[...] = nt(s.dmlp[...], weights[index].down[...])
-
-    def mlp(part):
+        w_steps(half - 3 + i, half - 2 + i)
+    w_end_own(head_part, thirds[1])
+    w_end_other(head_part, thirds[1])
+
+    def mlp_up(part):
         at = part_at(part)
-        total = 0.0
         for index in sets:
             hid = s.hid[index]
             hidden = nt(s.ag1[part].buf[...], weights[index].up[...])
             square = hidden * hidden
             bend = jnp.tanh(GELU_C * hidden * (1.0 + GELU_K * square))
             hid.gact[at, :] = (0.5 * hidden * (1.0 + bend)).astype(BF)
-            slope = 0.5 * (1.0 + bend) + 0.5 * hidden * (1.0 - bend * bend) * (
+            hid.slope[at, :] = 0.5 * (1.0 + bend) + 0.5 * hidden * (1.0 - bend * bend) * (
                 GELU_C * (1.0 + 3.0 * GELU_K * square)
             )
-            dz = (hid.dgact[at, :] * slope).astype(BF)
+
+    def mlp_back(part):
+        at = part_at(part)
+        total = 0.0
+        for index in sets:
+            hid = s.hid[index]
+            dgact = nt(s.dmlp[at, :], weights[index].down[...])
+            dz = (dgact * hid.slope[at, :]).astype(BF)
             hid.dz[at, :] = dz
             total = total + times(dz, weights[index].up[...])
         s.rs2[part].part[...] = total.astype(BF)
@@ -997,11 +986,6 @@
             total = total + times(s.hid[index].gact[part_at(part), :], weights[index].down[...])
         s.rs4[part].part[...] = total.astype(BF)
 
-    for i in parts:
-        ag_end(s.ag1[i])
-        mlp(i)
-        rs_start(s.rs2[i])
-
     cols = 384
 
     def over_parts(left, gathered, at):
@@ -1010,23 +994,52 @@
             total = total + tn(left[part_at(part), :], gathered[part].buf[:, at])
         return total.astype(BF)
 
-    def grad_tile(i, carry):
-        at = pl.ds(pl.multiple_of(i * cols, 128), cols)
-        for index, first in ((1, z.wide), (0, 4 * hc)):
-            hid = s.hid[index]
-            s.placed[first : first + fc, at] = over_parts(hid.dz, s.ag1, at)
-            down_grad = tn(hid.gact[...], s.dmlp[:, at]).astype(BF)
-            s.placed[first + fc : first + 2 * fc, at] = down_grad
-        return carry
-
-    lax.fori_loop(0, D // cols, grad_tile, 0)
-    first_one = z.wide - 4 * hc
-    g_one(head_part, half, s.placed, first_one)
+    def tiles(body):
+        loop(0, D // cols, lambda i: body(pl.ds(pl.multiple_of(i * cols, 128), cols)))
+
+    def up_grad(index, target, first):
+        def tile(at):
+            target[first : first + fc, at] = over_parts(s.hid[index].dz, s.ag1, at)
+
+        tiles(tile)
+
+    def down_grad(index, target, first):
+        def tile(at):
+            grad = tn(s.hid[index].gact[...], s.dmlp[:, at])
+            target[first + fc : first + 2 * fc, at] = grad.astype(BF)
+
+        tiles(tile)
+
+    first_one = -4 * hc
+    for i in parts:
+        ag_end(s.ag1[i])
+        w_steps(half - 1 + i, half + i)
+        mlp_up(i)
+    down_grad(1, s.thin, 0)
+    g_one(1, thirds[1], half, s.thin, first_one)
+    w_steps(half + 1, half + LAG)
+    w_end_own(thirds[1], half)
+    w_end_other(thirds[1], half)
+    g_two(thirds[1], half, s.thin, first_one)
+    for i in g_order[:LAG]:
+        g_x(i).start()
+    for i in parts:
+        mlp_back(i)
+        rs_start(s.rs2[i])
+    up_grad(1, s.thin, 0)
+    g_one(1, head_part, thirds[1], s.thin, first_one)
+    down_grad(0, s.placed, 4 * hc)
+    g_one(0, thirds[1], half, s.placed, 0)
+    g_two_own(thirds[1], half)
     for i in parts:
         rs_middle(s.rs2[i])
-    g_two(head_part, half, s.placed, first_one)
+    g_two(head_part, thirds[1], s.thin, first_one)
+    g_steps(0, 2)
+    up_grad(0, s.placed, 4 * hc)
+    g_one(0, head_part, thirds[1], s.placed, 0)
     for i in parts:
         down(i)
+    g_two_own(head_part, thirds[1])
 
     def norm_back_of(normed, inverse, upstream):
         return inverse * (
@@ -1041,11 +1054,10 @@
     def dy_of(part):
         return s.grad[mine_at(part), :].astype(F32) * (group_scale * live)
 
-    step = (half - head_part) // 6
-    g_three(head_part, head_part + step)
     gate_a_sum = shift_m_sum = scale_m_sum = 0.0
     for i in parts:
         dw = rs_end(s.rs2[i])
+        g_steps(2 + i, 3 + i)
         normed_m, inverse_m = norm_parts(s.h1[i])
         dh1 = dy_of(i) + norm_back_of(normed_m, inverse_m, dw * (1.0 + mod_line(4)))
         ag_start(s.ag2[i], (mod_line(2) * dh1).astype(BF))
@@ -1056,12 +1068,12 @@
     s.dmod[2:3, :] = gate_a_sum
     s.dmod[3:4, :] = shift_m_sum
     s.dmod[4:5, :] = scale_m_sum
-    g_three(head_part + step, head_part + 2 * step)
+    g_steps(4, 5)
     for i in parts:
         ag_middle(s.ag2[i])
+        g_steps(5 + i, 6 + i)
     for i in parts:
         rs_start(s.rs4[i])
-    g_three(head_part + 2 * step, head_part + 3 * step)
 
     def attend_back(index):
         own, at = weights[index], s.heads[index]
@@ -1086,8 +1098,10 @@
 
     for i in parts:
         ag_end(s.ag2[i])
+        g_steps(7 + i, 8 + i)
     for index in sets:
         attend_back(index)
+        g_steps(9 + index, 10)
     for i in parts:
         total = 0.0
         for index in sets:
@@ -1101,22 +1115,28 @@
     for i in parts:
         rs_middle(s.rs4[i])
 
-    def attn_grad_tile(i, carry):
-        at = pl.ds(pl.multiple_of(i * cols, 128), cols)
-        mixed = s.u[:, at]
-        for index, target in ((1, s.extra), (0, s.placed)):
-            own = s.heads[index]
+    def attn_grad_of(index, target):
+        own = s.heads[index]
+
+        def tile(i):
+            at = pl.ds(pl.multiple_of(i * cols, 128), cols)
+            mixed = s.u[:, at]
             target[0:hc, at] = tn(own.dq[...], mixed).astype(BF)
             target[hc : 2 * hc, at] = tn(own.dk[...], mixed).astype(BF)
             target[2 * hc : 3 * hc, at] = tn(own.dv[...], mixed).astype(BF)
             target[3 * hc : 4 * hc, at] = over_parts(own.o, s.ag2, at)
-        return carry
-
-    lax.fori_loop(0, D // cols, attn_grad_tile, 0)
-    g_one(0, head_part, s.extra, 0)
+
+        loop(0, D // cols, tile)
+
+    attn_grad_of(1, s.extra)
+    g_one(1, 0, head_part, s.extra, 0)
     for i in parts:
         rs_middle(s.rs3[i])
     g_two(0, head_part, s.extra, 0)
+    g_steps(12 - LAG, 12)
+    attn_grad_of(0, s.placed)
+    g_one(0, 0, head_part, s.placed, 0)
+    g_two_own(0, head_part)
 
     def dsum_copy():
         return remote(s.dsum, s.dsum_in, s.dsum_s.at[0], s.dsum_r.at[0], xp)
@@ -1125,21 +1145,22 @@
     s.dsum[0:1, 0:hc] = column_sum(s.heads[1].dq[...].astype(F32))
     s.dsum[1:2, 0:hc] = column_sum(s.heads[1].dv[...].astype(F32))
     go(dsum_copy())
-    g_three(head_part + 3 * step, head_part + 5 * step)
+    g_steps(12, 13)
 
     shift_a_sum = scale_a_sum = gate_m_sum = 0.0
     for i in parts:
         du = rs_end(s.rs3[i])
+        g_steps(13 + i, 14 + i)
         normed_a, inverse_a = norm_parts(s.x[mine_at(i), :].astype(F32))
         dx = s.dh1[i] + norm_back_of(normed_a, inverse_a, du * (1.0 + mod_line(1)))
-        ag_start(s.ag3[i], dx.astype(BF), True)
+        ag_start(s.ag3[i], dx.astype(BF))
         shift_a_sum = shift_a_sum + column_sum(du)
         scale_a_sum = scale_a_sum + column_sum(du * normed_a)
     for i in parts:
         mlp_sum = rs_end(s.rs4[i])
         gate_m_sum = gate_m_sum + column_sum(dy_of(i) * mlp_sum)
         result = (s.h1[i] + mod_line(5) * mlp_sum) * live
-        ag_start(s.ag4[i], result.astype(BF), True)
+        ag_start(s.ag4[i], result.astype(BF))
     s.dmod[0:1, :] = shift_a_sum
     s.dmod[1:2, :] = scale_a_sum
     s.dmod[5:6, :] = gate_m_sum
@@ -1171,15 +1192,11 @@
 
     for i in range(1, n_t):
         go(dmod_copy(i))
-    g_three(head_part + 5 * step, half)
-    for i in parts:
-        ag_middle(s.ag3[i], True)
-        ag_middle(s.ag4[i], True)
-    g_three(0, head_part)
-    g_four(head_part, half)
-    for i in parts:
-        ag_end(s.ag3[i], True)
-        ag_end(s.ag4[i], True)
+    for i in parts:
+        ag_middle(s.ag3[i])
+    for i in parts:
+        ag_middle(s.ag4[i])
+    g_steps(15, 16)
     dsum_copy().wait_recv()
     total = s.dmod_pack[t]
     for i in range(1, n_t):
@@ -1202,11 +1219,11 @@
 
     for i in range(1, n_dp):
         go(vec_copy(i, dp))
-    g_four(0, head_part)
+    g_steps(16, half + LAG)
+    for i in parts:
+        ag_end(s.ag3[i])
+        ag_end(s.ag4[i])
     g_end(0, half)
-    for i in parts:
-        ag_end_x(s.ag3[i])
-        ag_end_x(s.ag4[i])
     for i in range(1, n_dp):
         vec_copy(i, lax.rem(dp - i + n_dp, n_dp)).wait_recv()
     for copy in pending:
@@ -1215,9 +1232,8 @@
     outs = [(s.g.fin, out_g), (s.vec, out_vec), (s.tok_all, out_tok)]
     for i in parts:
         at = pl.ds(i * z.part_rows, z.part_rows)
-        for ph, out in ((s.ag4[i], out_bo), (s.ag3[i], out_ig)):
-            outs.append((ph.buf, out.at[xb, at]))
-            outs.append((ph.xbuf, out.at[1 - xb, at]))
+        outs.append((s.ag4[i].buf, out_own.at[0, at]))
+        outs.append((s.ag3[i].buf, out_own.at[1, at]))
     stores = [
         pltpu.make_async_copy(src, dst, s.out_sem.at[i]) for i, (src, dst) in enumerate(outs)
     ]
@@ -1322,17 +1338,16 @@
     vmem = pl.BlockSpec(memory_space=pltpu.VMEM)
     hbm = pl.BlockSpec(memory_space=pl.ANY)
     flops = 12 * z.seq * D * z.wide
-    block_output, input_grad, grads, vectors, tokens = pl.pallas_call(
+    own, grads, vectors, tokens = pl.pallas_call(
         partial(layer_kernel, z, plan),
         out_shape=(
-            jax.ShapeDtypeStruct(inputs.shape, BF),
-            jax.ShapeDtypeStruct(inputs.shape, BF),
+            jax.ShapeDtypeStruct((2, z.seq, D), BF),
             jax.ShapeDtypeStruct((z.wide, D), BF),
             jax.ShapeDtypeStruct((z.dp_count, 16, 256), F32),
             jax.ShapeDtypeStruct((16 * z.dp_count, D), BF),
         ),
         in_specs=[smem, smem, smem, vmem, hbm, hbm, hbm],
-        out_specs=(hbm,) * 5,
+        out_specs=(hbm,) * 4,
         scratch_shapes=flatten(plan),
         compiler_params=pltpu.CompilerParams(
             collective_id=0, has_side_effects=True, vmem_limit_bytes=62 * 2**20
@@ -1350,6 +1365,8 @@
         out_grad,
         master_weight,
     )
+    swap = [(member, member ^ 1) for member in range(z.tensor_count)]
+    other = lax.ppermute(own, axes[1], swap)
     columns = jnp.concatenate(
         [
             vectors[:, :8, :128].reshape(z.dp_count, 1024)[:, : z.mod_rows],
@@ -1369,11 +1386,18 @@
         out_specs=(block,) * 3,
         scratch_shapes=[pltpu.SMEM((z.slots,), jnp.int32)],
         compiler_params=pltpu.CompilerParams(vmem_limit_bytes=48 * 2**20),
+        cost_estimate=pl.CostEstimate(
+            flops=20 * master_weight.size,
+            bytes_accessed=24 * master_weight.size,
+            transcendentals=2 * master_weight.size,
+        ),
         name="update",
     )(owners, grads, columns, tokens, master_weight, first_moment, second_moment)
+    even = lax.rem(lax.axis_index(axes[1]), 2) == 0
+    images = jnp.stack([jnp.where(even, own, other), jnp.where(even, other, own)], axis=1)
     return (
-        block_output,
-        input_grad.astype(F32),
+        images[0],
+        images[1].astype(F32),
         new_first,
         new_second,
         new_master,

time: 196 us -> 184 us (0.939)
  Pallas kernels: 184 us -> 171 us
    pallas_call x1, Pallas kernels: 161 us -> 148 us  [per_device_fast(): pl.pallas_call(partial(layer_kernel, z, plan), out_shape=(jax.ShapeDtypeS...]
    unnamed x15 -> x12, local copies, waits for them, and re-layouts: 4.91 us -> 3.77 us
  transfers between devices with their start and end apart: 0 -> 1, of which waited for: 0 -> 0; matrix products, arithmetic and copies ran while one was open for 0% -> 1% of each run, Pallas kernels for 0% -> 13%
where the time goes in v4:
time: 184 us; the launch traced here: 182 us
  Pallas kernels  171 us (93%)
  local copies, waits for them, and re-layouts  5.6 us (3%)
  other arithmetic  2.4 us (1%)
  between operations  1.99 us (1%)
    pallas_call x1, Pallas kernels, per_device_fast(): pl.pallas_call(partial(layer_kernel, z, plan), out_shape=(jax.ShapeDtypeS...  148 us
    pallas_call x1, Pallas kernels, per_device_fast(): pl.pallas_call(partial(update_kernel, z, group_slots), grid=(z.slots // g...  23.1 us
    unnamed x12, local copies, waits for them, and re-layouts  3.77 us
  transfers between devices with their start and end apart: 1, of which 0 were waited for; matrix products, arithmetic and copies ran while one was open for 1% of the time, Pallas kernels for 13%

profile of v4, /device:TPU:0, one launch (start us, length us, event | category | flops | bytes accessed | tf_op | source)
XLA Modules:
  0.0 182.3 jit_solution(8197969552318803404)
XLA Ops:
  2.0 0.1 multiply_convert_fusion
  2.1 0.6 broadcast_in_dim.2.refs_3_
  2.7 0.0 copy-start.2
  2.7 147.9 %layer.1 = (bf16[2,256,1152]{2,1,0:T(8,128)(2,1)}, bf16[1728,1152]{1,0:T(8,128)(2,1)}, f32[4,16,256]{2,1,0:T(8,128)}, bf16[64,1152]{1,0:T(8,128)(2,1)}) custom-call(s32[120]{0:T(128)} %owners.1, s32[4]{0:T(128)} %refs_1_.1, s32[1]{0:T(128)S(6)} %copy.28.refs_2_, bf16[16,1152]{1,0:T(8,128)(2,1)} %broadcast_in_dim.2.refs_3_, bf16[2,256,1152]{2,1,0:T(8,128)(2,1)} %refs_4_.1, ...), custom_call_target="tpu_custom_call" | custom-call | flops 6115295232 | bytes 20971520 | tf_op jit(solution)/shard_map/layer/pallas_call | solution.py:1341
  150.6 1.3 collective-permute-start
  151.9 0.7 slice_bitcast_fusion
  152.7 0.8 fusion.6
  153.5 0.1 concatenate.14
  153.6 0.2 copy.17
  153.9 0.0 copy-done.2
  153.9 0.0 copy-start
  153.9 2.1 %copy-done = bf16[1728,1152]{1,0:T(8,128)(2,1)S(1)} copy-done((bf16[1728,1152]{1,0:T(8,128)(2,1)S(1)}, bf16[1728,1152]{1,0:T(8,128)(2,1)}, u32[]{:S(2)}) %copy-start) | copy-done | bytes 3981336
  156.0 0.0 copy-start.1
  156.0 0.9 copy-done.1
  156.9 0.0 copy-start.3
  156.9 23.1 %update.1 = (f32[90,24,1152]{2,1,0:T(8,128)}, f32[90,24,1152]{2,1,0:T(8,128)}, f32[90,24,1152]{2,1,0:T(8,128)}) custom-call(s32[120]{0:T(128)S(1)} %copy-done.2, bf16[1728,1152]{1,0:T(8,128)(2,1)S(1)} %copy-done, f32[48,24,4]{2,1,0:T(8,128)S(1)} %bitcast.25, bf16[64,1152]{1,0:T(8,128)(2,1)S(1)} %copy-done.1, f32[90,24,1152]{2,1,0:T(8,128)} %master.1, ...), custom_call_target="tpu_custom_call" | custom-call | flops 49766400 | bytes 59719680 | tf_op jit(solution)/shard_map/update/pallas_call | solution.py:1381
  180.0 0.0 collective-permute-done
  180.0 0.0 copy-done.3
  180.0 0.2 select_bitcast_fusion
  180.3 2.0 %fusion.3 = (f32[2,256,1152]{2,1,0:T(8,128)}, bf16[2,256,1152]{2,1,0:T(8,128)(2,1)}) fusion(bf16[2,1,256,1152]{3,2,0,1:T(8,128)(2,1)S(1)} %get-tuple-element.21, bf16[2,1,256,1152]{3,2,0,1:T(8,128)(2,1)S(1)} %get-tuple-element.22), kind=kLoop, calls=%fused_computation.6 | loop fusion | flops 1769472 | bytes 5898240 | tf_op jit(solution)/shard_map/convert_element_type | solution.py:1400
  (5 shorter events, 0.1 us)
Async XLA Ops:
  2.7 151.2 %copy-start.2 = (s32[120]{0:T(128)S(1)}, s32[120]{0:T(128)}, u32[]{:S(2)}) copy-start(s32[120]{0:T(128)} %owners.1) | copy-start | bytes 1444
  150.6 29.4 %collective-permute-start = (bf16[2,256,1152]{2,1,0:T(8,128)(2,1)}, bf16[2,256,1152]{2,1,0:T(8,128)(2,1)S(1)}, u32[]{:S(2)}, u32[]{:S(2)}) collective-permute-start(bf16[2,256,1152]{2,1,0:T(8,128)(2,1)} %get-tuple-element.12), channel_id=1, source_target_pairs={{0,1},{1,0},{2,3},{3,2},{4,5},{5,4},{6,7},{7,6},{8,9},{9,8},{10,11... | collective-permute-start | bytes 3538952 | tf_op jit(solution)/shard_map/ppermute | solution.py:1369
  153.9 2.1 %copy-start = (bf16[1728,1152]{1,0:T(8,128)(2,1)S(1)}, bf16[1728,1152]{1,0:T(8,128)(2,1)}, u32[]{:S(2)}) copy-start(bf16[1728,1152]{1,0:T(8,128)(2,1)} %get-tuple-element.13.grads) | copy-start | bytes 11943940
  156.0 0.9 copy-start.1
  156.9 23.1 %copy-start.3 = (bf16[2,256,1152]{2,1,0:T(8,128)(2,1)S(1)}, bf16[2,256,1152]{2,1,0:T(8,128)(2,1)}, u32[]{:S(2)}) copy-start(bf16[2,256,1152]{2,1,0:T(8,128)(2,1)} %get-tuple-element.12) | copy-start | bytes 3538948

commit v5 on v4

--- a/solution.py
+++ b/solution.py
@@ -430,9 +430,10 @@
         dsum_s=dma((1,)),
         dsum_r=dma((1,)),
         vec=vm((z.dp_count, 16, 256), F32),
+        table=vm((z.thin, 8), F32),
         vec_s=dma((3,)),
         vec_r=dma((3,)),
-        out_sem=dma((3 + 2 * z.parts,)),
+        out_sem=dma((5 + z.parts,)),
         sib=pairs(),
         mrg=pairs(),
         w=SimpleNamespace(
@@ -474,14 +475,17 @@
         ag1=each(gather),
         ag2=each(gather),
         ag3=each(gather),
-        ag4=each(gather),
+        bo=vm((z.parts * z.shard, D), BF),
+        bo_in=vm((z.parts * z.shard, D), BF),
+        bo_s=dma((1,)),
+        bo_r=dma((1,)),
     )
 
 
 def layer_kernel(z, plan, *refs):
     owners, counts, held, tok, x_hbm, grad_hbm, master_hbm = refs[:7]
-    out_own, out_g, out_vec, out_tok = refs[7:11]
-    s = rebuild(plan, iter(refs[11:]))
+    out_bo, out_ig, out_g, out_table, out_tok = refs[7:12]
+    s = rebuild(plan, iter(refs[12:]))
     nt_dims = (((1,), (1,)), ((), ()))
     tn_dims = (((0,), (0,)), ((), ()))
 
@@ -679,6 +683,7 @@
             g_core(i, 1, src, first).wait()
             mine = src[rows_at(first + (2 * i + core) * PAIR, PAIR), :].astype(F32)
             s.g.mrg1[i] = (mine + s.g.sib1[i].astype(F32)).astype(BF)
+            g_x(i).start()
 
         loop(lower, upper, one)
 
@@ -706,8 +711,6 @@
         for k in range(lower, upper):
             if k < half:
                 g_three(g_order[k])
-            if k + LAG < half:
-                g_x(g_order[k + LAG]).start()
             if 0 <= k - LAG < half:
                 g_four(g_order[k - LAG])
 
@@ -903,10 +906,13 @@
         block = shard_of(ph.buf, chip)
         return remote(block, block, ph.zs.at[k], ph.zr.at[k], across if k == 0 else near)
 
+    def ag_send(ph):
+        go(ag_z(ph, za, 0))
+        go(ag_z(ph, za, 1))
+
     def ag_start(ph, value):
         ph.buf[rows_at(za * sh, sh), :] = value
-        go(ag_z(ph, za, 0))
-        go(ag_z(ph, za, 1))
+        ag_send(ph)
 
     def ag_middle(ph):
         ag_z(ph, far_z, 0).wait_recv()
@@ -1021,8 +1027,6 @@
     w_end_own(thirds[1], half)
     w_end_other(thirds[1], half)
     g_two(thirds[1], half, s.thin, first_one)
-    for i in g_order[:LAG]:
-        g_x(i).start()
     for i in parts:
         mlp_back(i)
         rs_start(s.rs2[i])
@@ -1054,10 +1058,10 @@
     def dy_of(part):
         return s.grad[mine_at(part), :].astype(F32) * (group_scale * live)
 
+    g_steps(2, 4)
     gate_a_sum = shift_m_sum = scale_m_sum = 0.0
     for i in parts:
         dw = rs_end(s.rs2[i])
-        g_steps(2 + i, 3 + i)
         normed_m, inverse_m = norm_parts(s.h1[i])
         dh1 = dy_of(i) + norm_back_of(normed_m, inverse_m, dw * (1.0 + mod_line(4)))
         ag_start(s.ag2[i], (mod_line(2) * dh1).astype(BF))
@@ -1068,10 +1072,10 @@
     s.dmod[2:3, :] = gate_a_sum
     s.dmod[3:4, :] = shift_m_sum
     s.dmod[4:5, :] = scale_m_sum
-    g_steps(4, 5)
+    g_steps(4, 6)
     for i in parts:
         ag_middle(s.ag2[i])
-        g_steps(5 + i, 6 + i)
+        g_steps(6 + i, 7 + i)
     for i in parts:
         rs_start(s.rs4[i])
 
@@ -1096,12 +1100,33 @@
         at.dk[...] = (dk * scale).astype(BF)
         at.dv[...] = dv.astype(BF)
 
+    def proj_grad(index, target):
+        def tile(at):
+            target[3 * hc : 4 * hc, at] = over_parts(s.heads[index].o, s.ag2, at)
+
+        tiles(tile)
+
+    def attn_grad(index, target):
+        own = s.heads[index]
+
+        def tile(at):
+            mixed = s.u[:, at]
+            target[0:hc, at] = tn(own.dq[...], mixed).astype(BF)
+            target[hc : 2 * hc, at] = tn(own.dk[...], mixed).astype(BF)
+            target[2 * hc : 3 * hc, at] = tn(own.dv[...], mixed).astype(BF)
+
+        tiles(tile)
+
     for i in parts:
         ag_end(s.ag2[i])
-        g_steps(7 + i, 8 + i)
-    for index in sets:
-        attend_back(index)
-        g_steps(9 + index, 10)
+        g_steps(8 + i, 9 + i)
+    attend_back(1)
+    proj_grad(1, s.extra)
+    attn_grad(1, s.extra)
+    g_one(1, 0, head_part, s.extra, 0)
+    g_steps(10, 11)
+    attend_back(0)
+    g_two(0, head_part, s.extra, 0)
     for i in parts:
         total = 0.0
         for index in sets:
@@ -1112,31 +1137,17 @@
             total = total + times(at.dv[rows, :], own.v[...])
         s.rs3[i].part[...] = total.astype(BF)
         rs_start(s.rs3[i])
+    g_steps(11, 12)
+    proj_grad(0, s.placed)
+    attn_grad(0, s.placed)
+    g_one(0, 0, head_part, s.placed, 0)
     for i in parts:
         rs_middle(s.rs4[i])
-
-    def attn_grad_of(index, target):
-        own = s.heads[index]
-
-        def tile(i):
-            at = pl.ds(pl.multiple_of(i * cols, 128), cols)
-            mixed = s.u[:, at]
-            target[0:hc, at] = tn(own.dq[...], mixed).astype(BF)
-            target[hc : 2 * hc, at] = tn(own.dk[...], mixed).astype(BF)
-            target[2 * hc : 3 * hc, at] = tn(own.dv[...], mixed).astype(BF)
-            target[3 * hc : 4 * hc, at] = over_parts(own.o, s.ag2, at)
-
-        loop(0, D // cols, tile)
-
-    attn_grad_of(1, s.extra)
-    g_one(1, 0, head_part, s.extra, 0)
+    g_two_own(0, head_part)
+    g_steps(12, 14)
     for i in parts:
         rs_middle(s.rs3[i])
-    g_two(0, head_part, s.extra, 0)
-    g_steps(12 - LAG, 12)
-    attn_grad_of(0, s.placed)
-    g_one(0, 0, head_part, s.placed, 0)
-    g_two_own(0, head_part)
+    g_steps(14, 15)
 
     def dsum_copy():
         return remote(s.dsum, s.dsum_in, s.dsum_s.at[0], s.dsum_r.at[0], xp)
@@ -1145,25 +1156,31 @@
     s.dsum[0:1, 0:hc] = column_sum(s.heads[1].dq[...].astype(F32))
     s.dsum[1:2, 0:hc] = column_sum(s.heads[1].dv[...].astype(F32))
     go(dsum_copy())
-    g_steps(12, 13)
-
-    shift_a_sum = scale_a_sum = gate_m_sum = 0.0
-    for i in parts:
-        du = rs_end(s.rs3[i])
-        g_steps(13 + i, 14 + i)
-        normed_a, inverse_a = norm_parts(s.x[mine_at(i), :].astype(F32))
-        dx = s.dh1[i] + norm_back_of(normed_a, inverse_a, du * (1.0 + mod_line(1)))
-        ag_start(s.ag3[i], dx.astype(BF))
-        shift_a_sum = shift_a_sum + column_sum(du)
-        scale_a_sum = scale_a_sum + column_sum(du * normed_a)
+
+    gate_m_sum = 0.0
     for i in parts:
         mlp_sum = rs_end(s.rs4[i])
         gate_m_sum = gate_m_sum + column_sum(dy_of(i) * mlp_sum)
         result = (s.h1[i] + mod_line(5) * mlp_sum) * live
-        ag_start(s.ag4[i], result.astype(BF))
+        s.bo[i * sh : (i + 1) * sh, :] = result.astype(BF)
+    s.dmod[5:6, :] = gate_m_sum
+
+    def bo_copy():
+        return remote(s.bo, s.bo_in, s.bo_s.at[0], s.bo_r.at[0], xp)
+
+    go(bo_copy())
+    g_steps(15, 16)
+    shift_a_sum = scale_a_sum = 0.0
+    for i in parts:
+        du = rs_end(s.rs3[i])
+        g_steps(16 + i, 17 + i)
+        normed_a, inverse_a = norm_parts(s.x[mine_at(i), :].astype(F32))
+        dx = s.dh1[i] + norm_back_of(normed_a, inverse_a, du * (1.0 + mod_line(1)))
+        s.ag3[i].buf[rows_at(za * sh, sh), :] = dx.astype(BF)
+        shift_a_sum = shift_a_sum + column_sum(du)
+        scale_a_sum = scale_a_sum + column_sum(du * normed_a)
     s.dmod[0:1, :] = shift_a_sum
     s.dmod[1:2, :] = scale_a_sum
-    s.dmod[5:6, :] = gate_m_sum
     s.dmod[6:8, :] = jnp.zeros((2, D), F32)
 
     dlines = [spread(s.dmod[i : i + 1, :]) for i in range(6)]
@@ -1193,10 +1210,9 @@
     for i in range(1, n_t):
         go(dmod_copy(i))
     for i in parts:
+        ag_send(s.ag3[i])
+    for i in parts:
         ag_middle(s.ag3[i])
-    for i in parts:
-        ag_middle(s.ag4[i])
-    g_steps(15, 16)
     dsum_copy().wait_recv()
     total = s.dmod_pack[t]
     for i in range(1, n_t):
@@ -1219,21 +1235,31 @@
 
     for i in range(1, n_dp):
         go(vec_copy(i, dp))
-    g_steps(16, half + LAG)
+    g_steps(half, half + LAG)
     for i in parts:
         ag_end(s.ag3[i])
-        ag_end(s.ag4[i])
     g_end(0, half)
     for i in range(1, n_dp):
         vec_copy(i, lax.rem(dp - i + n_dp, n_dp)).wait_recv()
+    group_lines = []
+    for group in range(n_dp):
+        line = [unpack_rows(s.vec[group, 0:8, 0:128]), jnp.zeros((1, D - 1024), F32)]
+        line = spread(jnp.concatenate(line, axis=1))
+        for index in range(2):
+            ends = [s.vec[group, 8 + index : 9 + index, :], jnp.zeros((1, D - 256), F32)]
+            ends = spread(jnp.concatenate(ends, axis=1))
+            line = line + pltpu.roll(ends, z.mod_rows + index * hc, 1)
+        group_lines.append(line[0:1, :])
+    group_lines.append(jnp.zeros((8 - n_dp, D), F32))
+    s.table[...] = jnp.transpose(jnp.concatenate(group_lines, axis=0))
+    bo_copy().wait_recv()
     for copy in pending:
         copy.wait_send()
 
-    outs = [(s.g.fin, out_g), (s.vec, out_vec), (s.tok_all, out_tok)]
-    for i in parts:
-        at = pl.ds(i * z.part_rows, z.part_rows)
-        outs.append((s.ag4[i].buf, out_own.at[0, at]))
-        outs.append((s.ag3[i].buf, out_own.at[1, at]))
+    outs = [(s.g.fin, out_g), (s.table, out_table), (s.tok_all, out_tok)]
+    outs += [(s.bo, out_bo.at[xb]), (s.bo_in, out_bo.at[1 - xb])]
+    for i in parts:
+        outs.append((s.ag3[i].buf, out_ig.at[pl.ds(i * z.part_rows, z.part_rows)]))
     stores = [
         pltpu.make_async_copy(src, dst, s.out_sem.at[i]) for i, (src, dst) in enumerate(outs)
     ]
@@ -1243,12 +1269,31 @@
         store.wait()
 
 
-def update_kernel(z, group_slots, owners, grads, table, tokens, master, first, second, new_first, new_second, new_master, bos):
+def update_kernel(
+    z,
+    group_slots,
+    owners,
+    grads_hbm,
+    table,
+    tokens,
+    master,
+    first,
+    second,
+    new_first,
+    new_second,
+    new_master,
+    bos,
+    grads,
+    sem,
+):
     step = pl.program_id(0)
     dp = lax.axis_index("dp")
 
     @pl.when(step == 0)
     def _():
+        load = pltpu.make_async_copy(grads_hbm, grads, sem)
+        load.start()
+
         def clear(slot, carry):
             bos[slot] = -1
             return carry
@@ -1265,6 +1310,7 @@
             return taken + mine.astype(jnp.int32)
 
         lax.fori_loop(0, z.blocks, note, jnp.int32(0))
+        load.wait()
 
     rows = z.block_rows
     mod_blocks = z.mod_rows // rows
@@ -1280,8 +1326,8 @@
         new_second[i] = two
         spread = two * (1.0 / fix_two)
         root = spread * lax.rsqrt(spread)
-        change = one * (1.0 / fix_one) * pltpu.reciprocal(root + eps_adam) + decay_rate * weight
-        new_master[i] = weight - learn_rate * change
+        move = one * (learn_rate / fix_one) * pltpu.reciprocal(root + eps_adam)
+        new_master[i] = weight * (1.0 - learn_rate * decay_rate) - move
 
     def slot(i, carry):
         block = bos[step * group_slots + i]
@@ -1297,7 +1343,7 @@
         @pl.when((block >= 0) & (is_mod | is_time))
         def _():
             index = jnp.where(is_mod, block, block - 3 * head_blocks)
-            columns = table[index]
+            columns = table[pl.ds(pl.multiple_of(index * rows, 8), rows), :]
             grad = columns[:, 0:1] * tokens[0:1, :].astype(F32)
             for group in range(1, z.dp_count):
                 grad = grad + columns[:, group : group + 1] * tokens[
@@ -1305,15 +1351,21 @@
                 ].astype(F32)
             put(i, grad)
 
-        @pl.when((block >= 0) & jnp.logical_not(is_mod | is_time))
+        is_wide = (block >= 0) & jnp.logical_not(is_mod | is_time)
+        index = jnp.where(
+            block < mod_blocks + 3 * head_blocks,
+            block - mod_blocks,
+            block - mod_blocks - 2 * head_blocks,
+        )
+        pair = jnp.clip(index, 0, z.wide // rows - 1) // 2 * PAIR
+
+        @pl.when(is_wide & (lax.rem(index, 2) == 0))
         def _():
-            index = jnp.where(
-                block < mod_blocks + 3 * head_blocks,
-                block - mod_blocks,
-                block - mod_blocks - 2 * head_blocks,
-            )
-            both = grads[rows_at(index // 2 * PAIR, PAIR), :].astype(F32)
-            put(i, jnp.where(lax.rem(index, 2) == 0, both[:rows], both[rows:]))
+            put(i, grads[rows_at(pair, 32), :].astype(F32)[:rows])
+
+        @pl.when(is_wide & (lax.rem(index, 2) == 1))
+        def _():
+            put(i, grads[rows_at(pair + 16, 32), :].astype(F32)[8:])
 
         return carry
 
@@ -1338,16 +1390,17 @@
     vmem = pl.BlockSpec(memory_space=pltpu.VMEM)
     hbm = pl.BlockSpec(memory_space=pl.ANY)
     flops = 12 * z.seq * D * z.wide
-    own, grads, vectors, tokens = pl.pallas_call(
+    bo, own, grads, table, tokens = pl.pallas_call(
         partial(layer_kernel, z, plan),
         out_shape=(
-            jax.ShapeDtypeStruct((2, z.seq, D), BF),
+            jax.ShapeDtypeStruct((2, z.parts * z.shard, D), BF),
+            jax.ShapeDtypeStruct((z.seq, D), BF),
             jax.ShapeDtypeStruct((z.wide, D), BF),
-            jax.ShapeDtypeStruct((z.dp_count, 16, 256), F32),
+            jax.ShapeDtypeStruct((z.thin, 8), F32),
             jax.ShapeDtypeStruct((16 * z.dp_count, D), BF),
         ),
         in_specs=[smem, smem, smem, vmem, hbm, hbm, hbm],
-        out_specs=(hbm,) * 4,
+        out_specs=(hbm,) * 5,
         scratch_shapes=flatten(plan),
         compiler_params=pltpu.CompilerParams(
             collective_id=0, has_side_effects=True, vmem_limit_bytes=62 * 2**20
@@ -1365,16 +1418,12 @@
         out_grad,
         master_weight,
     )
-    swap = [(member, member ^ 1) for member in range(z.tensor_count)]
-    other = lax.ppermute(own, axes[1], swap)
-    columns = jnp.concatenate(
-        [
-            vectors[:, :8, :128].reshape(z.dp_count, 1024)[:, : z.mod_rows],
-            vectors[:, 8, : z.head_cols],
-            vectors[:, 9, : z.head_cols],
-        ],
-        axis=1,
-    ).T.reshape(z.thin // z.block_rows, z.block_rows, z.dp_count)
+    def partner(value, bits):
+        swap = [(member, member ^ bits) for member in range(z.tensor_count)]
+        return lax.ppermute(value, axes[1], swap)
+
+    shards = [bo] + [partner(bo, 2 * step) for step in range(1, 4)]
+    other = partner(own, 1)
     group_slots = next(size for size in (15, 12, 10, 8, 6, 5, 4, 3, 2, 1) if z.slots % size == 0)
     block = pl.BlockSpec((group_slots, z.block_rows, D), lambda i: (i, 0, 0))
     state = jax.ShapeDtypeStruct(master_weight.shape, F32)
@@ -1382,22 +1431,32 @@
         partial(update_kernel, z, group_slots),
         grid=(z.slots // group_slots,),
         out_shape=(state,) * 3,
-        in_specs=[smem, vmem, vmem, vmem, block, block, block],
+        in_specs=[smem, hbm, vmem, vmem, block, block, block],
         out_specs=(block,) * 3,
-        scratch_shapes=[pltpu.SMEM((z.slots,), jnp.int32)],
-        compiler_params=pltpu.CompilerParams(vmem_limit_bytes=48 * 2**20),
+        scratch_shapes=[
+            pltpu.SMEM((z.slots,), jnp.int32),
+            pltpu.VMEM((z.wide, D), BF),
+            pltpu.SemaphoreType.DMA,
+        ],
+        compiler_params=pltpu.CompilerParams(vmem_limit_bytes=60 * 2**20),
         cost_estimate=pl.CostEstimate(
             flops=20 * master_weight.size,
             bytes_accessed=24 * master_weight.size,
             transcendentals=2 * master_weight.size,
         ),
         name="update",
-    )(owners, grads, columns, tokens, master_weight, first_moment, second_moment)
-    even = lax.rem(lax.axis_index(axes[1]), 2) == 0
-    images = jnp.stack([jnp.where(even, own, other), jnp.where(even, other, own)], axis=1)
+    )(owners, grads, table, tokens, master_weight, first_moment, second_moment)
+    place = lax.axis_index(axes[1])
+    even = lax.rem(place, 2) == 0
+    for bit in (1, 2):
+        swapped = lax.rem(place // (2 * bit), 2) == 1
+        shards = [jnp.where(swapped, shards[step ^ bit], shards[step]) for step in range(4)]
+    split = (z.images, z.parts, 1, z.shard, D)
+    block_output = jnp.concatenate([shard.reshape(split) for shard in shards], axis=2)
+    input_grad = jnp.stack([jnp.where(even, own, other), jnp.where(even, other, own)])
     return (
-        images[0],
-        images[1].astype(F32),
+        block_output.reshape(inputs.shape),
+        input_grad.astype(F32),
         new_first,
         new_second,
         new_master,

time: 184 us -> 181 us (0.984)
  local copies, waits for them, and re-layouts: 5.6 us -> 1.82 us
  starting transfers between devices: 1.29 us -> 4.53 us
  Pallas kernels: 171 us -> 169 us
    unnamed x12 -> x4, local copies, waits for them, and re-layouts: 3.77 us -> 0.06 us
    pallas_call x1, Pallas kernels: 148 us -> 144 us  [per_device_fast(): pl.pallas_call(partial(layer_kernel, z, plan), out_shape=(jax.ShapeDtypeS...]
    ppermute x1 -> x4, starting transfers between devices: 1.29 us -> 4.53 us  [partner(): return lax.ppermute(value, axes[1], swap)]
  transfers between devices with their start and end apart: 1 -> 4, of which waited for: 0 -> 0; matrix products, arithmetic and copies ran while one was open for 1% -> 1% of each run, Pallas kernels for 13% -> 14%
where the time goes in v5:
time: 181 us; the launch traced here: 179 us
  Pallas kernels  169 us (93%)
  starting transfers between devices  4.53 us (3%)
  other arithmetic  2.18 us (1%)
  between operations  2.01 us (1%)
  local copies, waits for them, and re-layouts  1.82 us (1%)
    pallas_call x1, Pallas kernels, per_device_fast(): pl.pallas_call(partial(layer_kernel, z, plan), out_shape=(jax.ShapeDtypeS...  144 us
    pallas_call x1, Pallas kernels, per_device_fast(): pl.pallas_call(partial(update_kernel, z, group_slots), grid=(z.slots // g...  24.7 us
    ppermute x4, starting transfers between devices, partner(): return lax.ppermute(value, axes[1], swap)  4.53 us
  transfers between devices with their start and end apart: 4, of which 0 were waited for; matrix products, arithmetic and copies ran while one was open for 1% of the time, Pallas kernels for 14%

profile of v5, /device:TPU:0, one launch (start us, length us, event | category | flops | bytes accessed | tf_op | source)
XLA Modules:
  0.0 179.5 jit_solution(9976112791495415283)
XLA Ops:
  2.0 0.1 multiply_convert_fusion
  2.1 0.6 broadcast_in_dim.2.refs_3_
  2.7 144.2 %layer.1 = (bf16[2,64,1152]{2,1,0:T(8,128)(2,1)}, bf16[256,1152]{1,0:T(8,128)(2,1)}, bf16[1728,1152]{1,0:T(8,128)(2,1)}, f32[1152,8]{1,0:T(8,128)}, bf16[64,1152]{1,0:T(8,128)(2,1)}) custom-call(s32[120]{0:T(128)} %owners.1, s32[4]{0:T(128)} %refs_1_.1, s32[1]{0:T(128)S(6)} %copy.16.refs_2_, bf16[16,1152]{1,0:T(8,128)(2,1)} %broadcast_in_dim.2.refs_3_, ...), custom_call_target="tpu_custom_call" | custom-call | flops 6115295232 | bytes 20971520 | tf_op jit(solution)/shard_map/layer/pallas_call | solution.py:1393
  146.9 0.8 collective-permute-start.2
  147.8 2.0 %collective-permute-start.1 = (bf16[2,64,1152]{2,1,0:T(8,128)(2,1)}, bf16[2,64,1152]{2,1,0:T(8,128)(2,1)S(1)}, u32[]{:S(2)}, u32[]{:S(2)}) collective-permute-start(bf16[2,64,1152]{2,1,0:T(8,128)(2,1)} %get-tuple-element.13), channel_id=1, source_target_pairs={{0,4},{1,5},{2,6},{3,7},{4,0},{5,1},{6,2},{7,3},{8,12},{9,13},{10,... | collective-permute-start | bytes 884744 | tf_op jit(solution)/shard_map/ppermute | solution.py:1423
  149.8 1.6 collective-permute-start
  151.4 0.1 collective-permute-start.3
  151.5 0.0 copy-start.1
  151.5 24.7 %update.1 = (f32[90,24,1152]{2,1,0:T(8,128)}, f32[90,24,1152]{2,1,0:T(8,128)}, f32[90,24,1152]{2,1,0:T(8,128)}) custom-call(s32[120]{0:T(128)} %owners.1, bf16[1728,1152]{1,0:T(8,128)(2,1)} %get-tuple-element.15.grads_hbm, f32[1152,8]{1,0:T(8,128)} %get-tuple-element.16.table, bf16[64,1152]{1,0:T(8,128)(2,1)} %get-tuple-element.17.tokens, ...), custom_call_target="tpu_custom_call" | custom-call | flops 49766400 | bytes 59719680 | tf_op jit(solution)/shard_map/update/pallas_call | solution.py:1430
  176.2 0.0 collective-permute-done.2
  176.2 0.0 collective-permute-done.1
  176.2 0.0 collective-permute-done
  176.2 0.0 copy-done.1
  176.2 0.2 broadcast_select_fusion.7
  176.4 0.2 pad_maximum_fusion
  176.6 0.0 copy-start
  176.6 1.1 copy.14
  177.7 0.0 collective-permute-done.3
  177.7 0.1 copy-done
  177.7 0.2 select_bitcast_fusion.1
  177.9 1.6 maximum_convert_fusion
  (1 shorter events, 0.0 us)
Async XLA Ops:
  146.9 29.2 %collective-permute-start.2 = (bf16[2,64,1152]{2,1,0:T(8,128)(2,1)}, bf16[2,64,1152]{2,1,0:T(8,128)(2,1)S(1)}, u32[]{:S(2)}, u32[]{:S(2)}) collective-permute-start(bf16[2,64,1152]{2,1,0:T(8,128)(2,1)} %get-tuple-element.13), channel_id=1, source_target_pairs={{0,2},{1,3},{2,0},{3,1},{4,6},{5,7},{6,4},{7,5},{8,10},{9,11},{10,... | collective-permute-start | bytes 884744 | tf_op jit(solution)/shard_map/ppermute | solution.py:1423
  147.8 28.4 %collective-permute-start.1 = (bf16[2,64,1152]{2,1,0:T(8,128)(2,1)}, bf16[2,64,1152]{2,1,0:T(8,128)(2,1)S(1)}, u32[]{:S(2)}, u32[]{:S(2)}) collective-permute-start(bf16[2,64,1152]{2,1,0:T(8,128)(2,1)} %get-tuple-element.13), channel_id=1, source_target_pairs={{0,4},{1,5},{2,6},{3,7},{4,0},{5,1},{6,2},{7,3},{8,12},{9,13},{10,... | collective-permute-start | bytes 884744 | tf_op jit(solution)/shard_map/ppermute | solution.py:1423
  149.8 26.4 %collective-permute-start = (bf16[2,64,1152]{2,1,0:T(8,128)(2,1)}, bf16[2,64,1152]{2,1,0:T(8,128)(2,1)S(1)}, u32[]{:S(2)}, u32[]{:S(2)}) collective-permute-start(bf16[2,64,1152]{2,1,0:T(8,128)(2,1)} %get-tuple-element.13), channel_id=1, source_target_pairs={{0,6},{1,7},{2,4},{3,5},{4,2},{5,3},{6,0},{7,1},{8,14},{9,15},{10,... | collective-permute-start | bytes 884744 | tf_op jit(solution)/shard_map/ppermute | solution.py:1423
  151.4 26.3 %collective-permute-start.3 = (bf16[256,1152]{1,0:T(8,128)(2,1)}, bf16[256,1152]{1,0:T(8,128)(2,1)S(1)}, u32[]{:S(2)}, u32[]{:S(2)}) collective-permute-start(bf16[256,1152]{1,0:T(8,128)(2,1)} %get-tuple-element.14), channel_id=1, source_target_pairs={{0,1},{1,0},{2,3},{3,2},{4,5},{5,4},{6,7},{7,6},{8,9},{9,8},{10,11... | collective-permute-start | bytes 1769480 | tf_op jit(solution)/shard_map/ppermute | solution.py:1423
  151.5 24.7 %copy-start.1 = (bf16[2,64,1152]{2,1,0:T(8,128)(2,1)S(1)}, bf16[2,64,1152]{2,1,0:T(8,128)(2,1)}, u32[]{:S(2)}) copy-start(bf16[2,64,1152]{2,1,0:T(8,128)(2,1)} %get-tuple-element.13) | copy-start | bytes 884740
  176.6 1.2 copy-start

commit v6 on v5

--- a/solution.py
+++ b/solution.py
@@ -1058,6 +1058,8 @@
     def dy_of(part):
         return s.grad[mine_at(part), :].astype(F32) * (group_scale * live)
 
+    for i in parts:
+        rs_start(s.rs4[i])
     g_steps(2, 4)
     gate_a_sum = shift_m_sum = scale_m_sum = 0.0
     for i in parts:
@@ -1076,8 +1078,6 @@
     for i in parts:
         ag_middle(s.ag2[i])
         g_steps(6 + i, 7 + i)
-    for i in parts:
-        rs_start(s.rs4[i])
 
     def attend_back(index):
         own, at = weights[index], s.heads[index]

time: 181 us -> 179 us (0.989)
  no operation moved by 1% of the time
where the time goes in v6:
time: 179 us
  Pallas kernels  169 us (94%)
  starting transfers between devices  4.58 us (3%)
  other arithmetic  2.18 us (1%)
  between operations  2.01 us (1%)
  local copies, waits for them, and re-layouts  1.82 us (1%)
    pallas_call x1, Pallas kernels, per_device_fast(): pl.pallas_call(partial(layer_kernel, z, plan), out_shape=(jax.ShapeDtypeS...  144 us
    pallas_call x1, Pallas kernels, per_device_fast(): pl.pallas_call(partial(update_kernel, z, group_slots), grid=(z.slots // g...  24.9 us
    ppermute x4, starting transfers between devices, partner(): return lax.ppermute(value, axes[1], swap)  4.58 us
  transfers between devices with their start and end apart: 4, of which 0 were waited for; matrix products, arithmetic and copies ran while one was open for 1% of the time, Pallas kernels for 14%

profile of v6, /device:TPU:0, one launch (start us, length us, event | category | flops | bytes accessed | tf_op | source)
XLA Modules:
  0.0 179.2 jit_solution(17803217294539077625)
XLA Ops:
  2.0 0.1 multiply_convert_fusion
  2.1 0.6 broadcast_in_dim.2.refs_3_
  2.7 143.7 %layer.1 = (bf16[2,64,1152]{2,1,0:T(8,128)(2,1)}, bf16[256,1152]{1,0:T(8,128)(2,1)}, bf16[1728,1152]{1,0:T(8,128)(2,1)}, f32[1152,8]{1,0:T(8,128)}, bf16[64,1152]{1,0:T(8,128)(2,1)}) custom-call(s32[120]{0:T(128)} %owners.1, s32[4]{0:T(128)} %refs_1_.1, s32[1]{0:T(128)S(6)} %copy.16.refs_2_, bf16[16,1152]{1,0:T(8,128)(2,1)} %broadcast_in_dim.2.refs_3_, ...), custom_call_target="tpu_custom_call" | custom-call | flops 6115295232 | bytes 20971520 | tf_op jit(solution)/shard_map/layer/pallas_call | solution.py:1393
  146.4 0.5 collective-permute-start.2
  146.9 2.2 %collective-permute-start.1 = (bf16[2,64,1152]{2,1,0:T(8,128)(2,1)}, bf16[2,64,1152]{2,1,0:T(8,128)(2,1)S(1)}, u32[]{:S(2)}, u32[]{:S(2)}) collective-permute-start(bf16[2,64,1152]{2,1,0:T(8,128)(2,1)} %get-tuple-element.13), channel_id=1, source_target_pairs={{0,4},{1,5},{2,6},{3,7},{4,0},{5,1},{6,2},{7,3},{8,12},{9,13},{10,... | collective-permute-start | bytes 884744 | tf_op jit(solution)/shard_map/ppermute | solution.py:1423
  149.1 1.8 collective-permute-start
  150.9 0.1 collective-permute-start.3
  151.0 0.0 copy-start.1
  151.0 24.9 %update.1 = (f32[90,24,1152]{2,1,0:T(8,128)}, f32[90,24,1152]{2,1,0:T(8,128)}, f32[90,24,1152]{2,1,0:T(8,128)}) custom-call(s32[120]{0:T(128)} %owners.1, bf16[1728,1152]{1,0:T(8,128)(2,1)} %get-tuple-element.15.grads_hbm, f32[1152,8]{1,0:T(8,128)} %get-tuple-element.16.table, bf16[64,1152]{1,0:T(8,128)(2,1)} %get-tuple-element.17.tokens, ...), custom_call_target="tpu_custom_call" | custom-call | flops 49766400 | bytes 59719680 | tf_op jit(solution)/shard_map/update/pallas_call | solution.py:1430
  175.9 0.0 collective-permute-done.2
  175.9 0.0 collective-permute-done.1
  175.9 0.0 collective-permute-done
  175.9 0.0 copy-done.1
  175.9 0.2 broadcast_select_fusion.7
  176.1 0.2 pad_maximum_fusion
  176.3 0.0 copy-start
  176.3 1.1 copy.14
  177.4 0.0 collective-permute-done.3
  177.4 0.1 copy-done
  177.5 0.2 select_bitcast_fusion.1
  177.6 1.6 maximum_convert_fusion
  (1 shorter events, 0.0 us)
Async XLA Ops:
  146.4 29.5 %collective-permute-start.2 = (bf16[2,64,1152]{2,1,0:T(8,128)(2,1)}, bf16[2,64,1152]{2,1,0:T(8,128)(2,1)S(1)}, u32[]{:S(2)}, u32[]{:S(2)}) collective-permute-start(bf16[2,64,1152]{2,1,0:T(8,128)(2,1)} %get-tuple-element.13), channel_id=1, source_target_pairs={{0,2},{1,3},{2,0},{3,1},{4,6},{5,7},{6,4},{7,5},{8,10},{9,11},{10,... | collective-permute-start | bytes 884744 | tf_op jit(solution)/shard_map/ppermute | solution.py:1423
  146.9 29.0 %collective-permute-start.1 = (bf16[2,64,1152]{2,1,0:T(8,128)(2,1)}, bf16[2,64,1152]{2,1,0:T(8,128)(2,1)S(1)}, u32[]{:S(2)}, u32[]{:S(2)}) collective-permute-start(bf16[2,64,1152]{2,1,0:T(8,128)(2,1)} %get-tuple-element.13), channel_id=1, source_target_pairs={{0,4},{1,5},{2,6},{3,7},{4,0},{5,1},{6,2},{7,3},{8,12},{9,13},{10,... | collective-permute-start | bytes 884744 | tf_op jit(solution)/shard_map/ppermute | solution.py:1423
  149.1 26.8 %collective-permute-start = (bf16[2,64,1152]{2,1,0:T(8,128)(2,1)}, bf16[2,64,1152]{2,1,0:T(8,128)(2,1)S(1)}, u32[]{:S(2)}, u32[]{:S(2)}) collective-permute-start(bf16[2,64,1152]{2,1,0:T(8,128)(2,1)} %get-tuple-element.13), channel_id=1, source_target_pairs={{0,6},{1,7},{2,4},{3,5},{4,2},{5,3},{6,0},{7,1},{8,14},{9,15},{10,... | collective-permute-start | bytes 884744 | tf_op jit(solution)/shard_map/ppermute | solution.py:1423
  150.9 26.5 %collective-permute-start.3 = (bf16[256,1152]{1,0:T(8,128)(2,1)}, bf16[256,1152]{1,0:T(8,128)(2,1)S(1)}, u32[]{:S(2)}, u32[]{:S(2)}) collective-permute-start(bf16[256,1152]{1,0:T(8,128)(2,1)} %get-tuple-element.14), channel_id=1, source_target_pairs={{0,1},{1,0},{2,3},{3,2},{4,5},{5,4},{6,7},{7,6},{8,9},{9,8},{10,11... | collective-permute-start | bytes 1769480 | tf_op jit(solution)/shard_map/ppermute | solution.py:1423
  151.0 24.9 %copy-start.1 = (bf16[2,64,1152]{2,1,0:T(8,128)(2,1)S(1)}, bf16[2,64,1152]{2,1,0:T(8,128)(2,1)}, u32[]{:S(2)}) copy-start(bf16[2,64,1152]{2,1,0:T(8,128)(2,1)} %get-tuple-element.13) | copy-start | bytes 884740
  176.3 1.2 copy-start
